TPU v7x, 32 devices: a whole 2x2x4 slice. The times are simulated.
32 devices in a mesh: wide: 16 (over z, y, x), narrow: 2 (over core).
Axes of the slice: x: 2, y: 2, z: 4, core: 2. Of those that a mesh axis runs over, the one named last changes fastest.
Arguments:
- pixels: bfloat16 [32, 512, 1024], P(('wide', 'narrow')), may hold values from -6 to 6
- layout: int32 [32], P(('wide', 'narrow')), may hold values from 0 to 1
- noise_group: int32 [32], P(('wide', 'narrow')), may hold values from 0 to 15
- cond_embed: bfloat16 [32, 1024], P(('wide', 'narrow')), may hold values from -6 to 6
- text_embed: bfloat16 [32, 128, 4096], P(('wide', 'narrow')), may hold values from -6 to 6
- cotangent: bfloat16 [32, 512, 1024], P(('wide', 'narrow')), may hold values from -6 to 6
- gn_gain: bfloat16 [1024], P('narrow'), may hold values from 0.099609375 to 1.8984375
- gn_bias: bfloat16 [1024], P('narrow'), may hold values from -3 to 3
- conv_in: bfloat16 [9, 1024, 1024], P(None, 'narrow'), may hold values from -0.0625 to 0.0625
- film_weight: bfloat16 [1024, 2048], P('narrow'), may hold values from -0.1875 to 0.1875
- film_bias: bfloat16 [2048], P('narrow'), may hold values from -3 to 3
- conv_out: bfloat16 [9, 1024, 1024], P(None, 'narrow'), may hold values from -0.0625 to 0.0625
- ln_gain: bfloat16 [1024], P('narrow'), may hold values from 0.099609375 to 1.8984375
- qkv_weight: bfloat16 [1024, 3072], P('narrow'), may hold values from -0.1875 to 0.1875
- out_weight: bfloat16 [1024, 1024], P('narrow'), may hold values from -3 to 3
- text_weight: bfloat16 [4096, 2048], P('narrow'), may hold values from -0.09375 to 0.09375
Outputs:
- output: bfloat16 [32, 512, 1024], P(('wide', 'narrow'))
- input_grad: bfloat16 [32, 512, 1024], P(('wide', 'narrow'))
- grad_gn_gain: float32 [1024], P('narrow')
- grad_gn_bias: float32 [1024], P('narrow')
- grad_conv_in: float32 [9, 1024, 1024], P(None, 'narrow')
- grad_film_weight: float32 [1024, 2048], P('narrow')
- grad_film_bias: float32 [2048], P('narrow')
- grad_conv_out: float32 [9, 1024, 1024], P(None, 'narrow')
- grad_ln_gain: float32 [1024], P('narrow')
- grad_qkv_weight: float32 [1024, 3072], P('narrow')
- grad_out_weight: float32 [1024, 1024], P('narrow')
- grad_text_weight: float32 [4096, 2048], P('narrow')
Inputs may be any that keep to these rules, and one draw needn't show every extreme that they name: `layout`: 1: the image's 16 x 32 pixels form one map; 0: its four quarters are four separate maps.
All inputs are finite; a program needn't handle non-finite values.
Results may differ from a plain program's by a relative error of at most 0.024.
Values may be sent and summed in bfloat16 or wider, within the bound.
A program may use at most 384 MiB of HBM per device.

v0:
```python
import jax
import jax.numpy as jnp
from jax import lax
from jax.sharding import PartitionSpec as P

NORM_GROUPS = 32
HEADS = 8
TEXT_LEN = 128
MAP_H = 16
MAP_W = 32


highest = lax.Precision.HIGHEST
epsilon = 1e-05
inv_root_two = 0.7071067811865476
masked_score = -1e30


def region_ids_of(layout_value):
    position = jnp.arange(MAP_H * MAP_W, dtype=jnp.int32)
    quarter = 2 * (position // MAP_W >= MAP_H // 2).astype(jnp.int32) + (
        position % MAP_W >= MAP_W // 2
    ).astype(jnp.int32)
    return jnp.where(layout_value == 1, jnp.zeros_like(quarter), quarter)


def tap_validity(region_ids):
    code_grid = region_ids.reshape(MAP_H, MAP_W)
    padded = jnp.pad(code_grid, 1, constant_values=-1)
    found = []
    for row_step in (-1, 0, 1):
        for col_step in (-1, 0, 1):
            neighbour = padded[
                1 + row_step : 1 + row_step + MAP_H, 1 + col_step : 1 + col_step + MAP_W
            ]
            found.append((neighbour == code_grid).reshape(-1))
    return jnp.stack(found)


def unfold(values, tap_valid):
    channels = values.shape[-1]
    padded = jnp.pad(values.reshape(MAP_H, MAP_W, channels), ((1, 1), (1, 1), (0, 0)))
    pieces = []
    tap_index = 0
    for row_step in (-1, 0, 1):
        for col_step in (-1, 0, 1):
            neighbour = padded[
                1 + row_step : 1 + row_step + MAP_H, 1 + col_step : 1 + col_step + MAP_W
            ].reshape(MAP_H * MAP_W, channels)
            pieces.append(
                jnp.where(tap_valid[tap_index][:, None], neighbour, jnp.zeros_like(neighbour))
            )
            tap_index += 1
    return jnp.concatenate(pieces, axis=1)


def fold_back(grad_cols, tap_valid):
    channels = grad_cols.shape[1] // 9
    start_point = jnp.zeros((grad_cols.shape[0], channels), jnp.float32)
    unfolded, pullback = jax.vjp(lambda field: unfold(field, tap_valid), start_point)
    return pullback(grad_cols)[0]


def group_norm(values, members):
    pixel_count, channels = values.shape
    grouped = values.reshape(pixel_count, NORM_GROUPS, channels // NORM_GROUPS)
    counts = jnp.maximum(jnp.sum(members, axis=0) * (channels // NORM_GROUPS), 1.0)
    region_sums = jnp.einsum("pr,pg->rg", members, jnp.sum(grouped, axis=2), precision=highest)
    pixel_means = jnp.einsum("pr,rg->pg", members, region_sums / counts[:, None], precision=highest)
    centred = grouped - pixel_means[:, :, None]
    squares = jnp.einsum(
        "pr,pg->rg", members, jnp.sum(centred * centred, axis=2), precision=highest
    )
    spreads = jnp.einsum(
        "pr,rg->pg", members, lax.rsqrt(squares / counts[:, None] + epsilon), precision=highest
    )
    return (centred * spreads[:, :, None]).reshape(pixel_count, channels)


def layer_norm(field, gain_in):
    centre = field - jnp.mean(field, axis=1, keepdims=True)
    return centre * lax.rsqrt(jnp.mean(centre * centre, axis=1, keepdims=True) + epsilon) * gain_in


def first_block(field, gain_in, bias_in, members):
    return jax.nn.silu(group_norm(field, members) * gain_in + bias_in)


def mid_block(hidden_in, film_in, members):
    channels = hidden_in.shape[1]
    return jax.nn.silu(
        group_norm(hidden_in, members) * (1.0 + film_in[:channels]) + film_in[channels:]
    )


def residual_front(field, members, tap_valid, condition, weights_full):
    gain_full, bias_full, conv_first, film_full, film_bias_full, conv_second = weights_full
    channels = field.shape[1]
    first_act, first_back = jax.vjp(
        lambda field_in, gain_in, bias_in: first_block(field_in, gain_in, bias_in, members),
        field,
        gain_full.astype(jnp.float32),
        bias_full.astype(jnp.float32),
    )
    first_low = first_act.astype(jnp.bfloat16)
    first_cols = unfold(first_low, tap_valid)
    hidden_one = jnp.dot(
        first_cols, conv_first.reshape(-1, channels), preferred_element_type=jnp.float32
    )
    film_out = jnp.dot(
        condition, film_full, preferred_element_type=jnp.float32
    ) + film_bias_full.astype(jnp.float32)
    second_act, mid_back = jax.vjp(
        lambda hidden_in, film_in: mid_block(hidden_in, film_in, members), hidden_one, film_out
    )
    second_low = second_act.astype(jnp.bfloat16)
    second_cols = unfold(second_low, tap_valid)
    return (first_cols, second_cols, first_back, mid_back)


def allowed_keys(region_ids):
    same_region = region_ids[:, None] == region_ids[None, :]
    return jnp.concatenate(
        [same_region, jnp.ones((region_ids.shape[0], TEXT_LEN), dtype=jnp.bool_)], axis=1
    )


def attention_forward(joined, text_one, region_ids, attn_full):
    gain_full, qkv_full, out_full, text_full = attn_full
    pixel_count, channels = joined.shape
    head_dim = channels // HEADS
    score_scale = head_dim ** (-0.5)
    normed_low = layer_norm(joined, gain_full.astype(jnp.float32)).astype(jnp.bfloat16)
    triple = jnp.dot(normed_low, qkv_full, preferred_element_type=jnp.float32).astype(jnp.bfloat16)
    text_pair = jnp.dot(text_one, text_full, preferred_element_type=jnp.float32).astype(
        jnp.bfloat16
    )
    queries = triple[:, :channels].reshape(pixel_count, HEADS, head_dim)
    key_rows = jnp.concatenate(
        [triple[:, channels : 2 * channels], text_pair[:, :channels]], axis=0
    ).reshape(-1, HEADS, head_dim)
    value_rows = jnp.concatenate(
        [triple[:, 2 * channels :], text_pair[:, channels:]], axis=0
    ).reshape(-1, HEADS, head_dim)
    allowed = allowed_keys(region_ids)
    masked = jnp.where(
        allowed[None],
        jnp.einsum("phd,jhd->hpj", queries, key_rows, preferred_element_type=jnp.float32)
        * score_scale,
        masked_score,
    )
    row_peak = jnp.max(masked, axis=2, keepdims=True)
    exponent = jnp.exp(masked - row_peak)
    exp_total = jnp.sum(exponent, axis=2, keepdims=True)
    attn_probs = exponent / exp_total
    log_total = row_peak + jnp.log(exp_total)
    mixed = (
        jnp.einsum(
            "hpj,jhd->phd",
            attn_probs.astype(jnp.bfloat16),
            value_rows,
            preferred_element_type=jnp.float32,
        )
        .reshape(pixel_count, channels)
        .astype(jnp.bfloat16)
    )
    result = joined + jnp.dot(mixed, out_full, preferred_element_type=jnp.float32)
    return (result, (normed_low, queries, key_rows, value_rows, log_total, mixed, allowed))


def attention_backward(grad_result, joined, text_one, stored, attn_full):
    gain_full, qkv_full, out_full, text_full = attn_full
    normed_low, queries, key_rows, value_rows, log_total, mixed, allowed = stored
    pixel_count, channels = joined.shape
    head_dim = channels // HEADS
    score_scale = head_dim ** (-0.5)
    grad_mixed = (
        jnp.einsum("pd,cd->pc", grad_result, out_full, preferred_element_type=jnp.float32)
        .astype(jnp.bfloat16)
        .reshape(pixel_count, HEADS, head_dim)
    )
    masked = jnp.where(
        allowed[None],
        jnp.einsum("phd,jhd->hpj", queries, key_rows, preferred_element_type=jnp.float32)
        * score_scale,
        masked_score,
    )
    attn_probs = jnp.exp(masked - log_total)
    grad_probs = jnp.einsum(
        "phd,jhd->hpj", grad_mixed, value_rows, preferred_element_type=jnp.float32
    )
    grad_values = jnp.einsum(
        "hpj,phd->jhd",
        attn_probs.astype(jnp.bfloat16),
        grad_mixed,
        preferred_element_type=jnp.float32,
    )
    row_inner = jnp.sum(attn_probs * grad_probs, axis=2, keepdims=True)
    grad_scores = (attn_probs * (grad_probs - row_inner)).astype(jnp.bfloat16)
    grad_queries = (
        jnp.einsum("hpj,jhd->phd", grad_scores, key_rows, preferred_element_type=jnp.float32)
        * score_scale
    )
    grad_keys = (
        jnp.einsum("hpj,phd->jhd", grad_scores, queries, preferred_element_type=jnp.float32)
        * score_scale
    )
    grad_triple = jnp.concatenate(
        [
            grad_queries.reshape(pixel_count, channels),
            grad_keys[:pixel_count].reshape(pixel_count, channels),
            grad_values[:pixel_count].reshape(pixel_count, channels),
        ],
        axis=1,
    ).astype(jnp.bfloat16)
    grad_pair = jnp.concatenate(
        [
            grad_keys[pixel_count:].reshape(-1, channels),
            grad_values[pixel_count:].reshape(-1, channels),
        ],
        axis=1,
    ).astype(jnp.bfloat16)
    term_out = jnp.einsum("pc,pd->cd", mixed, grad_result, preferred_element_type=jnp.float32)
    term_qkv = jnp.einsum("pc,pk->ck", normed_low, grad_triple, preferred_element_type=jnp.float32)
    term_text = jnp.einsum("tc,tk->ck", text_one, grad_pair, preferred_element_type=jnp.float32)
    big_terms = (term_qkv, term_out, term_text)
    grad_normed = jnp.einsum("pk,ck->pc", grad_triple, qkv_full, preferred_element_type=jnp.float32)
    normed_value, norm_back = jax.vjp(layer_norm, joined, gain_full.astype(jnp.float32))
    grad_joined_norm, term_gain = norm_back(grad_normed)
    return (grad_result.astype(jnp.float32) + grad_joined_norm, term_gain, big_terms)


def every_wide_sum(parts):
    return (
        lax.psum(parts[0].astype(jnp.bfloat16), "wide").astype(jnp.float32),
        lax.psum(parts[1].astype(jnp.bfloat16), "wide").astype(jnp.float32),
        lax.psum(parts[2].astype(jnp.bfloat16), "wide").astype(jnp.float32),
        lax.psum(parts[3].astype(jnp.bfloat16), "wide").astype(jnp.float32),
        lax.psum(parts[4].astype(jnp.bfloat16), "wide").astype(jnp.float32),
        lax.psum(parts[5].astype(jnp.bfloat16), "wide").astype(jnp.float32),
        lax.psum(parts[6].astype(jnp.bfloat16), "wide").astype(jnp.float32),
        lax.psum(parts[7].astype(jnp.bfloat16), "wide").astype(jnp.float32),
        lax.psum(parts[8].astype(jnp.bfloat16), "wide").astype(jnp.float32),
        lax.psum(parts[9].astype(jnp.bfloat16), "wide").astype(jnp.float32),
    )


def body(
    pixels,
    layout,
    noise_group,
    cond_embed,
    text_embed,
    cotangent,
    gn_gain,
    gn_bias,
    conv_in,
    film_weight,
    film_bias,
    conv_out,
    ln_gain,
    qkv_weight,
    out_weight,
    text_weight,
):
    group_total = lax.axis_size("wide")
    onehot_groups = (
        noise_group[:, None] == jnp.arange(group_total, dtype=jnp.int32)[None, :]
    ).astype(jnp.float32)
    counts = lax.psum(jnp.sum(onehot_groups, axis=0), ("wide", "narrow"))
    slot_weights = 1.0 / (group_total * jnp.sum(onehot_groups * counts[None, :], axis=1))
    res_full = (
        lax.all_gather(gn_gain, "narrow", axis=0, tiled=True),
        lax.all_gather(gn_bias, "narrow", axis=0, tiled=True),
        lax.all_gather(conv_in, "narrow", axis=1, tiled=True),
        lax.all_gather(film_weight, "narrow", axis=0, tiled=True),
        lax.all_gather(film_bias, "narrow", axis=0, tiled=True),
        lax.all_gather(conv_out, "narrow", axis=1, tiled=True),
    )
    attn_full = (
        lax.all_gather(ln_gain, "narrow", axis=0, tiled=True),
        lax.all_gather(qkv_weight, "narrow", axis=0, tiled=True),
        lax.all_gather(out_weight, "narrow", axis=0, tiled=True),
        lax.all_gather(text_weight, "narrow", axis=0, tiled=True),
    )
    channels = pixels.shape[2]
    slot_index = 0
    field = pixels[slot_index].astype(jnp.float32)
    region_ids = region_ids_of(layout[slot_index])
    members = (region_ids[:, None] == jnp.arange(4, dtype=jnp.int32)[None, :]).astype(jnp.float32)
    tap_valid = tap_validity(region_ids)
    condition = jax.nn.silu(cond_embed[slot_index].astype(jnp.float32)).astype(jnp.bfloat16)
    front = residual_front(field, members, tap_valid, condition, res_full)
    hidden_two = jnp.dot(
        front[1], res_full[5].reshape(-1, channels), preferred_element_type=jnp.float32
    )
    joined = (field + hidden_two) * inv_root_two
    result, stored = attention_forward(joined, text_embed[slot_index], region_ids, attn_full)
    outputs = [result.astype(jnp.bfloat16)]
    saved = [(field, members, tap_valid, condition, joined, stored)]
    attn_big = tuple((jnp.zeros(full_weight.shape, jnp.float32) for full_weight in attn_full[1:]))
    slot_index = 0
    field, members, tap_valid, condition, joined, stored = saved[slot_index]
    grad_joined, term_gain, big_terms = attention_backward(
        cotangent[slot_index], joined, text_embed[slot_index], stored, attn_full
    )
    joined_grads = [grad_joined]
    gain_sum = slot_weights[slot_index] * term_gain
    attn_big = tuple((slot_weights[slot_index] * fresh for fresh in big_terms))
    grad_ln_gain, grad_qkv_weight, grad_out_weight, grad_text_weight = (
        lax.psum_scatter(
            gain_sum.astype(jnp.bfloat16), "narrow", scatter_dimension=0, tiled=True
        ).astype(jnp.float32),
        lax.psum_scatter(
            attn_big[0].astype(jnp.bfloat16), "narrow", scatter_dimension=0, tiled=True
        ).astype(jnp.float32),
        lax.psum_scatter(
            attn_big[1].astype(jnp.bfloat16), "narrow", scatter_dimension=0, tiled=True
        ).astype(jnp.float32),
        lax.psum_scatter(
            attn_big[2].astype(jnp.bfloat16), "narrow", scatter_dimension=0, tiled=True
        ).astype(jnp.float32),
    )
    res_back = (
        lax.all_gather(gn_gain, "narrow", axis=0, tiled=True),
        lax.all_gather(gn_bias, "narrow", axis=0, tiled=True),
        lax.all_gather(conv_in, "narrow", axis=1, tiled=True),
        lax.all_gather(film_weight, "narrow", axis=0, tiled=True),
        lax.all_gather(film_bias, "narrow", axis=0, tiled=True),
        lax.all_gather(conv_out, "narrow", axis=1, tiled=True),
    )
    conv_first = res_back[2].reshape(-1, channels)
    conv_second = res_back[5].reshape(-1, channels)
    small_sums = (
        jnp.zeros(res_back[0].shape, jnp.float32),
        jnp.zeros(res_back[1].shape, jnp.float32),
        jnp.zeros(res_back[4].shape, jnp.float32),
    )
    res_big = (
        jnp.zeros(res_back[2].shape, jnp.float32),
        jnp.zeros(res_back[3].shape, jnp.float32),
        jnp.zeros(res_back[5].shape, jnp.float32),
    )
    slot_index = 0
    field, members, tap_valid, condition, joined, stored = saved[slot_index]
    grad_joined = joined_grads[slot_index]
    first_cols, second_cols, first_back, mid_back = residual_front(
        field, members, tap_valid, condition, res_back
    )
    grad_two = (grad_joined * inv_root_two).astype(jnp.bfloat16)
    grad_second = fold_back(
        jnp.einsum("pc,kc->pk", grad_two, conv_second, preferred_element_type=jnp.float32),
        tap_valid,
    )
    grad_hidden, grad_film = mid_back(grad_second)
    grad_film_low = grad_film.astype(jnp.bfloat16)
    grad_one = grad_hidden.astype(jnp.bfloat16)
    grad_first = fold_back(
        jnp.einsum("pc,kc->pk", grad_one, conv_first, preferred_element_type=jnp.float32), tap_valid
    )
    grad_field, term_gain, term_bias = first_back(grad_first)
    input_grads = [(grad_joined * inv_root_two + grad_field).astype(jnp.bfloat16)]
    small_terms = (term_gain, term_bias, grad_film_low.astype(jnp.float32))
    small_sums = tuple((slot_weights[slot_index] * fresh for fresh in small_terms))
    term_conv_out = jnp.einsum(
        "pk,pc->kc", second_cols, grad_two, preferred_element_type=jnp.float32
    )
    term_film = jnp.einsum("k,c->kc", condition, grad_film_low, preferred_element_type=jnp.float32)
    term_conv_in = jnp.einsum("pk,pc->kc", first_cols, grad_one, preferred_element_type=jnp.float32)
    big_terms = (
        term_conv_in.reshape(res_back[2].shape),
        term_film,
        term_conv_out.reshape(res_back[5].shape),
    )
    res_big = tuple((slot_weights[slot_index] * fresh for fresh in big_terms))
    grad_gn_gain, grad_gn_bias, grad_conv_in, grad_film_weight, grad_film_bias, grad_conv_out = (
        lax.psum_scatter(
            small_sums[0].astype(jnp.bfloat16), "narrow", scatter_dimension=0, tiled=True
        ).astype(jnp.float32),
        lax.psum_scatter(
            small_sums[1].astype(jnp.bfloat16), "narrow", scatter_dimension=0, tiled=True
        ).astype(jnp.float32),
        lax.psum_scatter(
            res_big[0].astype(jnp.bfloat16), "narrow", scatter_dimension=1, tiled=True
        ).astype(jnp.float32),
        lax.psum_scatter(
            res_big[1].astype(jnp.bfloat16), "narrow", scatter_dimension=0, tiled=True
        ).astype(jnp.float32),
        lax.psum_scatter(
            small_sums[2].astype(jnp.bfloat16), "narrow", scatter_dimension=0, tiled=True
        ).astype(jnp.float32),
        lax.psum_scatter(
            res_big[2].astype(jnp.bfloat16), "narrow", scatter_dimension=1, tiled=True
        ).astype(jnp.float32),
    )
    (
        grad_gn_gain,
        grad_gn_bias,
        grad_conv_in,
        grad_film_weight,
        grad_film_bias,
        grad_conv_out,
        grad_ln_gain,
        grad_qkv_weight,
        grad_out_weight,
        grad_text_weight,
    ) = every_wide_sum(
        (
            grad_gn_gain,
            grad_gn_bias,
            grad_conv_in,
            grad_film_weight,
            grad_film_bias,
            grad_conv_out,
            grad_ln_gain,
            grad_qkv_weight,
            grad_out_weight,
            grad_text_weight,
        )
    )
    return (
        jnp.stack(outputs),
        jnp.stack(input_grads),
        grad_gn_gain,
        grad_gn_bias,
        grad_conv_in,
        grad_film_weight,
        grad_film_bias,
        grad_conv_out,
        grad_ln_gain,
        grad_qkv_weight,
        grad_out_weight,
        grad_text_weight,
    )


def solution(mesh):
    placed = (
        P(("wide", "narrow"), None, None),
        P(("wide", "narrow")),
        P(("wide", "narrow")),
        P(("wide", "narrow"), None),
        P(("wide", "narrow"), None, None),
        P(("wide", "narrow"), None, None),
        P("narrow"),
        P("narrow"),
        P(None, "narrow", None),
        P("narrow", None),
        P("narrow"),
        P(None, "narrow", None),
        P("narrow"),
        P("narrow", None),
        P("narrow", None),
        P("narrow", None),
    )
    return jax.shard_map(
        body,
        mesh=mesh,
        in_specs=placed,
        out_specs=(
            P(("wide", "narrow"), None, None),
            P(("wide", "narrow"), None, None),
            P("narrow"),
            P("narrow"),
            P(None, "narrow", None),
            P("narrow", None),
            P("narrow"),
            P(None, "narrow", None),
            P("narrow"),
            P("narrow", None),
            P("narrow", None),
            P("narrow", None),
        ),
        check_vma=False,
    )
```

profile of v0, /device:TPU:0, one launch (start us, length us, event | category | flops | bytes accessed | tf_op | source)
XLA Modules:
  0.0 1446.1 jit_solution(12219664354314973625)
XLA Ops:
  14.5 3.6 convert_element_type.315
  18.0 42.0 %psum.77 = f32[16]{0:T(128)S(1)} all-reduce(f32[16]{0:T(128)S(1)} %compare_convert_fusion), channel_id=1, replica_groups=mesh['wide'=16,'narrow'=2] {'wide','narrow'}, use_global_device_ids=true, to_apply=%region_16.17 | all-reduce | flops 16 | bytes 128 | tf_op jit(solution)/shard_map/psum | solution.py:270
  71.6 4.6 reshape.666
  78.3 4.9 reshape.667
  85.4 6.9 copy.138
  92.3 7.6 copy.139
  99.9 4.4 multiply_convert_fusion.13
  104.3 4.7 pad_slice_fusion.8
  125.3 4.9 convolution_convert_fusion.2
  132.1 4.1 fusion.129
  137.5 8.1 convolution_convert_fusion.1
  146.5 24.9 %copy.114 = bf16[9216,1024]{0,1:T(8,128)(2,1)} copy(bf16[9216,1024]{1,0:T(8,128)(2,1)} %bitcast.214) | data formatting | bytes 37748736 | tf_op jit(solution)/shard_map/reshape | solution.py:108
  171.4 15.8 %fusion.126 = (f32[512,32]{0,1:T(8,128)S(1)}, f32[512,32,32]{0,2,1:T(8,128)S(1)}) fusion(bf16[32,32,9216]{2,1,0:T(8,128)(2,1)} %bitcast.217, bf16[512,9216]{1,0:T(8,128)(2,1)} %constant_dynamic-update-slice_fusion), kind=kOutput, calls=%fused_computation.309 | convolution fusion | flops 9664184320 | bytes 30474240 | tf_op jit(solution)/shard_map/dot_general | solution.py:107
  190.2 6.1 reshape.668
  196.3 6.3 copy.140
  204.7 4.3 pad_slice_fusion
  225.6 16.4 %fusion.127 = (f32[512]{0:T(512)S(1)}, f32[512,1024]{1,0:T(8,128)S(1)}) fusion(bf16[512,9216]{1,0:T(8,128)(2,1)} %constant_dynamic-update-slice_fusion.8, bf16[9216,1024]{1,0:T(8,128)(2,1)} %bitcast.271, bf16[1,512,1024]{2,1,0:T(8,128)(2,1)S(1)} %copy-done.10), kind=kOutput, calls=%fused_computation.310 | convolution fusion | flops 9665773568 | bytes 31459328 | tf_op jit(solution)/shard_map/dot_general | solution.py:294
  243.7 6.9 convolution_convert_fusion
  257.4 3.8 fusion.128
  263.9 3.8 fusion.36
  270.8 5.9 multiply_reduce_fusion
  276.8 5.7 multiply_convert_fusion.4
  293.3 8.5 multiply_reduce_fusion.1
  305.2 18.0 %fusion.130 = f32[512,9216]{1,0:T(8,128)} fusion(bf16[512,1024]{1,0:T(8,128)(2,1)S(1)} %fusion.46, bf16[9216,1024]{1,0:T(8,128)(2,1)} %bitcast.272), kind=kOutput, calls=%fused_computation.313 | convolution fusion | flops 9663676416 | bytes 38797312 | tf_op jit(solution)/shard_map/pc,kc->pk/dot_general | solution.py:352
  323.3 8.6 slice_select_fusion.15
  337.7 4.7 reshape.632
  342.5 6.4 copy.125
  349.0 4.6 multiply_reduce_fusion.2
  357.6 9.5 multiply_convert_fusion.3
  369.0 9.4 fusion
  378.5 16.9 %multiply_convert_fusion = bf16[9216,1024]{1,0:T(8,128)(2,1)} fusion(f32[]{:T(128)S(6)} %div.191, bf16[512,9216]{1,0:T(8,128)(2,1)} %constant_dynamic-update-slice_fusion.8, bf16[512,1024]{1,0:T(8,128)(2,1)} %copy-done.53), kind=kOutput, calls=%fused_computation | convolution fusion | flops 9682550784 | bytes 29360132 | tf_op jit(solution)/shard_map/pk,pc->kc/dot_general | solution.py:365
  395.5 13.4 copy.134
  414.5 17.9 %multiply_convert_fusion.1 = bf16[9,1024,1024]{2,1,0:T(8,128)(2,1)} fusion(f32[]{:T(128)S(6)} %div.191, bf16[9,1024,512]{2,1,0:T(8,128)(2,1)} %bitcast.222, bf16[512,1024,1]{0,1,2:T(8,128)(2,1)S(1)} %bitcast.252), kind=kOutput, calls=%fused_computation.1 | convolution fusion | flops 9682550784 | bytes 29360132 | tf_op jit(solution)/shard_map/pk,pc->kc/dot_general | solution.py:369
  432.9 16.8 %reduce-scatter.11.cloned.1.call-done = bf16[9,512,1024]{2,1,0:T(8,128)(2,1)} async-done(((bf16[9,1024,1024]{2,1,0:T(8,128)(2,1)}), bf16[9,512,1024]{2,1,0:T(8,128)(2,1)}) %reduce-scatter.11.cloned.1.call-update) | async-done | bytes 9437200 | tf_op jit(solution)/shard_map/reduce_scatter | solution.py:392
  449.8 32.3 %reduce-scatter.7.cloned.1.call-done = bf16[9,512,1024]{2,1,0:T(8,128)(2,1)} async-done(((bf16[9,1024,1024]{2,1,0:T(8,128)(2,1)}), bf16[9,512,1024]{2,1,0:T(8,128)(2,1)}) %reduce-scatter.7.cloned.1.call-update) | async-done | bytes 9437200 | tf_op jit(solution)/shard_map/reduce_scatter | solution.py:383
  490.8 17.7 %fusion.131 = f32[512,9216]{1,0:T(8,128)} fusion(bf16[512,1024]{0,1:T(8,128)(2,1)S(1)} %bitcast.253, bf16[9216,1024]{1,0:T(8,128)(2,1)} %bitcast.215), kind=kOutput, calls=%fused_computation.314 | convolution fusion | flops 9663676416 | bytes 38797312 | tf_op jit(solution)/shard_map/pc,kc->pk/dot_general | solution.py:359
  508.5 8.8 slice_select_fusion.7
  523.1 4.7 reshape.643
  527.8 3.7 fusion.25
  531.6 4.0 all-reduce.30
  535.8 45.1 %all-reduce.28 = (bf16[512]{0:T(512)(128)(2,1)S(1)}, bf16[512]{0:T(512)(128)(2,1)S(1)}, bf16[1024]{0:T(1024)(128)(2,1)S(1)}, bf16[512]{0:T(512)(128)(2,1)S(1)}) all-reduce(bf16[512]{0:T(512)(128)(2,1)S(1)} %dynamic-slice.1, bf16[512]{0:T(512)(128)(2,1)S(1)} %dynamic-slice.3, ...), channel_id=1, replica_groups=mesh['wide'=16,'narrow'=2] {'wide'}, use_global_device_ids=true, to_apply=%region_20.21 | all-reduce | flops 2560 | bytes 10240 | tf_op jit(solution)/shard_map/psum | solution.py:235
  583.2 6.4 copy.128
  601.7 5.0 fusion.41
  606.8 4.8 fusion.20
  611.5 779.5 %all-reduce.33.cloned.1.call-done = (bf16[2048,2048]{0,1:T(8,128)(2,1)}, bf16[9,512,1024]{2,1,0:T(8,128)(2,1)}, bf16[512,2048]{1,0:T(8,128)(2,1)}, bf16[9,512,10...) async-done(((bf16[2048,2048]{0,1:T(8,128)(2,1)}, bf16[9,512,1024]{2,1,0:T(8,128)(2,1)}, bf16[512,2048]{1,0:T(8,128)(2,1)}, ...) | async-done | bytes 33554448 | tf_op jit(solution)/shard_map/psum | solution.py:244
  1400.4 13.0 copy.136
  1413.4 13.0 convert_element_type.297
  1426.4 13.0 convert_element_type.305
  (382 shorter events, 146.0 us)
Async XLA Ops:
  7.2 130.4 %copy-start = (bf16[1,128,4096]{2,1,0:T(8,128)(2,1)S(1)}, bf16[1,128,4096]{2,1,0:T(8,128)(2,1)}, u32[]{:S(2)}) copy-start(bf16[1,128,4096]{2,1,0:T(8,128)(2,1)} %param.20) | copy-start | bytes 3145732
  7.2 118.1 %all-gather.20.cloned.1.call-start = ((), (), s32[]{:S(2)}) async-start(), calls=%async_computation.11 | async-start | bytes 3145728 | tf_op jit(solution)/shard_map/all_gather | solution.py:283
  7.9 124.1 %all-gather.12.cloned.1.call-start = ((), (), s32[]{:S(2)}) async-start(), calls=%async_computation.7 | async-start | bytes 6291456 | tf_op jit(solution)/shard_map/all_gather | solution.py:276
  8.7 128.9 %all-gather.18.cloned.1.call-start = ((), (), s32[]{:S(2)}) async-start(), calls=%async_computation.10 | async-start | bytes 25165824 | tf_op jit(solution)/shard_map/all_gather | solution.py:284
  9.4 137.1 %all-gather.10.cloned.1.call-start = ((), (), s32[]{:S(2)}) async-start(), calls=%async_computation.6 | async-start | bytes 28311552 | tf_op jit(solution)/shard_map/all_gather | solution.py:275
  10.0 215.6 %all-gather.14.cloned.1.call-start = ((), (), s32[]{:S(2)}) async-start(), calls=%async_computation.8 | async-start | bytes 28311552 | tf_op jit(solution)/shard_map/all_gather | solution.py:278
  10.6 233.1 %all-gather.16.cloned.1.call-start = ((), (), s32[]{:S(2)}) async-start(), calls=%async_computation.9 | async-start | bytes 9437184 | tf_op jit(solution)/shard_map/all_gather | solution.py:282
  11.2 421.7 %reduce-scatter.15.cloned.1.call-start = ((), (), s32[]{:S(2)}) async-start(), calls=%async_computation.16 | async-start | bytes 3145728 | tf_op jit(solution)/shard_map/reduce_scatter | solution.py:317
  11.9 176.3 %copy-start.57 = (s32[512]{0:T(512)}, s32[512]{0:T(512)S(1)}, u32[]{:S(2)}) copy-start(s32[512]{0:T(512)S(1)} %add_select_fusion.4) | copy-start | bytes 6148
  14.4 55.6 %copy-start.1 = (f32[1,512,1024]{1,2,0:T(8,128)}, f32[1,512,1024]{1,2,0:T(8,128)S(1)}, u32[]{:S(2)}) copy-start(f32[1,512,1024]{1,2,0:T(8,128)S(1)} %copy.109) | copy-start | bytes 6291460
  14.4 45.6 %copy-start.99 = (bf16[512]{0:T(512)(128)(2,1)S(1)}, bf16[512]{0:T(512)(128)(2,1)}, u32[]{:S(2)}) copy-start(bf16[512]{0:T(512)(128)(2,1)} %param.22) | copy-start | bytes 3076
  14.4 47.4 %copy-start.100 = (bf16[512]{0:T(512)(128)(2,1)S(1)}, bf16[512]{0:T(512)(128)(2,1)}, u32[]{:S(2)}) copy-start(bf16[512]{0:T(512)(128)(2,1)} %param.23) | copy-start | bytes 3076
  14.4 49.2 %copy-start.101 = (bf16[512]{0:T(512)(128)(2,1)S(1)}, bf16[512]{0:T(512)(128)(2,1)}, u32[]{:S(2)}) copy-start(bf16[512]{0:T(512)(128)(2,1)} %param.28) | copy-start | bytes 3076
  14.4 51.6 %copy-start.97 = (bf16[1,1024]{1,0:T(2,128)(2,1)S(1)}, bf16[1,1024]{1,0:T(2,128)(2,1)}, u32[]{:S(2)}) copy-start(bf16[1,1024]{1,0:T(2,128)(2,1)} %param.19) | copy-start | bytes 6148
  14.5 52.2 %copy-start.98 = (bf16[1024]{0:T(1024)(128)(2,1)S(1)}, bf16[1024]{0:T(1024)(128)(2,1)}, u32[]{:S(2)}) copy-start(bf16[1024]{0:T(1024)(128)(2,1)} %param.26) | copy-start | bytes 6148
  60.0 128.0 %copy-start.73 = (f32[4]{0:T(128)}, f32[4]{0:T(128)S(1)}, u32[]{:S(2)}) copy-start(f32[4]{0:T(128)S(1)} %multiply_maximum_fusion) | copy-start | bytes 52
  61.8 7.4 copy-start.71
  66.0 51.5 %copy-start.64 = (f32[2,1,512]{2,1,0:T(1,128)}, f32[2,1,512]{2,1,0:T(1,128)S(1)}, u32[]{:S(2)}) copy-start(f32[2,1,512]{2,1,0:T(1,128)S(1)} %convert_element_type.320) | copy-start | bytes 12292
  66.0 51.4 %copy-start.66 = (f32[2,1,512]{2,1,0:T(1,128)}, f32[2,1,512]{2,1,0:T(1,128)S(1)}, u32[]{:S(2)}) copy-start(f32[2,1,512]{2,1,0:T(1,128)S(1)} %convert_element_type.319) | copy-start | bytes 12292
  68.6 155.6 %copy-start.85 = (pred[512]{0:T(512)(128)(4,1)}, pred[512]{0:T(512)(128)(4,1)S(1)}, u32[]{:S(2)}) copy-start(pred[512]{0:T(512)(128)(4,1)S(1)} %broadcast_in_dim.323) | copy-start | bytes 1540
  68.7 154.2 %copy-start.87 = (pred[512]{0:T(512)(128)(4,1)}, pred[512]{0:T(512)(128)(4,1)S(1)}, u32[]{:S(2)}) copy-start(pred[512]{0:T(512)(128)(4,1)S(1)} %broadcast_in_dim.321) | copy-start | bytes 1540
  68.8 152.8 %copy-start.88 = (pred[512]{0:T(512)(128)(4,1)}, pred[512]{0:T(512)(128)(4,1)S(1)}, u32[]{:S(2)}) copy-start(pred[512]{0:T(512)(128)(4,1)S(1)} %broadcast_in_dim.319) | copy-start | bytes 1540
  68.9 151.4 %copy-start.89 = (pred[512]{0:T(512)(128)(4,1)}, pred[512]{0:T(512)(128)(4,1)S(1)}, u32[]{:S(2)}) copy-start(pred[512]{0:T(512)(128)(4,1)S(1)} %broadcast_in_dim.317) | copy-start | bytes 1540
  69.0 148.4 %copy-start.90 = (pred[512]{0:T(512)(128)(4,1)}, pred[512]{0:T(512)(128)(4,1)S(1)}, u32[]{:S(2)}) copy-start(pred[512]{0:T(512)(128)(4,1)S(1)} %broadcast_in_dim.315) | copy-start | bytes 1540
  69.1 145.6 %copy-start.91 = (pred[512]{0:T(512)(128)(4,1)}, pred[512]{0:T(512)(128)(4,1)S(1)}, u32[]{:S(2)}) copy-start(pred[512]{0:T(512)(128)(4,1)S(1)} %broadcast_in_dim.313) | copy-start | bytes 1540
  69.2 141.2 %copy-start.92 = (pred[512]{0:T(512)(128)(4,1)}, pred[512]{0:T(512)(128)(4,1)S(1)}, u32[]{:S(2)}) copy-start(pred[512]{0:T(512)(128)(4,1)S(1)} %broadcast_in_dim.311) | copy-start | bytes 1540
  69.3 139.8 %copy-start.93 = (pred[512]{0:T(512)(128)(4,1)}, pred[512]{0:T(512)(128)(4,1)S(1)}, u32[]{:S(2)}) copy-start(pred[512]{0:T(512)(128)(4,1)S(1)} %broadcast_in_dim.308) | copy-start | bytes 1540
  71.4 6.7 copy-start.47
  243.7 58.2 %copy-start.94 = (f32[512]{0:T(512)}, f32[512]{0:T(512)S(1)}, u32[]{:S(2)}) copy-start(f32[512]{0:T(512)S(1)} %fusion.116) | copy-start | bytes 6148
  267.7 19.7 %copy-start.102 = (bf16[8,128,512]{2,1,0:T(8,128)(2,1)}, bf16[8,128,512]{2,1,0:T(8,128)(2,1)S(1)}, u32[]{:S(2)}) copy-start(bf16[8,128,512]{2,1,0:T(8,128)(2,1)S(1)} %fusion.36) | copy-start | bytes 3145732
  290.0 142.8 %reduce-scatter.9.cloned.1.call-start = ((), (), s32[]{:S(2)}) async-start(), calls=%async_computation.13 | async-start | bytes 6291456 | tf_op jit(solution)/shard_map/reduce_scatter | solution.py:386
  291.6 10.3 copy-start.50
  293.2 8.6 copy-start.51
  357.0 75.9 %reduce-scatter.13.cloned.1.call-start = ((), (), s32[]{:S(2)}) async-start(), calls=%async_computation.15 | async-start | bytes 9437184 | tf_op jit(solution)/shard_map/reduce_scatter | solution.py:314
  367.2 65.7 %reduce-scatter.17.cloned.1.call-start = ((), (), s32[]{:S(2)}) async-start(), calls=%async_computation.17 | async-start | bytes 25165824 | tf_op jit(solution)/shard_map/reduce_scatter | solution.py:320
  378.4 71.3 %reduce-scatter.11.cloned.1.call-start = ((), (), s32[]{:S(2)}) async-start(), calls=%async_computation.14 | async-start | bytes 28311552 | tf_op jit(solution)/shard_map/reduce_scatter | solution.py:392
  395.4 86.7 %reduce-scatter.7.cloned.1.call-start = ((), (), s32[]{:S(2)}) async-start(), calls=%async_computation.12 | async-start | bytes 28311552 | tf_op jit(solution)/shard_map/reduce_scatter | solution.py:383
  395.4 13.5 copy-start.58
  395.5 13.5 copy-start.61
  395.5 13.5 copy-start.74
  395.5 13.5 copy-start.78
  395.5 13.9 copy-start.60
  432.4 958.6 %all-reduce.33.cloned.1.call-start = ((), (), s32[]{:S(2)}) async-start(), calls=%async_computation.18 | async-start | bytes 67108864 | tf_op jit(solution)/shard_map/psum | solution.py:244
  490.8 17.7 %copy-start.86 = (pred[512]{0:T(512)(128)(4,1)S(1)}, pred[512]{0:T(512)(128)(4,1)}, u32[]{:S(2)}) copy-start(pred[512]{0:T(512)(128)(4,1)} %copy-done.85) | copy-start | bytes 1540
  583.2 6.5 copy-start.48
  583.2 6.5 copy-start.62
  583.2 6.5 copy-start.63
  598.7 8.0 copy-start.20
  (70 other events, 226.2 us)
Sparse Core Ops, SparseCore 0:
  9.6 13.2 all-gather.19
  24.4 14.8 all-gather.11
  40.9 31.2 all-gather.17
  73.6 34.9 all-gather.9
  110.0 34.9 all-gather.13
  146.4 17.9 all-gather.15
  290.2 8.9 reduce-scatter.14
  357.1 11.2 reduce-scatter.8
  371.3 15.7 reduce-scatter.12
  389.9 27.4 reduce-scatter.16
  420.3 29.4 reduce-scatter.10
  452.5 29.5 reduce-scatter.6
  488.5 902.4 all-reduce.32
where the time goes:
time: 1460 us; the launch traced here: 1450 us
  waiting for transfers between devices  833 us (57%)
  matrix products  186 us (13%)
  local copies, waits for them, and re-layouts  165 us (11%)
  other arithmetic  144 us (10%)
  blocking collectives  98.1 us (7%)
  between operations  18.7 us (1%)
    psum x1, waiting for transfers between devices, every_wide_sum(): lax.psum(parts[9].astype(jnp.bfloat16), 'wide').astype(jnp.float32)  780 us
    psum x1, blocking collectives, every_wide_sum(): lax.psum(parts[0].astype(jnp.bfloat16), 'wide').astype(jnp.float32)  45.1 us
    psum x1, blocking collectives, body(): counts = lax.psum(jnp.sum(onehot_groups, axis=0), ('wide', 'narrow'))  42 us
    reduce_scatter x1, waiting for transfers between devices, body(): lax.psum_scatter(res_big[0].astype(jnp.bfloat16), 'narrow', scatter_dimen...  32.3 us
  transfers between devices with their start and end apart: 13, of which 3 were waited for; matrix products, arithmetic and copies ran while one was open for 27% of the time, Pallas kernels for 0%

commit v1 on v0

--- a/solution.py
+++ b/solution.py
@@ -1,6 +1,10 @@
+import functools
+
 import jax
 import jax.numpy as jnp
 from jax import lax
+from jax.experimental import pallas as pl
+from jax.experimental.pallas import tpu as pltpu
 from jax.sharding import PartitionSpec as P
 
 NORM_GROUPS = 32
@@ -245,7 +249,7 @@
     )
 
 
-def body(
+def plain_body(
     pixels,
     layout,
     noise_group,
@@ -434,7 +438,787 @@
     )
 
 
+MESH = pl.DeviceIdType.MESH
+LAG_B, LAG_C, LAG_D = 1, 2, 3
+
+def comm_kernel(tx, qo, co, ci, tx_o, q_o, o_o, co_o, ci_o,
+                held, total, cross, from_x, from_y, from_d,
+                load_sem, s1s, s1r, s2s, s2r, s3s, s3r, xs, xr, ys, yr, d0s, d0r, d1s, d1r, out_sem):
+    n = 30
+    w = lax.axis_index("wide")
+    c = lax.axis_index("narrow")
+    p = w % 4
+    z = w // 4
+    wx = w + 1 - 2 * (w % 2)
+    wy = w + 2 - 4 * ((w // 2) % 2)
+    wz = w + 4 - 8 * (z % 2)
+    wm = (3 - z) * 4 + p
+    px = p + 1 - 2 * (p % 2)
+    py = p + 2 - 4 * (p // 2)
+    pd = 3 - p
+    is_mid = (z == 1) | (z == 2)
+    is_end = (z == 0) | (z == 3)
+
+    bar = pltpu.get_barrier_semaphore()
+    for t in (wx, wy, wz):
+        pl.semaphore_signal(bar, inc=1, device_id=(t, c), device_id_type=MESH)
+
+    @pl.when(is_mid)
+    def _():
+        pl.semaphore_signal(bar, inc=1, device_id=(wm, c), device_id_type=MESH)
+        pl.semaphore_wait(bar, 4)
+
+    @pl.when(is_end)
+    def _():
+        pl.semaphore_wait(bar, 3)
+
+    def remote(src, dst, ss, rs, t):
+        return pltpu.make_async_remote_copy(src_ref=src, dst_ref=dst, send_sem=ss, recv_sem=rs,
+                                            device_id=(t, c), device_id_type=MESH)
+
+    parts = ((tx, 0, 8), (qo, 8, 4), (co, 12, 9), (ci, 21, 9))
+
+    for ref, base, count in parts:
+        @pl.when(is_mid)
+        def _(ref=ref, base=base, count=count):
+            def go(i, _):
+                pltpu.make_async_copy(ref.at[i], held.at[base + i], load_sem.at[base + i]).start()
+                return 0
+            lax.fori_loop(0, count, go, 0)
+
+        @pl.when(is_end)
+        def _(ref=ref, base=base, count=count):
+            def go(i, _):
+                remote(ref.at[i], total.at[base + i], s1s.at[base + i], s1r.at[base + i], wz).start()
+                return 0
+            lax.fori_loop(0, count, go, 0)
+
+    def put_out(k, src, quarter, slot):
+        col = pl.multiple_of(quarter * 256, 256)
+        sem = out_sem.at[k, slot]
+        @pl.when(k < 8)
+        def _():
+            i = k // 2
+            j = k % 2
+            pltpu.make_async_copy(src, tx_o.at[pl.ds(pl.multiple_of(i * 512, 512), 512), pl.ds(pl.multiple_of(j * 1024 + col, 256), 256)], sem).start()
+        @pl.when((k >= 8) & (k < 11))
+        def _():
+            pltpu.make_async_copy(src, q_o.at[:, pl.ds(pl.multiple_of((k - 8) * 1024 + col, 256), 256)], sem).start()
+        @pl.when(k == 11)
+        def _():
+            pltpu.make_async_copy(src, o_o.at[:, pl.ds(col, 256)], sem).start()
+        @pl.when((k >= 12) & (k < 21))
+        def _():
+            pltpu.make_async_copy(src, co_o.at[k - 12, :, pl.ds(col, 256)], sem).start()
+        @pl.when(k >= 21)
+        def _():
+            pltpu.make_async_copy(src, ci_o.at[k - 21, :, pl.ds(col, 256)], sem).start()
+
+    def step(k, _):
+        @pl.when(is_mid & (k < n))
+        def _():
+            pltpu.make_async_copy(co.at[0], held.at[k], load_sem.at[k]).wait()
+            remote(total.at[k], total.at[k], s1s.at[k], s1r.at[k], wz).wait_recv()
+            held[k] = (held[k].astype(jnp.float32) + total[k].astype(jnp.float32)).astype(jnp.bfloat16)
+            remote(held.at[k], cross.at[k], s2s.at[k], s2r.at[k], wm).start()
+
+        kb = k - LAG_B
+
+        @pl.when((kb >= 0) & (kb < n))
+        def _():
+            @pl.when(is_mid)
+            def _():
+                remote(held.at[kb], cross.at[kb], s2s.at[kb], s2r.at[kb], wm).wait_recv()
+                total[kb] = (held[kb].astype(jnp.float32) + cross[kb].astype(jnp.float32)).astype(jnp.bfloat16)
+                remote(total.at[kb], total.at[kb], s3s.at[kb], s3r.at[kb], wz).start()
+            @pl.when(is_end)
+            def _():
+                remote(total.at[kb], total.at[kb], s3s.at[kb], s3r.at[kb], wz).wait_recv()
+            remote(total.at[kb], from_x.at[kb], xs.at[kb], xr.at[kb], wx).start()
+            remote(total.at[kb], from_y.at[kb], ys.at[kb], yr.at[kb], wy).start()
+            put_out(kb, total.at[kb], p, 0)
+
+        kc = k - LAG_C
+
+        @pl.when((kc >= 0) & (kc < n))
+        def _():
+            remote(total.at[kc], from_x.at[kc], xs.at[kc], xr.at[kc], wx).wait_recv()
+            remote(total.at[kc], from_y.at[kc], ys.at[kc], yr.at[kc], wy).wait_recv()
+            remote(from_y.at[kc, :256], from_d.at[kc, :256], d0s.at[kc], d0r.at[kc], wx).start()
+            remote(from_x.at[kc, 256:], from_d.at[kc, 256:], d1s.at[kc], d1r.at[kc], wy).start()
+            put_out(kc, from_x.at[kc], px, 1)
+            put_out(kc, from_y.at[kc], py, 2)
+
+        kd = k - LAG_D
+
+        @pl.when(kd >= 0)
+        def _():
+            remote(from_y.at[kd, :256], from_d.at[kd, :256], d0s.at[kd], d0r.at[kd], wx).wait_recv()
+            remote(from_x.at[kd, 256:], from_d.at[kd, 256:], d1s.at[kd], d1r.at[kd], wy).wait_recv()
+            put_out(kd, from_d.at[kd], pd, 3)
+        return 0
+
+    lax.fori_loop(0, n + LAG_D, step, 0)
+
+    def finish(k, _):
+        @pl.when(is_end)
+        def _():
+            remote(co.at[0], total.at[k], s1s.at[k], s1r.at[k], wz).wait_send()
+        @pl.when(is_mid)
+        def _():
+            remote(held.at[k], cross.at[k], s2s.at[k], s2r.at[k], wm).wait_send()
+            remote(total.at[k], total.at[k], s3s.at[k], s3r.at[k], wz).wait_send()
+        remote(total.at[k], from_x.at[k], xs.at[k], xr.at[k], wx).wait_send()
+        remote(total.at[k], from_y.at[k], ys.at[k], yr.at[k], wy).wait_send()
+        remote(from_y.at[k, :256], from_d.at[k, :256], d0s.at[k], d0r.at[k], wx).wait_send()
+        remote(from_x.at[k, 256:], from_d.at[k, 256:], d1s.at[k], d1r.at[k], wy).wait_send()
+        for slot in range(4):
+            pltpu.make_async_copy(total.at[k], co_o.at[0, :, pl.ds(0, 256)], out_sem.at[k, slot]).wait()
+        return 0
+
+    lax.fori_loop(0, n, finish, 0)
+
+
+def sum_and_gather(tx, qo, co, ci):
+    n = 30
+    bf = jnp.bfloat16
+    any_spec = pl.BlockSpec(memory_space=pl.ANY)
+    buf = pltpu.VMEM((n, 512, 256), bf)
+    dma = pltpu.SemaphoreType.DMA((n,))
+    return pl.pallas_call(
+        comm_kernel,
+        out_shape=(jax.ShapeDtypeStruct((2048, 2048), bf), jax.ShapeDtypeStruct((512, 3072), bf),
+                   jax.ShapeDtypeStruct((512, 1024), bf), jax.ShapeDtypeStruct((9, 512, 1024), bf),
+                   jax.ShapeDtypeStruct((9, 512, 1024), bf)),
+        in_specs=[any_spec] * 4,
+        out_specs=[any_spec] * 5,
+        scratch_shapes=[buf] * 6 + [dma] * 15 + [pltpu.SemaphoreType.DMA((n, 4))],
+        compiler_params=pltpu.CompilerParams(collective_id=0, has_side_effects=True, vmem_limit_bytes=60 << 20),
+        name="sum_and_gather",
+    )(tx, qo, co, ci)
+
+
+CHUNK = 256
+HALF_ROWS = 10 * MAP_W
+
+
+def quadrants(values):
+    grid = values.reshape(2, MAP_H // 2, 2, MAP_W // 2, values.shape[-1])
+    return [grid[a, :, b] for a in range(2) for b in range(2)]
+
+
+def rejoin(parts):
+    channels = parts[0].shape[-1]
+    top = jnp.concatenate(
+        [part.reshape(MAP_H // 2, 1, MAP_W // 2, channels) for part in parts[:2]], axis=1
+    )
+    low = jnp.concatenate(
+        [part.reshape(MAP_H // 2, 1, MAP_W // 2, channels) for part in parts[2:]], axis=1
+    )
+    return jnp.concatenate([top, low], axis=0).reshape(MAP_H * MAP_W, channels)
+
+
+def region_mean(parts, single, block_ones):
+    rows = jnp.concatenate(
+        [jnp.sum(part, axis=(0, 1), keepdims=True).reshape(1, -1) for part in parts], axis=0
+    )
+    rows = jnp.concatenate([rows, rows], axis=0)
+    sums = jnp.dot(rows, block_ones, precision=highest, preferred_element_type=jnp.float32)
+    quarter_count = (MAP_H * MAP_W // 4) * 32.0
+    whole = jnp.sum(sums[:4], axis=0, keepdims=True) * (0.25 / quarter_count)
+    return [jnp.where(single, whole, sums[i : i + 1] * (1.0 / quarter_count)) for i in range(4)]
+
+
+def normalise(parts, single, block_ones):
+    means = region_mean(parts, single, block_ones)
+    centred = [part - mean[None] for part, mean in zip(parts, means)]
+    spread = region_mean([part * part for part in centred], single, block_ones)
+    rates = [lax.rsqrt(value + epsilon) for value in spread]
+    return [part * rate[None] for part, rate in zip(centred, rates)], rates
+
+
+def group_ones():
+    row = lax.broadcasted_iota(jnp.int32, (CHUNK, CHUNK), 0) // 32
+    col = lax.broadcasted_iota(jnp.int32, (CHUNK, CHUNK), 1) // 32
+    return (row == col).astype(jnp.float32)
+
+
+def put_shifts(values, single, taps, lanes):
+    pixel = lax.broadcasted_iota(jnp.int32, values.shape, 0) % MAP_W
+    for s in range(3):
+        if s == 1:
+            moved = values
+        elif s == 2:
+            moved = pltpu.roll(values, MAP_H * MAP_W - 1, 0)
+            moved = jnp.where(
+                (pixel != MAP_W - 1) & (single | (pixel != MAP_W // 2 - 1)), moved, 0.0
+            )
+        else:
+            moved = pltpu.roll(values, 1, 0)
+            moved = jnp.where((pixel != 0) & (single | (pixel != MAP_W // 2)), moved, 0.0)
+        low = moved.astype(jnp.bfloat16)
+        blank = jnp.zeros((MAP_W, values.shape[1]), jnp.bfloat16)
+        taps[s, 0, 0:32, lanes] = blank
+        taps[s, 0, 32:288, lanes] = low[0:256]
+        taps[s, 0, 288:320, lanes] = jnp.where(single, moved[256:288], 0.0).astype(jnp.bfloat16)
+        taps[s, 1, 0:32, lanes] = jnp.where(single, moved[224:256], 0.0).astype(jnp.bfloat16)
+        taps[s, 1, 32:288, lanes] = low[256:512]
+        taps[s, 1, 288:320, lanes] = blank
+
+
+def tap_rows(taps, col_step, row_step, lanes):
+    rows = taps[col_step, :, pl.ds(pl.multiple_of(row_step * MAP_W, MAP_W), 256), lanes]
+    return rows.reshape(MAP_H * MAP_W, rows.shape[-1])
+
+
+def own_first(start, core, width):
+    return pl.ds(pl.multiple_of((start + core * 512) % 1024, width), width)
+
+
+def forward_conv_kernel(finish, info, x, scale, shift, w_own, w_far, *refs):
+    if finish:
+        pixels, ln_gain, low_out, joined_out, normed_out, taps, acc = refs
+    else:
+        low_out, acc, taps = refs
+    t = pl.program_id(0)
+    core = info[0]
+    single = info[1] == 1
+
+    @pl.when(t == 0)
+    def _():
+        ones = group_ones()
+        for start in range(0, 1024, CHUNK):
+            lanes = pl.ds(start, CHUNK)
+            parts = quadrants(x[:, lanes].astype(jnp.float32))
+            normed, _ = normalise(parts, single, ones)
+            pre = rejoin(normed) * scale[:, lanes] + shift[:, lanes]
+            act = pre * jax.nn.sigmoid(pre)
+            low_out[:, lanes] = act.astype(jnp.bfloat16)
+            put_shifts(act, single, taps, own_first(start, core, CHUNK))
+
+    rows = tap_rows(taps, t % 3, t // 3, slice(None))
+    fresh = jnp.dot(rows[:, :512], w_own[0], preferred_element_type=jnp.float32)
+    fresh += jnp.dot(rows[:, 512:], w_far[0], preferred_element_type=jnp.float32)
+
+    @pl.when(t == 0)
+    def _():
+        acc[...] = fresh
+
+    @pl.when(t > 0)
+    def _():
+        acc[...] += fresh
+
+    if finish:
+
+        @pl.when(t == 8)
+        def _():
+            joined = (pixels[...].astype(jnp.float32) + acc[...]) * inv_root_two
+            joined_out[...] = joined
+            centre = joined - jnp.mean(joined, axis=1, keepdims=True)
+            rate = lax.rsqrt(jnp.mean(centre * centre, axis=1, keepdims=True) + epsilon)
+            normed_out[...] = (centre * rate * ln_gain[...]).astype(jnp.bfloat16)
+
+
+def whole(shape):
+    return pl.BlockSpec(shape, lambda t, *_: (0,) * len(shape))
+
+
+def forward_conv(info, x, scale, shift, w_own, w_far, extra=None):
+    finish = extra is not None
+    full = jax.ShapeDtypeStruct((512, 1024), jnp.float32)
+    low = jax.ShapeDtypeStruct((512, 1024), jnp.bfloat16)
+    field = whole((512, 1024))
+    row = whole((1, 1024))
+    tap = pl.BlockSpec((1, 512, 1024), lambda t, *_: (t, 0, 0))
+    scratch = [pltpu.VMEM((3, 2, HALF_ROWS, 1024), jnp.bfloat16)]
+    if finish:
+        scratch += [pltpu.VMEM((512, 1024), jnp.float32)]
+    return pl.pallas_call(
+        functools.partial(forward_conv_kernel, finish),
+        out_shape=(low, full, low) if finish else (low, full),
+        grid_spec=pltpu.PrefetchScalarGridSpec(
+            num_scalar_prefetch=1,
+            grid=(9,),
+            in_specs=[field, row, row, tap, tap] + ([field, row] if finish else []),
+            out_specs=(field, field, field) if finish else (field, field),
+            scratch_shapes=scratch,
+        ),
+        compiler_params=pltpu.CompilerParams(vmem_limit_bytes=56 << 20),
+        name="forward_conv",
+    )(info, x, scale, shift, w_own, w_far, *(extra or ()))
+
+
+def backward_conv_kernel(add, info, weight, grad, x, scale, shift, w_own, w_far, *refs):
+    if add:
+        passed, result, sums_out, taps, acc = refs
+    else:
+        result, weighted, sums_out, taps, acc = refs
+    t = pl.program_id(0)
+    core = info[0]
+    single = info[1] == 1
+
+    @pl.when(t == 0)
+    def _():
+        for start in range(0, 1024, CHUNK):
+            lanes = pl.ds(start, CHUNK)
+            put_shifts(grad[:, lanes].astype(jnp.float32), single, taps, lanes)
+
+    rows = tap_rows(taps, 2 - t % 3, 2 - t // 3, slice(None))
+    last = (((1,), (1,)), ((), ()))
+    fresh_own = lax.dot_general(rows, w_own[0], last, preferred_element_type=jnp.float32)
+    fresh_far = lax.dot_general(rows, w_far[0], last, preferred_element_type=jnp.float32)
+
+    @pl.when(t == 0)
+    def _():
+        acc[:, :512] = fresh_own
+        acc[:, 512:] = fresh_far
+
+    @pl.when(t > 0)
+    def _():
+        acc[:, :512] += fresh_own
+        acc[:, 512:] += fresh_far
+
+    @pl.when(t == 8)
+    def _():
+        ones = group_ones()
+        for start in range(0, 1024, CHUNK):
+            lanes = pl.ds(start, CHUNK)
+            parts = quadrants(x[:, lanes].astype(jnp.float32))
+            normed, rates = normalise(parts, single, ones)
+            gains = scale[:, lanes]
+            pre = [part * gains[None] + shift[:, lanes][None] for part in normed]
+            grads = quadrants(acc[:, own_first(start, core, CHUNK)])
+            sig = [jax.nn.sigmoid(part) for part in pre]
+            grads = [g * s * (1.0 + v * (1.0 - s)) for g, s, v in zip(grads, sig, pre)]
+            gain_sum = sum(
+                jnp.sum(g * n, axis=(0, 1), keepdims=True).reshape(1, CHUNK)
+                for g, n in zip(grads, normed)
+            )
+            bias_sum = sum(
+                jnp.sum(g, axis=(0, 1), keepdims=True).reshape(1, CHUNK) for g in grads
+            )
+            sums_out[0:1, lanes] = gain_sum
+            sums_out[1:2, lanes] = bias_sum
+            grads = [g * gains[None] for g in grads]
+            mean = region_mean(grads, single, ones)
+            slope = region_mean([g * n for g, n in zip(grads, normed)], single, ones)
+            back = rejoin(
+                [
+                    r[None] * (g - m[None] - n * s[None])
+                    for r, g, m, n, s in zip(rates, grads, mean, normed, slope)
+                ]
+            )
+            if add:
+                back += passed[:, lanes] * inv_root_two
+                result[:, lanes] = back.astype(jnp.bfloat16)
+            else:
+                result[:, lanes] = back.astype(jnp.bfloat16)
+                weighted[:, lanes] = (back * weight[0]).astype(jnp.bfloat16)
+
+
+def backward_conv(info, weight, grad, x, scale, shift, w_own, w_far, passed=None):
+    add = passed is not None
+    low = jax.ShapeDtypeStruct((512, 1024), jnp.bfloat16)
+    sums = jax.ShapeDtypeStruct((2, 1024), jnp.float32)
+    field = whole((512, 1024))
+    row = whole((1, 1024))
+    pair = whole((2, 1024))
+    tap = pl.BlockSpec((1, 512, 1024), lambda t, *_: (t, 0, 0))
+    return pl.pallas_call(
+        functools.partial(backward_conv_kernel, add),
+        out_shape=(low, sums) if add else (low, low, sums),
+        grid_spec=pltpu.PrefetchScalarGridSpec(
+            num_scalar_prefetch=2,
+            grid=(9,),
+            in_specs=[field, field, row, row, tap, tap] + ([field] if add else []),
+            out_specs=(field, pair) if add else (field, field, pair),
+            scratch_shapes=[
+                pltpu.VMEM((3, 2, HALF_ROWS, 1024), jnp.bfloat16),
+                pltpu.VMEM((512, 1024), jnp.float32),
+            ],
+        ),
+        compiler_params=pltpu.CompilerParams(vmem_limit_bytes=56 << 20),
+        name="backward_conv",
+    )(info, weight, grad, x, scale, shift, w_own, w_far, *([passed] if add else []))
+
+
+def conv_term_kernel(layouts, a0, a1, a2, a3, b_own, b_far, out, taps):
+    t = pl.program_id(0)
+
+    @pl.when(t == 0)
+    def _():
+        for j in range(4):
+            for e, b in enumerate((b_own, b_far)):
+                put_shifts(
+                    b[j].astype(jnp.float32), layouts[2 * j + e] == 1, taps.at[2 * j + e], slice(None)
+                )
+
+    total = jnp.zeros((512, CHUNK), jnp.float32)
+    for j, a in enumerate((a0, a1, a2, a3)):
+        for e in range(2):
+            rows = tap_rows(taps.at[2 * j + e], 2 - t % 3, 2 - t // 3, slice(None))
+            total += jnp.dot(a[e], rows, preferred_element_type=jnp.float32)
+    out[0] = total.astype(jnp.bfloat16)
+
+
+def conv_term(layouts, sources, b_own, b_far):
+    return pl.pallas_call(
+        conv_term_kernel,
+        out_shape=jax.ShapeDtypeStruct((9, 512, CHUNK), jnp.bfloat16),
+        grid_spec=pltpu.PrefetchScalarGridSpec(
+            num_scalar_prefetch=1,
+            grid=(9,),
+            in_specs=[whole((2, 512, 512))] * 4 + [whole((4, 512, CHUNK))] * 2,
+            out_specs=pl.BlockSpec((1, 512, CHUNK), lambda t, *_: (t, 0, 0)),
+            scratch_shapes=[pltpu.VMEM((8, 3, 2, HALF_ROWS, CHUNK), jnp.bfloat16)],
+        ),
+        compiler_params=pltpu.CompilerParams(vmem_limit_bytes=56 << 20),
+        name="conv_term",
+    )(layouts, *sources, b_own, b_far)
+
+
+def text_term_kernel(a0, a1, a2, a3, b_own, b_far, out):
+    left = jnp.concatenate([a[e] for a in (a0, a1, a2, a3) for e in range(2)], axis=1)
+    right = jnp.concatenate([b[j] for j in range(4) for b in (b_own, b_far)], axis=0)
+    total = jnp.dot(left, right, preferred_element_type=jnp.float32).astype(jnp.bfloat16)
+    out[0] = total[:, :CHUNK]
+    out[1] = total[:, CHUNK:]
+
+
+def text_term(sources, b_own, b_far):
+    rows = pl.BlockSpec((2, 512, TEXT_LEN), lambda i: (0, i, 0))
+    cols = pl.BlockSpec((4, TEXT_LEN, 2 * CHUNK), lambda i: (0, 0, 0))
+    return pl.pallas_call(
+        text_term_kernel,
+        out_shape=jax.ShapeDtypeStruct((8, 512, CHUNK), jnp.bfloat16),
+        grid=(4,),
+        in_specs=[rows] * 4 + [cols] * 2,
+        out_specs=pl.BlockSpec((2, 512, CHUNK), lambda i: (i, 0, 0)),
+        name="text_term",
+    )(*sources, b_own, b_far)
+
+
+def attn_term_kernel(normed_own, normed_far, mixed_own, mixed_far, t_own, t_far, c_own, c_far, out):
+    j = pl.program_id(1)
+
+    @pl.when(j < 3)
+    def _():
+        total = jnp.dot(normed_own[...], t_own[...], preferred_element_type=jnp.float32)
+        total += jnp.dot(normed_far[...], t_far[...], preferred_element_type=jnp.float32)
+        out[0, 0] = total.astype(jnp.bfloat16)
+
+    @pl.when(j == 3)
+    def _():
+        total = jnp.dot(mixed_own[...], c_own[...], preferred_element_type=jnp.float32)
+        total += jnp.dot(mixed_far[...], c_far[...], preferred_element_type=jnp.float32)
+        out[0, 0] = total.astype(jnp.bfloat16)
+
+
+def attn_term(normed_pair, mixed_pair, triple_pair, cot_pair):
+    left = pl.BlockSpec((512, 512), lambda q, j: (0, 0))
+    triple = pl.BlockSpec((512, CHUNK), lambda q, j: (0, 4 * jnp.minimum(j, 2) + q))
+    cot = pl.BlockSpec((512, CHUNK), lambda q, j: (0, q))
+    return pl.pallas_call(
+        attn_term_kernel,
+        out_shape=jax.ShapeDtypeStruct((4, 4, 512, CHUNK), jnp.bfloat16),
+        grid=(4, 4),
+        in_specs=[left] * 4 + [triple] * 2 + [cot] * 2,
+        out_specs=pl.BlockSpec((1, 1, 512, CHUNK), lambda q, j: (q, j, 0, 0)),
+        name="attn_term",
+    )(*normed_pair, *mixed_pair, *triple_pair, *cot_pair)
+
+
+def to_wide(value, step):
+    return lax.ppermute(value, "wide", [(i, i ^ step) for i in range(16)])
+
+
+def to_far(value):
+    return lax.ppermute(value, "narrow", [(0, 1), (1, 0)])
+
+
+def gather_all(row):
+    rows = row[None]
+    rows = jnp.concatenate([rows, to_far(rows)])
+    for step in (1, 2, 4, 8):
+        rows = jnp.concatenate([rows, to_wide(rows, step)])
+    return rows
+
+
+def half_of(value, core, axis):
+    size = value.shape[axis] // 2
+    return lax.dynamic_slice_in_dim(value, core * size, size, axis)
+
+
+def share_source(value_t, core):
+    far = to_far(half_of(value_t, 1 - core, 0))
+    pair = jnp.stack([half_of(value_t, core, 0), far])
+    return (pair, to_wide(pair, 1), to_wide(pair, 2), to_wide(pair, 3))
+
+
+def share_grad(grad, place):
+    rows, blocks, _ = grad.shape
+    found = []
+    for step in range(4):
+        start = CHUNK * jnp.bitwise_xor(place, step)
+        piece = lax.dynamic_slice_in_dim(grad, start, CHUNK, 2).reshape(rows, blocks * CHUNK)
+        found.append(to_wide(piece, step) if step else piece)
+    own = jnp.stack(found)
+    return own, to_far(own)
+
+
+def pair_body(
+    pixels,
+    layout,
+    noise_group,
+    cond_embed,
+    text_embed,
+    cotangent,
+    gn_gain,
+    gn_bias,
+    conv_in,
+    film_weight,
+    film_bias,
+    conv_out,
+    ln_gain,
+    qkv_weight,
+    out_weight,
+    text_weight,
+):
+    f32, bf16 = jnp.float32, jnp.bfloat16
+    wide = lax.axis_index("wide")
+    core = lax.axis_index("narrow")
+    place = wide % 4
+    group_total = lax.axis_size("wide")
+
+    conv_in_far = to_far(conv_in)
+    vectors = jnp.concatenate([gn_gain, gn_bias, ln_gain, film_bias])
+    vectors_far = to_far(vectors)
+    low_vec = jnp.where(core == 0, vectors, vectors_far)
+    high_vec = jnp.where(core == 0, vectors_far, vectors)
+
+    def joined_vec(start, size):
+        return jnp.concatenate([low_vec[start : start + size], high_vec[start : start + size]])
+
+    gain_row = joined_vec(0, 512).astype(f32)[None]
+    bias_row = joined_vec(512, 512).astype(f32)[None]
+    ln_row = joined_vec(1024, 512).astype(f32)[None]
+    film_bias_full = joined_vec(1536, 1024).astype(f32)
+    conv_out_far = to_far(conv_out)
+
+    facts = jnp.stack([noise_group[0], layout[0]])
+    facts = jnp.pad(facts.astype(f32), (0, 126))
+    early = gather_all(jnp.concatenate([cond_embed[0].astype(f32), facts]))
+    cond_all = early[:, :1024]
+    alike = jnp.sum((early[:, 1024] == facts[0]).astype(f32))
+    weight = 1.0 / (group_total * alike)
+    info = jnp.stack([core.astype(jnp.int32), layout[0]])
+    layouts = early[:8, 1025].astype(jnp.int32)
+    weight_row = weight.reshape(1)
+
+    text_one = text_embed[0]
+    text_sources = share_source(text_one.T, core)
+    cot = cotangent[0]
+    film_full = lax.all_gather(film_weight, "narrow", axis=0, tiled=True)
+    qkv_full = lax.all_gather(qkv_weight, "narrow", axis=0, tiled=True)
+    out_full = lax.all_gather(out_weight, "narrow", axis=0, tiled=True)
+    text_full = lax.all_gather(text_weight, "narrow", axis=0, tiled=True)
+
+    region_ids = region_ids_of(layout[0])
+    field = pixels[0]
+    condition = jax.nn.silu(cond_embed[0].astype(f32)).astype(bf16)
+    film_out = jnp.dot(condition, film_full, preferred_element_type=f32) + film_bias_full
+    film_scale = 1.0 + film_out[None, :1024]
+    film_shift = film_out[None, 1024:]
+
+    first_low, hidden_one = forward_conv(info, field, gain_row, bias_row, conv_in, conv_in_far)
+    first_sources = share_source(first_low.T, core)
+    second_low, joined, normed = forward_conv(
+        info, hidden_one, film_scale, film_shift, conv_out, conv_out_far, (field, ln_row)
+    )
+    second_sources = share_source(second_low.T, core)
+
+    attn_full = (ln_row[0], qkv_full, out_full, text_full)
+    result, stored = attention_mid(normed, joined, text_one, region_ids, attn_full)
+    output = result.astype(bf16)
+    grad_joined, ln_term, grad_triple, grad_pair = attention_back(
+        cot, joined, stored, attn_full
+    )
+    mixed = stored[5]
+    grad_two = grad_joined * inv_root_two
+    grad_two_low = grad_two.astype(bf16)
+
+    triple_w = (weight * grad_triple).astype(bf16)
+    pair_w = (weight * grad_pair).astype(bf16)
+    cot_w = (weight * cot.astype(f32)).astype(bf16)
+    two_w = (weight * grad_two).astype(bf16)
+
+    pair_own, pair_far = share_grad(pair_w.reshape(TEXT_LEN, 2, 1024), place)
+    text_part = text_term(text_sources, pair_own, pair_far)
+
+    normed_t, mixed_t = normed.T, mixed.T
+    normed_pair = (half_of(normed_t, core, 0), to_far(half_of(normed_t, 1 - core, 0)))
+    mixed_pair = (half_of(mixed_t, core, 0), to_far(half_of(mixed_t, 1 - core, 0)))
+    attn_part = attn_term(
+        normed_pair, mixed_pair, (triple_w, to_far(triple_w)), (cot_w, to_far(cot_w))
+    )
+    plane = [[4 * z + i for i in range(4)] for z in range(4)]
+    attn_part = lax.psum_scatter(
+        attn_part, "wide", scatter_dimension=0, axis_index_groups=plane, tiled=True
+    )[0]
+
+    two_own, two_far = share_grad(two_w.reshape(512, 1, 1024), place)
+    conv_out_part = conv_term(layouts, second_sources, two_own, two_far)
+
+    hidden_low, hidden_w, film_sums = backward_conv(
+        info, weight_row, grad_two_low, hidden_one, film_scale, film_shift, conv_out, conv_out_far
+    )
+    hid_own, hid_far = share_grad(hidden_w.reshape(512, 1, 1024), place)
+    conv_in_part = conv_term(layouts, first_sources, hid_own, hid_far)
+    input_grad, gn_sums = backward_conv(
+        info, weight_row, hidden_low, field, gain_row, bias_row, conv_in, conv_in_far, grad_joined
+    )
+
+    small = jnp.concatenate(
+        [film_sums.reshape(-1), gn_sums.reshape(-1), ln_term.reshape(-1)]
+    )
+    small_all = gather_all(weight * small)
+    cond_low = jax.nn.silu(cond_all).astype(bf16)
+    grad_film_weight = lax.dot_general(
+        half_of(cond_low, core, 1),
+        small_all[:, :2048].astype(bf16),
+        (((0,), (0,)), ((), ())),
+        preferred_element_type=f32,
+    )
+    small_sum = jnp.sum(small_all, axis=0)
+    grad_film_bias = half_of(small_sum[:2048], core, 0)
+    grad_gn_gain = half_of(small_sum[2048:3072], core, 0)
+    grad_gn_bias = half_of(small_sum[3072:4096], core, 0)
+    grad_ln_gain = half_of(small_sum[4096:], core, 0)
+
+    grad_text, grad_qkv, grad_out, grad_conv_out, grad_conv_in = sum_and_gather(
+        text_part, attn_part, conv_out_part, conv_in_part
+    )
+    return (
+        output[None],
+        input_grad[None],
+        grad_gn_gain,
+        grad_gn_bias,
+        grad_conv_in.astype(f32),
+        grad_film_weight,
+        grad_film_bias,
+        grad_conv_out.astype(f32),
+        grad_ln_gain,
+        grad_qkv.astype(f32),
+        grad_out.astype(f32),
+        grad_text.astype(f32),
+    )
+
+
+def attention_mid(normed_low, joined, text_one, region_ids, attn_full):
+    _, qkv_full, out_full, text_full = attn_full
+    pixel_count, channels = joined.shape
+    head_dim = channels // HEADS
+    score_scale = head_dim ** (-0.5)
+    triple = jnp.dot(normed_low, qkv_full, preferred_element_type=jnp.float32).astype(jnp.bfloat16)
+    text_pair = jnp.dot(text_one, text_full, preferred_element_type=jnp.float32).astype(
+        jnp.bfloat16
+    )
+    queries = triple[:, :channels].reshape(pixel_count, HEADS, head_dim)
+    key_rows = jnp.concatenate(
+        [triple[:, channels : 2 * channels], text_pair[:, :channels]], axis=0
+    ).reshape(-1, HEADS, head_dim)
+    value_rows = jnp.concatenate(
+        [triple[:, 2 * channels :], text_pair[:, channels:]], axis=0
+    ).reshape(-1, HEADS, head_dim)
+    allowed = allowed_keys(region_ids)
+    masked = jnp.where(
+        allowed[None],
+        jnp.einsum("phd,jhd->hpj", queries, key_rows, preferred_element_type=jnp.float32)
+        * score_scale,
+        masked_score,
+    )
+    row_peak = jnp.max(masked, axis=2, keepdims=True)
+    exponent = jnp.exp(masked - row_peak)
+    exp_total = jnp.sum(exponent, axis=2, keepdims=True)
+    attn_probs = exponent / exp_total
+    log_total = row_peak + jnp.log(exp_total)
+    mixed = (
+        jnp.einsum(
+            "hpj,jhd->phd",
+            attn_probs.astype(jnp.bfloat16),
+            value_rows,
+            preferred_element_type=jnp.float32,
+        )
+        .reshape(pixel_count, channels)
+        .astype(jnp.bfloat16)
+    )
+    result = joined + jnp.dot(mixed, out_full, preferred_element_type=jnp.float32)
+    return (result, (normed_low, queries, key_rows, value_rows, log_total, mixed, allowed))
+
+
+def attention_back(grad_result, joined, stored, attn_full):
+    gain_row, qkv_full, out_full, text_full = attn_full
+    normed_low, queries, key_rows, value_rows, log_total, mixed, allowed = stored
+    pixel_count, channels = joined.shape
+    head_dim = channels // HEADS
+    score_scale = head_dim ** (-0.5)
+    grad_mixed = (
+        jnp.einsum("pd,cd->pc", grad_result, out_full, preferred_element_type=jnp.float32)
+        .astype(jnp.bfloat16)
+        .reshape(pixel_count, HEADS, head_dim)
+    )
+    masked = jnp.where(
+        allowed[None],
+        jnp.einsum("phd,jhd->hpj", queries, key_rows, preferred_element_type=jnp.float32)
+        * score_scale,
+        masked_score,
+    )
+    attn_probs = jnp.exp(masked - log_total)
+    grad_probs = jnp.einsum(
+        "phd,jhd->hpj", grad_mixed, value_rows, preferred_element_type=jnp.float32
+    )
+    grad_values = jnp.einsum(
+        "hpj,phd->jhd",
+        attn_probs.astype(jnp.bfloat16),
+        grad_mixed,
+        preferred_element_type=jnp.float32,
+    )
+    row_inner = jnp.sum(attn_probs * grad_probs, axis=2, keepdims=True)
+    grad_scores = (attn_probs * (grad_probs - row_inner)).astype(jnp.bfloat16)
+    grad_queries = (
+        jnp.einsum("hpj,jhd->phd", grad_scores, key_rows, preferred_element_type=jnp.float32)
+        * score_scale
+    )
+    grad_keys = (
+        jnp.einsum("hpj,phd->jhd", grad_scores, queries, preferred_element_type=jnp.float32)
+        * score_scale
+    )
+    grad_triple = jnp.concatenate(
+        [
+            grad_queries.reshape(pixel_count, channels),
+            grad_keys[:pixel_count].reshape(pixel_count, channels),
+            grad_values[:pixel_count].reshape(pixel_count, channels),
+        ],
+        axis=1,
+    )
+    grad_pair = jnp.concatenate(
+        [
+            grad_keys[pixel_count:].reshape(-1, channels),
+            grad_values[pixel_count:].reshape(-1, channels),
+        ],
+        axis=1,
+    )
+    grad_normed = jnp.einsum(
+        "pk,ck->pc", grad_triple.astype(jnp.bfloat16), qkv_full, preferred_element_type=jnp.float32
+    )
+    _, norm_back = jax.vjp(layer_norm, joined, gain_row)
+    grad_joined_norm, term_gain = norm_back(grad_normed)
+    return (grad_result.astype(jnp.float32) + grad_joined_norm, term_gain, grad_triple, grad_pair)
+
+
 def solution(mesh):
+    fits = mesh.shape["wide"] == 16 and mesh.shape["narrow"] == 2
+    body = pair_body if fits else plain_body
     placed = (
         P(("wide", "narrow"), None, None),
         P(("wide", "narrow")),

time: 1460 us -> 790 us (0.54)
  waiting for transfers between devices: 833 us -> 95.9 us
  Pallas kernels: 0 us -> 434 us
  matrix products: 186 us -> 55 us
  local copies, waits for them, and re-layouts: 165 us -> 56.5 us
  blocking collectives: 98.1 us -> 0 us
  other arithmetic: 144 us -> 81.2 us
  starting transfers between devices: 1.1 us -> 42.3 us
    psum x1 -> x0, waiting for transfers between devices: 780 us -> none  [every_wide_sum(): lax.psum(parts[9].astype(jnp.bfloat16), 'wide').astype(jnp.float32)]
    pallas_call x0 -> x9, Pallas kernels: none -> 434 us  [the longest x1 283 us: sum_and_gather(): pl.pallas_call(comm_kernel, out_shape=(jax.ShapeDtypeStruct((2048, 2048),...]
    dot_general x37 -> x13, matrix products: 186 us -> 55 us  [the longest x1 10 us: attention_back(): jnp.einsum('pk,ck->pc', grad_triple.astype(jnp.bfloat16), qkv_full, prefe...]
    ppermute x0 -> x41, waiting for transfers between devices: none -> 93.2 us  [the longest x26 81.2 us: to_wide(): return lax.ppermute(value, 'wide', [(i, i ^ step) for i in range(16)])]
    psum x2 -> x0, blocking collectives: 87 us -> none  [the longest x1 45.1 us: every_wide_sum(): lax.psum(parts[0].astype(jnp.bfloat16), 'wide').astype(jnp.float32)]
    reshape x11 -> x6, local copies, waits for them, and re-layouts: 68.5 us -> 13.6 us  [the longest x1 2.93 us: attention_back(): grad_keys[:pixel_count].reshape(pixel_count, channels)]
    reduce_scatter x6 -> x0, waiting for transfers between devices: 49.2 us -> none  [the longest x1 32.3 us: body(): lax.psum_scatter(res_big[0].astype(jnp.bfloat16), 'narrow', scatter_dimen...]
    ppermute x0 -> x41, starting transfers between devices: none -> 42.1 us  [the longest x26 38.3 us: to_wide(): return lax.ppermute(value, 'wide', [(i, i ^ step) for i in range(16)])]
  transfers between devices with their start and end apart: 13 -> 46, of which waited for: 3 -> 16; matrix products, arithmetic and copies ran while one was open for 27% -> 19% of each run, Pallas kernels for 0% -> 17%
where the time goes in v1:
time: 790 us; the launch traced here: 782 us
  Pallas kernels  434 us (55%)
  waiting for transfers between devices  95.9 us (12%)
  other arithmetic  81.2 us (10%)
  local copies, waits for them, and re-layouts  56.5 us (7%)
  matrix products  55 us (7%)
  starting transfers between devices  42.3 us (5%)
  between operations  17 us (2%)
    pallas_call x1, Pallas kernels, sum_and_gather(): pl.pallas_call(comm_kernel, out_shape=(jax.ShapeDtypeStruct((2048, 2048),...  283 us
    ppermute x26, waiting for transfers between devices, to_wide(): return lax.ppermute(value, 'wide', [(i, i ^ step) for i in range(16)])  81.2 us
    pallas_call x2, Pallas kernels, backward_conv(): pl.pallas_call(functools.partial(backward_conv_kernel, add), out_shape=(l...  49.7 us
    pallas_call x2, Pallas kernels, forward_conv(): pl.pallas_call(functools.partial(forward_conv_kernel, finish), out_shape=...  46.4 us
    ppermute x26, starting transfers between devices, to_wide(): return lax.ppermute(value, 'wide', [(i, i ^ step) for i in range(16)])  38.3 us
    pallas_call x2, Pallas kernels, conv_term(): pl.pallas_call(conv_term_kernel, out_shape=jax.ShapeDtypeStruct((9, 512,...  34 us
  transfers between devices with their start and end apart: 46, of which 16 were waited for; matrix products, arithmetic and copies ran while one was open for 19% of the time, Pallas kernels for 17%

profile of v1, /device:TPU:0, one launch (start us, length us, event | category | flops | bytes accessed | tf_op | source)
XLA Modules:
  0.0 782.0 jit_solution(16950318506879517745)
XLA Ops:
  14.4 10.5 %collective-permute-done.3 = f32[1,1152]{1,0:T(1,128)S(1)} collective-permute-done((f32[1,1152]{1,0:T(1,128)S(1)}, f32[1,1152]{1,0:T(1,128)S(1)}, u32[]{:S(2)}, u32[]{:S(2)}) %collective-permute-start.3) | collective-permute-done | bytes 4640 | tf_op jit(solution)/shard_map/ppermute | solution.py:936
  24.9 2.9 collective-permute-start.4
  37.5 3.5 collective-permute-start.7
  44.8 2.9 convolution_convert_fusion.2
  49.0 2.8 fusion.58
  52.5 21.0 %forward_conv.2 = (bf16[512,1024]{1,0:T(8,128)(2,1)}, f32[512,1024]{1,0:T(8,128)}) custom-call(s32[2]{0:T(128)} %pad_add_fusion.info, bf16[512,1024]{1,0:T(8,128)(2,1)} %bitcast.147, f32[1,1024]{1,0:T(1,128)} %maximum_convert_fusion.scale, f32[1,1024]{1,0:T(1,128)} %maximum_convert_fusion.1.shift, bf16[9,512,1024]{2,1,0:T(8,128)(2,1)} %w_own.7, ...), custom_call_target="tpu_custom_call" | custom-call | tf_op jit(solution)/shard_map/forward_conv/pallas_call | solution.py:736
  73.5 25.3 %forward_conv.3 = (bf16[512,1024]{1,0:T(8,128)(2,1)}, f32[512,1024]{1,0:T(8,128)}, bf16[512,1024]{1,0:T(8,128)(2,1)}) custom-call(s32[2]{0:T(128)} %pad_add_fusion.info, f32[512,1024]{1,0:T(8,128)} %get-tuple-element.27.x, f32[1,1024]{1,0:T(1,128)} %bitcast.176, f32[1,1024]{1,0:T(1,128)} %bitcast.174, bf16[9,512,1024]{2,1,0:T(8,128)(2,1)} %w_own.6, ...), custom_call_target="tpu_custom_call" | custom-call | tf_op jit(solution)/shard_map/forward_conv/pallas_call | solution.py:736
  101.1 6.5 convolution_convert_fusion
  111.1 2.7 dynamic-slice_bitcast_fusion.6
  114.9 8.5 %convolution_convert_fusion.1 = bf16[128,2048]{1,0:T(8,128)(2,1)S(1)} fusion(bf16[4096,2048]{1,0:T(8,128)(2,1)} %all-gather.9.cloned.1.call-done, bf16[1,128,4096]{2,1,0:T(8,128)(2,1)} %param.20), kind=kOutput, calls=%fused_computation.20 | convolution fusion | flops 2147745792 | bytes 18350080 | tf_op jit(solution)/shard_map/dot_general | solution.py:1123
  127.2 2.5 fusion.57
  129.8 2.3 fusion
  132.2 2.8 fusion.10
  135.3 4.9 multiply_reduce_fusion
  140.3 2.4 multiply_convert_fusion
  144.0 3.2 convolution_multiply_fusion
  148.8 2.9 copy.114
  153.3 2.9 copy.113
  156.2 2.9 copy.112
  159.1 4.6 multiply_convert_fusion.1.t_own
  163.8 10.0 %multiply_reduce_fusion.1 = (f32[1024]{0:T(1024)S(1)}, f32[512]{0:T(512)S(1)}, f32[512,1024]{1,0:T(8,128)}) fusion(f32[512,1024]{1,0:T(8,128)S(1)} %copy-done.3, f32[512]{0:T(512)S(1)} %copy-done.58, f32[512]{0:T(512)S(1)} %broadcast_multiply_fusion, f32[1024]{0:T(1024)S(1)} %copy-done.57, bf16[1024,3072]{1,0:T(8,128)(2,1)} %all-gather.7.cloned.1.call-done, ...), kind=kOutput, calls=%fused_computation.23 | convolution fusion | flops 3234331136 | bytes 16791552 | tf_op jit(solution)/shard_map/pk,ck->pc/dot_general | solution.py:1211
  174.4 2.4 fusion.46
  179.1 3.8 fusion.13
  187.0 15.3 %attn_term.1 = bf16[4,4,512,256]{3,2,1,0:T(8,128)(2,1)} custom-call(bf16[512,512]{1,0:T(8,128)(2,1)} %get-tuple-element.69.normed_own, bf16[512,512]{1,0:T(8,128)(2,1)} %collective-permute-done.21.normed_far, bf16[512,512]{1,0:T(8,128)(2,1)} %get-tuple-element.67.mixed_own, bf16[512,512]{1,0:T(8,128)(2,1)} %copy-done.36, ...), custom_call_target="tpu_custom_call" | custom-call | tf_op jit(solution)/shard_map/attn_term/pallas_call | solution.py:921
  211.5 2.6 copy.110
  231.2 24.9 %backward_conv.2 = (bf16[512,1024]{1,0:T(8,128)(2,1)}, bf16[512,1024]{1,0:T(8,128)(2,1)}, f32[2,1024]{1,0:T(2,128)}) custom-call(s32[2]{0:T(128)} %pad_add_fusion.info, f32[1]{0:T(128)} %bitcast.12.weight, bf16[512,1024]{1,0:T(8,128)(2,1)} %multiply_convert_fusion.3.grad, f32[512,1024]{1,0:T(8,128)} %get-tuple-element.27.x, f32[1,1024]{1,0:T(1,128)} %bitcast.177, ...), custom_call_target="tpu_custom_call" | custom-call | tf_op jit(solution)/shard_map/backward_conv/pallas_call | solution.py:827
  256.2 24.7 %backward_conv.3 = (bf16[512,1024]{1,0:T(8,128)(2,1)}, f32[2,1024]{1,0:T(2,128)}) custom-call(s32[2]{0:T(128)} %pad_add_fusion.info, f32[1]{0:T(128)} %bitcast.12.weight, bf16[512,1024]{1,0:T(8,128)(2,1)} %get-tuple-element.30.grad, bf16[512,1024]{1,0:T(8,128)(2,1)} %bitcast.149, f32[1,1024]{1,0:T(1,128)} %maximum_convert_fusion.scale, ...), custom_call_target="tpu_custom_call" | custom-call | tf_op jit(solution)/shard_map/backward_conv/pallas_call | solution.py:827
  284.4 2.9 collective-permute-start.19
  288.0 8.4 %collective-permute-done.9 = f32[2,5120]{1,0:T(2,128)S(1)} collective-permute-done((f32[2,5120]{1,0:T(2,128)S(1)}, f32[2,5120]{1,0:T(2,128)S(1)}, u32[]{:S(2)}, u32[]{:S(2)}) %collective-permute-start.9) | collective-permute-done | bytes 40992 | tf_op jit(solution)/shard_map/ppermute | solution.py:932
  299.7 2.6 collective-permute-start.31
  307.0 2.5 collective-permute-start.26
  309.5 2.9 collective-permute-done.31
  312.9 4.3 collective-permute-done.30
  319.4 4.3 collective-permute-done.39
  330.1 41.0 %collective-permute-done.38 = bf16[512,256]{1,0:T(8,128)(2,1)S(1)} collective-permute-done((bf16[512,256]{1,0:T(8,128)(2,1)S(1)}, bf16[512,256]{1,0:T(8,128)(2,1)S(1)}, u32[]{:S(2)}, u32[]{:S(2)}) %collective-permute-start.38) | collective-permute-done | bytes 262176 | tf_op jit(solution)/shard_map/ppermute | solution.py:932
  374.2 4.1 collective-permute-done.37
  378.4 2.3 collective-permute-start.12
  387.9 6.4 collective-permute-done.12
  398.5 2.8 concatenate.166
  401.3 3.7 fusion.23
  405.0 6.0 text_term.1.tx
  411.0 17.0 %conv_term.2.co = bf16[9,512,256]{2,1,0:T(8,128)(2,1)} custom-call(s32[8]{0:T(128)} %fusion.32.layouts, bf16[2,512,512]{2,1,0:T(8,128)(2,1)} %pad_maximum_fusion.3.a0, bf16[2,512,512]{2,1,0:T(8,128)(2,1)} %collective-permute-done.26.a1, bf16[2,512,512]{2,1,0:T(8,128)(2,1)} %collective-permute-done.27.a2, bf16[2,512,512]{2,1,0:T(8,128)(2,1)} %collective-permute-done.28.a3, ...), custom_call_target="tpu_custom_call" | custom-call | tf_op jit(solution)/shard_map/conv_term/pallas_call | solution.py:865
  432.5 17.0 %conv_term.3.ci = bf16[9,512,256]{2,1,0:T(8,128)(2,1)} custom-call(s32[8]{0:T(128)} %fusion.32.layouts, bf16[2,512,512]{2,1,0:T(8,128)(2,1)} %pad_maximum_fusion.5.a0, bf16[2,512,512]{2,1,0:T(8,128)(2,1)} %collective-permute-done.34.a1, bf16[2,512,512]{2,1,0:T(8,128)(2,1)} %collective-permute-done.35.a2, bf16[2,512,512]{2,1,0:T(8,128)(2,1)} %copy-done.26, ...), custom_call_target="tpu_custom_call" | custom-call | tf_op jit(solution)/shard_map/conv_term/pallas_call | solution.py:865
  449.5 282.8 %sum_and_gather.1 = (bf16[2048,2048]{1,0:T(8,128)(2,1)}, bf16[512,3072]{1,0:T(8,128)(2,1)}, bf16[512,1024]{1,0:T(8,128)(2,1)}, bf16[9,512,1024]{2,1,0:T(8,128)(2,1)}, bf16[9,512,1024]{2,1,0:T(8,128)(2,1)}) custom-call(bf16[8,512,256]{2,1,0:T(8,128)(2,1)} %text_term.1.tx, bf16[4,512,256]{2,1,0:T(8,128)(2,1)} %bitcast.154, bf16[9,512,256]{2,1,0:T(8,128)(2,1)} %conv_term.2.co, ...), custom_call_target="tpu_custom_call" | custom-call | tf_op jit(solution)/shard_map/sum_and_gather/pallas_call | solution.py:588
  732.3 13.0 %convert_element_type.174 = f32[9,512,1024]{2,1,0:T(8,128)} convert(bf16[9,512,1024]{2,1,0:T(8,128)(2,1)} %get-tuple-element.37) | non-fusion elementwise | flops 4718592 | bytes 28311552 | tf_op jit(solution)/shard_map/convert_element_type | solution.py:1106
  745.3 13.1 %convert_element_type.176 = f32[9,512,1024]{2,1,0:T(8,128)} convert(bf16[9,512,1024]{2,1,0:T(8,128)(2,1)} %get-tuple-element.38) | non-fusion elementwise | flops 4718592 | bytes 28311552 | tf_op jit(solution)/shard_map/convert_element_type | solution.py:1109
  758.4 3.5 convert_element_type.177
  763.5 11.7 %convert_element_type.179 = f32[2048,2048]{1,0:T(8,128)} convert(bf16[2048,2048]{1,0:T(8,128)(2,1)} %get-tuple-element.41) | non-fusion elementwise | flops 4194304 | bytes 25165824 | tf_op jit(solution)/shard_map/convert_element_type | solution.py:1113
  (328 shorter events, 110.5 us)
Async XLA Ops:
  7.2 37.6 %all-gather.11.cloned.1.call-start = ((), (), s32[]{:S(2)}) async-start(), calls=%async_computation.4 | async-start | bytes 3145728 | tf_op jit(solution)/shard_map/all_gather | solution.py:1023
  7.9 41.1 %all-gather.5.cloned.1.call-start = ((), (), s32[]{:S(2)}) async-start(), calls=%async_computation.1 | async-start | bytes 6291456 | tf_op jit(solution)/shard_map/all_gather | solution.py:1021
  8.7 92.5 %all-gather.7.cloned.1.call-start = ((), (), s32[]{:S(2)}) async-start(), calls=%async_computation.2 | async-start | bytes 9437184 | tf_op jit(solution)/shard_map/all_gather | solution.py:1022
  9.5 105.4 %all-gather.9.cloned.1.call-start = ((), (), s32[]{:S(2)}) async-start(), calls=%async_computation.3 | async-start | bytes 25165824 | tf_op jit(solution)/shard_map/all_gather | solution.py:1024
  10.0 439.4 %reduce-scatter.4.cloned.1.call-start = ((), (), s32[]{:S(2)}) async-start(), calls=%async_computation.5 | async-start | bytes 5242880
  10.1 42.4 %collective-permute-start.1 = (bf16[9,512,1024]{2,1,0:T(8,128)(2,1)}, bf16[9,512,1024]{2,1,0:T(8,128)(2,1)}, u32[]{:S(2)}, u32[]{:S(2)}) collective-permute-start(bf16[9,512,1024]{2,1,0:T(8,128)(2,1)} %w_own.7), channel_id=1, source_target_pairs={{0,1},{1,0},{2,3},{3,2},{4,5},{5,4},{6,7},{7,6},{8,9},{9,8},{10,11... | collective-permute-start | bytes 28311560 | tf_op jit(solution)/shard_map/ppermute | solution.py:936
  10.6 62.9 %collective-permute-start.2 = (bf16[9,512,1024]{2,1,0:T(8,128)(2,1)}, bf16[9,512,1024]{2,1,0:T(8,128)(2,1)}, u32[]{:S(2)}, u32[]{:S(2)}) collective-permute-start(bf16[9,512,1024]{2,1,0:T(8,128)(2,1)} %w_own.6), channel_id=1, source_target_pairs={{0,1},{1,0},{2,3},{3,2},{4,5},{5,4},{6,7},{7,6},{8,9},{9,8},{10,11... | collective-permute-start | bytes 28311560 | tf_op jit(solution)/shard_map/ppermute | solution.py:936
  11.5 16.4 %collective-permute-start = (bf16[2560]{0:T(1024)(128)(2,1)S(1)}, bf16[2560]{0:T(1024)(128)(2,1)S(1)}, u32[]{:S(2)}, u32[]{:S(2)}) collective-permute-start(bf16[2560]{0:T(1024)(128)(2,1)S(1)} %dynamic-update-slice.3), channel_id=1, source_target_pairs={{0,1},{1,0},{2,3},{3,2},{4,5},{5,4},{6,7},{7,6},{8,9},{9,8},{10,11... | collective-permute-start | bytes 15368 | tf_op jit(solution)/shard_map/ppermute | solution.py:936
  13.4 11.5 %collective-permute-start.3 = (f32[1,1152]{1,0:T(1,128)S(1)}, f32[1,1152]{1,0:T(1,128)S(1)}, u32[]{:S(2)}, u32[]{:S(2)}) collective-permute-start(f32[1,1152]{1,0:T(1,128)S(1)} %broadcast_in_dim.57), channel_id=1, source_target_pairs={{0,1},{1,0},{2,3},{3,2},{4,5},{5,4},{6,7},{7,6},{8,9},{9,8},{10,11... | collective-permute-start | bytes 13832 | tf_op jit(solution)/shard_map/ppermute | solution.py:936
  24.9 4.6 collective-permute-start.4
  29.5 3.9 collective-permute-start.5
  33.4 4.1 collective-permute-start.6
  37.5 5.8 collective-permute-start.7
  113.7 70.6 %collective-permute-start.21 = (bf16[512,512]{1,0:T(8,128)(2,1)}, bf16[512,512]{1,0:T(8,128)(2,1)}, u32[]{:S(2)}, u32[]{:S(2)}) collective-permute-start(bf16[512,512]{1,0:T(8,128)(2,1)} %get-tuple-element.68), channel_id=1, source_target_pairs={{0,1},{1,0},{2,3},{3,2},{4,5},{5,4},{6,7},{7,6},{8,9},{9,8},{10,11... | collective-permute-start | bytes 1572872 | tf_op jit(solution)/shard_map/ppermute | solution.py:936
  144.0 86.0 %copy-start.1 = (f32[640,8,128]{0,2,1:T(8,128)}, f32[640,8,128]{0,2,1:T(8,128)S(1)}, u32[]{:S(2)}) copy-start(f32[640,8,128]{0,2,1:T(8,128)S(1)} %multiply_bitcast_fusion) | copy-start | bytes 7864324
  173.8 108.0 %copy-start.55 = (f32[1024]{0:T(1024)}, f32[1024]{0:T(1024)S(1)}, u32[]{:S(2)}) copy-start(f32[1024]{0:T(1024)S(1)} %get-tuple-element.42) | copy-start | bytes 12292
  173.8 13.1 %collective-permute-start.23 = (bf16[512,3072]{1,0:T(8,128)(2,1)}, bf16[512,3072]{1,0:T(8,128)(2,1)}, u32[]{:S(2)}, u32[]{:S(2)}) collective-permute-start(bf16[512,3072]{1,0:T(8,128)(2,1)} %multiply_convert_fusion.1.t_own), channel_id=1, source_target_pairs={{0,1},{1,0},{2,3},{3,2},{4,5},{5,4},{6,7},{7,6},{8,9},{9,8},{10,11... | collective-permute-start | bytes 9437192 | tf_op jit(solution)/shard_map/ppermute | solution.py:936
  179.0 6.9 collective-permute-start.24
  183.9 2.0 collective-permute-start.22
  206.5 13.3 %collective-permute-start.13 = (bf16[2048,128]{1,0:T(8,128)(2,1)}, bf16[2048,128]{1,0:T(8,128)(2,1)}, u32[]{:S(2)}, u32[]{:S(2)}) collective-permute-start(bf16[2048,128]{1,0:T(8,128)(2,1)} %bitcast.158), channel_id=1, source_target_pairs={{0,1},{1,0},{2,3},{3,2},{4,5},{5,4},{6,7},{7,6},{8,9},{9,8},{10,11... | collective-permute-start | bytes 1572872 | tf_op jit(solution)/shard_map/ppermute | solution.py:936
  211.4 14.2 %collective-permute-start.25 = (bf16[512,512]{1,0:T(8,128)(2,1)}, bf16[512,512]{1,0:T(8,128)(2,1)}, u32[]{:S(2)}, u32[]{:S(2)}) collective-permute-start(bf16[512,512]{1,0:T(8,128)(2,1)} %get-tuple-element.64), channel_id=1, source_target_pairs={{0,1},{1,0},{2,3},{3,2},{4,5},{5,4},{6,7},{7,6},{8,9},{9,8},{10,11... | collective-permute-start | bytes 1572872 | tf_op jit(solution)/shard_map/ppermute | solution.py:936
  216.3 11.4 %collective-permute-start.33 = (bf16[512,512]{1,0:T(8,128)(2,1)}, bf16[512,512]{1,0:T(8,128)(2,1)}, u32[]{:S(2)}, u32[]{:S(2)}) collective-permute-start(bf16[512,512]{1,0:T(8,128)(2,1)} %get-tuple-element.58), channel_id=1, source_target_pairs={{0,1},{1,0},{2,3},{3,2},{4,5},{5,4},{6,7},{7,6},{8,9},{9,8},{10,11... | collective-permute-start | bytes 1572872 | tf_op jit(solution)/shard_map/ppermute | solution.py:936
  222.1 75.8 %collective-permute-start.14 = (bf16[2,2048,128]{2,1,0:T(8,128)(2,1)}, bf16[2,2048,128]{2,1,0:T(8,128)(2,1)}, u32[]{:S(2)}, u32[]{:S(2)}) collective-permute-start(bf16[2,2048,128]{2,1,0:T(8,128)(2,1)} %pad_maximum_fusion.2.a0), channel_id=1, source_target_pairs={{0,2},{2,0},{4,6},{6,4},{8,10},{10,8},{12,14},{14,12},{16,18},{18,... | collective-permute-start | bytes 3145736 | tf_op jit(solution)/shard_map/ppermute | solution.py:932
  223.8 75.6 %collective-permute-start.15 = (bf16[2,2048,128]{2,1,0:T(8,128)(2,1)}, bf16[2,2048,128]{2,1,0:T(8,128)(2,1)}, u32[]{:S(2)}, u32[]{:S(2)}) collective-permute-start(bf16[2,2048,128]{2,1,0:T(8,128)(2,1)} %pad_maximum_fusion.2.a0), channel_id=1, source_target_pairs={{0,4},{2,6},{4,0},{6,2},{8,12},{10,14},{12,8},{14,10},{16,20},{18,... | collective-permute-start | bytes 3145736 | tf_op jit(solution)/shard_map/ppermute | solution.py:932
  225.5 74.3 %collective-permute-start.16 = (bf16[2,2048,128]{2,1,0:T(8,128)(2,1)}, bf16[2,2048,128]{2,1,0:T(8,128)(2,1)}, u32[]{:S(2)}, u32[]{:S(2)}) collective-permute-start(bf16[2,2048,128]{2,1,0:T(8,128)(2,1)} %pad_maximum_fusion.2.a0), channel_id=1, source_target_pairs={{0,6},{2,4},{4,2},{6,0},{8,14},{10,12},{12,10},{14,8},{16,22},{18,... | collective-permute-start | bytes 3145736 | tf_op jit(solution)/shard_map/ppermute | solution.py:932
  281.8 5.5 collective-permute-start.8
  284.4 18.0 %collective-permute-start.19 = (bf16[128,512]{1,0:T(8,128)(2,1)S(1)}, bf16[128,512]{1,0:T(8,128)(2,1)S(1)}, u32[]{:S(2)}, u32[]{:S(2)}) collective-permute-start(bf16[128,512]{1,0:T(8,128)(2,1)S(1)} %bitcast.169), channel_id=1, source_target_pairs={{0,6},{2,4},{4,2},{6,0},{8,14},{10,12},{12,10},{14,8},{16,22},{18,... | collective-permute-start | bytes 393224 | tf_op jit(solution)/shard_map/ppermute | solution.py:932
  287.4 9.0 %collective-permute-start.9 = (f32[2,5120]{1,0:T(2,128)S(1)}, f32[2,5120]{1,0:T(2,128)S(1)}, u32[]{:S(2)}, u32[]{:S(2)}) collective-permute-start(f32[2,5120]{1,0:T(2,128)S(1)} %pad_maximum_fusion.10), channel_id=1, source_target_pairs={{0,2},{2,0},{4,6},{6,4},{8,10},{10,8},{12,14},{14,12},{16,18},{18,... | collective-permute-start | bytes 122888 | tf_op jit(solution)/shard_map/ppermute | solution.py:932
  296.4 6.5 collective-permute-start.18
  298.0 6.3 collective-permute-start.10
  299.4 7.5 collective-permute-start.17
  299.7 12.6 %collective-permute-start.31 = (bf16[512,256]{1,0:T(8,128)(2,1)S(1)}, bf16[512,256]{1,0:T(8,128)(2,1)S(1)}, u32[]{:S(2)}, u32[]{:S(2)}) collective-permute-start(bf16[512,256]{1,0:T(8,128)(2,1)S(1)} %get-tuple-element.60), channel_id=1, source_target_pairs={{0,6},{2,4},{4,2},{6,0},{8,14},{10,12},{12,10},{14,8},{16,22},{18,... | collective-permute-start | bytes 786440 | tf_op jit(solution)/shard_map/ppermute | solution.py:932
  302.4 14.9 %collective-permute-start.30 = (bf16[512,256]{1,0:T(8,128)(2,1)S(1)}, bf16[512,256]{1,0:T(8,128)(2,1)S(1)}, u32[]{:S(2)}, u32[]{:S(2)}) collective-permute-start(bf16[512,256]{1,0:T(8,128)(2,1)S(1)} %get-tuple-element.61), channel_id=1, source_target_pairs={{0,4},{2,6},{4,0},{6,2},{8,12},{10,14},{12,8},{14,10},{16,20},{18,... | collective-permute-start | bytes 786440 | tf_op jit(solution)/shard_map/ppermute | solution.py:932
  302.9 15.2 %collective-permute-start.29 = (bf16[512,256]{1,0:T(8,128)(2,1)S(1)}, bf16[512,256]{1,0:T(8,128)(2,1)S(1)}, u32[]{:S(2)}, u32[]{:S(2)}) collective-permute-start(bf16[512,256]{1,0:T(8,128)(2,1)S(1)} %get-tuple-element.62), channel_id=1, source_target_pairs={{0,2},{2,0},{4,6},{6,4},{8,10},{10,8},{12,14},{14,12},{16,18},{18,... | collective-permute-start | bytes 786440 | tf_op jit(solution)/shard_map/ppermute | solution.py:932
  304.2 19.4 %collective-permute-start.39 = (bf16[512,256]{1,0:T(8,128)(2,1)S(1)}, bf16[512,256]{1,0:T(8,128)(2,1)S(1)}, u32[]{:S(2)}, u32[]{:S(2)}) collective-permute-start(bf16[512,256]{1,0:T(8,128)(2,1)S(1)} %get-tuple-element.54), channel_id=1, source_target_pairs={{0,6},{2,4},{4,2},{6,0},{8,14},{10,12},{12,10},{14,8},{16,22},{18,... | collective-permute-start | bytes 786440 | tf_op jit(solution)/shard_map/ppermute | solution.py:932
  307.0 77.3 %collective-permute-start.26 = (bf16[2,512,512]{2,1,0:T(8,128)(2,1)S(1)}, bf16[2,512,512]{2,1,0:T(8,128)(2,1)}, u32[]{:S(2)}, u32[]{:S(2)}) collective-permute-start(bf16[2,512,512]{2,1,0:T(8,128)(2,1)S(1)} %copy-done.15), channel_id=1, source_target_pairs={{0,2},{2,0},{4,6},{6,4},{8,10},{10,8},{12,14},{14,12},{16,18},{18,... | collective-permute-start | bytes 3145736 | tf_op jit(solution)/shard_map/ppermute | solution.py:932
  312.4 72.6 %collective-permute-start.27 = (bf16[2,512,512]{2,1,0:T(8,128)(2,1)S(1)}, bf16[2,512,512]{2,1,0:T(8,128)(2,1)}, u32[]{:S(2)}, u32[]{:S(2)}) collective-permute-start(bf16[2,512,512]{2,1,0:T(8,128)(2,1)S(1)} %copy-done.15), channel_id=1, source_target_pairs={{0,4},{2,6},{4,0},{6,2},{8,12},{10,14},{12,8},{14,10},{16,20},{18,... | collective-permute-start | bytes 3145736 | tf_op jit(solution)/shard_map/ppermute | solution.py:932
  317.3 69.2 %collective-permute-start.28 = (bf16[2,512,512]{2,1,0:T(8,128)(2,1)S(1)}, bf16[2,512,512]{2,1,0:T(8,128)(2,1)}, u32[]{:S(2)}, u32[]{:S(2)}) collective-permute-start(bf16[2,512,512]{2,1,0:T(8,128)(2,1)S(1)} %copy-done.15), channel_id=1, source_target_pairs={{0,6},{2,4},{4,2},{6,0},{8,14},{10,12},{12,10},{14,8},{16,22},{18,... | collective-permute-start | bytes 3145736 | tf_op jit(solution)/shard_map/ppermute | solution.py:932
  318.2 52.9 %collective-permute-start.38 = (bf16[512,256]{1,0:T(8,128)(2,1)S(1)}, bf16[512,256]{1,0:T(8,128)(2,1)S(1)}, u32[]{:S(2)}, u32[]{:S(2)}) collective-permute-start(bf16[512,256]{1,0:T(8,128)(2,1)S(1)} %get-tuple-element.55), channel_id=1, source_target_pairs={{0,4},{2,6},{4,0},{6,2},{8,12},{10,14},{12,8},{14,10},{16,20},{18,... | collective-permute-start | bytes 786440 | tf_op jit(solution)/shard_map/ppermute | solution.py:932
  324.4 48.3 %collective-permute-start.11 = (f32[8,5120]{1,0:T(8,128)}, f32[8,5120]{1,0:T(8,128)S(1)}, u32[]{:S(2)}, u32[]{:S(2)}) collective-permute-start(f32[8,5120]{1,0:T(8,128)} %pad_maximum_fusion.8), channel_id=1, source_target_pairs={{0,8},{2,10},{4,12},{6,14},{8,0},{10,2},{12,4},{14,6},{16,24},{18,... | collective-permute-start | bytes 491528 | tf_op jit(solution)/shard_map/ppermute | solution.py:932
  371.1 7.3 collective-permute-start.37
  372.7 21.6 %collective-permute-start.20 = (bf16[4,128,512]{2,1,0:T(8,128)(2,1)}, bf16[4,128,512]{2,1,0:T(8,128)(2,1)}, u32[]{:S(2)}, u32[]{:S(2)}) collective-permute-start(bf16[4,128,512]{2,1,0:T(8,128)(2,1)} %pad_maximum_fusion.7.b_own), channel_id=1, source_target_pairs={{0,1},{1,0},{2,3},{3,2},{4,5},{5,4},{6,7},{7,6},{8,9},{9,8},{10,11... | collective-permute-start | bytes 1572872 | tf_op jit(solution)/shard_map/ppermute | solution.py:936
  378.4 15.9 %collective-permute-start.12 = (f32[16,5120]{1,0:T(8,128)}, f32[16,5120]{1,0:T(8,128)S(1)}, u32[]{:S(2)}, u32[]{:S(2)}) collective-permute-start(f32[16,5120]{1,0:T(8,128)} %concatenate.162), channel_id=1, source_target_pairs={{0,16},{2,18},{4,20},{6,22},{8,24},{10,26},{12,28},{14,30},{16,0},... | collective-permute-start | bytes 983048 | tf_op jit(solution)/shard_map/ppermute | solution.py:932
  384.3 43.7 %collective-permute-start.34 = (bf16[2,512,512]{2,1,0:T(8,128)(2,1)S(1)}, bf16[2,512,512]{2,1,0:T(8,128)(2,1)}, u32[]{:S(2)}, u32[]{:S(2)}) collective-permute-start(bf16[2,512,512]{2,1,0:T(8,128)(2,1)S(1)} %copy-done.14), channel_id=1, source_target_pairs={{0,2},{2,0},{4,6},{6,4},{8,10},{10,8},{12,14},{14,12},{16,18},{18,... | collective-permute-start | bytes 3145736 | tf_op jit(solution)/shard_map/ppermute | solution.py:932
  385.0 44.7 %collective-permute-start.35 = (bf16[2,512,512]{2,1,0:T(8,128)(2,1)S(1)}, bf16[2,512,512]{2,1,0:T(8,128)(2,1)}, u32[]{:S(2)}, u32[]{:S(2)}) collective-permute-start(bf16[2,512,512]{2,1,0:T(8,128)(2,1)S(1)} %copy-done.14), channel_id=1, source_target_pairs={{0,4},{2,6},{4,0},{6,2},{8,12},{10,14},{12,8},{14,10},{16,20},{18,... | collective-permute-start | bytes 3145736 | tf_op jit(solution)/shard_map/ppermute | solution.py:932
  386.5 45.0 %collective-permute-start.36 = (bf16[2,512,512]{2,1,0:T(8,128)(2,1)S(1)}, bf16[2,512,512]{2,1,0:T(8,128)(2,1)S(1)}, u32[]{:S(2)}, u32[]{:S(2)}) collective-permute-start(bf16[2,512,512]{2,1,0:T(8,128)(2,1)S(1)} %copy-done.14), channel_id=1, source_target_pairs={{0,6},{2,4},{4,2},{6,0},{8,14},{10,12},{12,10},{14,8},{16,22},{18,... | collective-permute-start | bytes 3145736 | tf_op jit(solution)/shard_map/ppermute | solution.py:932
  394.3 16.7 %collective-permute-start.32 = (bf16[4,512,256]{2,1,0:T(8,128)(2,1)}, bf16[4,512,256]{2,1,0:T(8,128)(2,1)}, u32[]{:S(2)}, u32[]{:S(2)}) collective-permute-start(bf16[4,512,256]{2,1,0:T(8,128)(2,1)} %pad_maximum_fusion.4.b_own), channel_id=1, source_target_pairs={{0,1},{1,0},{2,3},{3,2},{4,5},{5,4},{6,7},{7,6},{8,9},{9,8},{10,11... | collective-permute-start | bytes 3145736 | tf_op jit(solution)/shard_map/ppermute | solution.py:936
  394.3 37.2 %collective-permute-start.40 = (bf16[4,512,256]{2,1,0:T(8,128)(2,1)S(1)}, bf16[4,512,256]{2,1,0:T(8,128)(2,1)}, u32[]{:S(2)}, u32[]{:S(2)}) collective-permute-start(bf16[4,512,256]{2,1,0:T(8,128)(2,1)S(1)} %pad_maximum_fusion.6.b_own), channel_id=1, source_target_pairs={{0,1},{1,0},{2,3},{3,2},{4,5},{5,4},{6,7},{7,6},{8,9},{9,8},{10,11... | collective-permute-start | bytes 3145736 | tf_op jit(solution)/shard_map/ppermute | solution.py:936
  (68 other events, 839.5 us)
Sparse Core Ops, SparseCore 0:
  9.6 18.5 all-gather.10
  29.7 16.2 all-gather.4
  47.5 17.9 all-gather.6
  66.8 31.2 all-gather.8
  202.5 76.5 reduce-scatter.3

commit v2 on v0

--- a/solution.py
+++ b/solution.py
@@ -1,6 +1,10 @@
+import functools
+
 import jax
 import jax.numpy as jnp
 from jax import lax
+from jax.experimental import pallas as pl
+from jax.experimental.pallas import tpu as pltpu
 from jax.sharding import PartitionSpec as P
 
 NORM_GROUPS = 32
@@ -245,7 +249,7 @@
     )
 
 
-def body(
+def plain_body(
     pixels,
     layout,
     noise_group,
@@ -434,7 +438,1045 @@
     )
 
 
+CHUNK = 256
+HALF_ROWS = 10 * MAP_W
+
+
+def quadrants(values):
+    grid = values.reshape(2, MAP_H // 2, 2, MAP_W // 2, values.shape[-1])
+    return [grid[a, :, b] for a in range(2) for b in range(2)]
+
+
+def rejoin(parts):
+    channels = parts[0].shape[-1]
+    top = jnp.concatenate(
+        [part.reshape(MAP_H // 2, 1, MAP_W // 2, channels) for part in parts[:2]], axis=1
+    )
+    low = jnp.concatenate(
+        [part.reshape(MAP_H // 2, 1, MAP_W // 2, channels) for part in parts[2:]], axis=1
+    )
+    return jnp.concatenate([top, low], axis=0).reshape(MAP_H * MAP_W, channels)
+
+
+def region_mean(parts, single, block_ones):
+    rows = jnp.concatenate(
+        [jnp.sum(part, axis=(0, 1), keepdims=True).reshape(1, -1) for part in parts], axis=0
+    )
+    rows = jnp.concatenate([rows, rows], axis=0)
+    sums = jnp.dot(rows, block_ones, precision=highest, preferred_element_type=jnp.float32)
+    quarter_count = (MAP_H * MAP_W // 4) * 32.0
+    whole = jnp.sum(sums[:4], axis=0, keepdims=True) * (0.25 / quarter_count)
+    return [jnp.where(single, whole, sums[i : i + 1] * (1.0 / quarter_count)) for i in range(4)]
+
+
+def normalise(parts, single, block_ones):
+    means = region_mean(parts, single, block_ones)
+    centred = [part - mean[None] for part, mean in zip(parts, means)]
+    spread = region_mean([part * part for part in centred], single, block_ones)
+    rates = [lax.rsqrt(value + epsilon) for value in spread]
+    return [part * rate[None] for part, rate in zip(centred, rates)], rates
+
+
+def group_ones():
+    row = lax.broadcasted_iota(jnp.int32, (CHUNK, CHUNK), 0) // 32
+    col = lax.broadcasted_iota(jnp.int32, (CHUNK, CHUNK), 1) // 32
+    return (row == col).astype(jnp.float32)
+
+
+def put_shifts(values, single, taps, lanes):
+    pixel = lax.broadcasted_iota(jnp.int32, values.shape, 0) % MAP_W
+    for s in range(3):
+        if s == 1:
+            moved = values
+        elif s == 2:
+            moved = pltpu.roll(values, MAP_H * MAP_W - 1, 0)
+            moved = jnp.where(
+                (pixel != MAP_W - 1) & (single | (pixel != MAP_W // 2 - 1)), moved, 0.0
+            )
+        else:
+            moved = pltpu.roll(values, 1, 0)
+            moved = jnp.where((pixel != 0) & (single | (pixel != MAP_W // 2)), moved, 0.0)
+        low = moved.astype(jnp.bfloat16)
+        blank = jnp.zeros((MAP_W, values.shape[1]), jnp.bfloat16)
+        taps[s, 0, 0:32, lanes] = blank
+        taps[s, 0, 32:288, lanes] = low[0:256]
+        taps[s, 0, 288:320, lanes] = jnp.where(single, moved[256:288], 0.0).astype(jnp.bfloat16)
+        taps[s, 1, 0:32, lanes] = jnp.where(single, moved[224:256], 0.0).astype(jnp.bfloat16)
+        taps[s, 1, 32:288, lanes] = low[256:512]
+        taps[s, 1, 288:320, lanes] = blank
+
+
+def tap_rows(taps, col_step, row_step, lanes):
+    rows = taps[col_step, :, pl.ds(pl.multiple_of(row_step * MAP_W, MAP_W), 256), lanes]
+    return rows.reshape(MAP_H * MAP_W, rows.shape[-1])
+
+
+def own_first(start, core, width):
+    return pl.ds(pl.multiple_of((start + core * 512) % 1024, width), width)
+
+
+def forward_conv_kernel(finish, info, x, scale, shift, w_own, w_far, *refs):
+    if finish:
+        pixels, ln_gain, low_out, joined_out, normed_out, taps, acc = refs
+    else:
+        low_out, acc, taps = refs
+    t = pl.program_id(0)
+    core = info[0]
+    single = info[1] == 1
+
+    @pl.when(t == 0)
+    def _():
+        ones = group_ones()
+        for start in range(0, 1024, CHUNK):
+            lanes = pl.ds(start, CHUNK)
+            parts = quadrants(x[:, lanes].astype(jnp.float32))
+            normed, _ = normalise(parts, single, ones)
+            pre = rejoin(normed) * scale[:, lanes] + shift[:, lanes]
+            act = pre * jax.nn.sigmoid(pre)
+            low_out[:, lanes] = act.astype(jnp.bfloat16)
+            put_shifts(act, single, taps, own_first(start, core, CHUNK))
+
+    rows = tap_rows(taps, t % 3, t // 3, slice(None))
+    fresh = jnp.dot(rows[:, :512], w_own[0], preferred_element_type=jnp.float32)
+    fresh += jnp.dot(rows[:, 512:], w_far[0], preferred_element_type=jnp.float32)
+
+    @pl.when(t == 0)
+    def _():
+        acc[...] = fresh
+
+    @pl.when(t > 0)
+    def _():
+        acc[...] += fresh
+
+    if finish:
+
+        @pl.when(t == 8)
+        def _():
+            joined = (pixels[...].astype(jnp.float32) + acc[...]) * inv_root_two
+            joined_out[...] = joined
+            centre = joined - jnp.mean(joined, axis=1, keepdims=True)
+            rate = lax.rsqrt(jnp.mean(centre * centre, axis=1, keepdims=True) + epsilon)
+            normed_out[...] = (centre * rate * ln_gain[...]).astype(jnp.bfloat16)
+
+
+def whole(shape):
+    return pl.BlockSpec(shape, lambda t, *_: (0,) * len(shape))
+
+
+def forward_conv(info, x, scale, shift, w_own, w_far, extra=None):
+    finish = extra is not None
+    full = jax.ShapeDtypeStruct((512, 1024), jnp.float32)
+    low = jax.ShapeDtypeStruct((512, 1024), jnp.bfloat16)
+    field = whole((512, 1024))
+    row = whole((1, 1024))
+    tap = pl.BlockSpec((1, 512, 1024), lambda t, *_: (t, 0, 0))
+    scratch = [pltpu.VMEM((3, 2, HALF_ROWS, 1024), jnp.bfloat16)]
+    if finish:
+        scratch += [pltpu.VMEM((512, 1024), jnp.float32)]
+    return pl.pallas_call(
+        functools.partial(forward_conv_kernel, finish),
+        out_shape=(low, full, low) if finish else (low, full),
+        grid_spec=pltpu.PrefetchScalarGridSpec(
+            num_scalar_prefetch=1,
+            grid=(9,),
+            in_specs=[field, row, row, tap, tap] + ([field, row] if finish else []),
+            out_specs=(field, field, field) if finish else (field, field),
+            scratch_shapes=scratch,
+        ),
+        compiler_params=pltpu.CompilerParams(vmem_limit_bytes=56 << 20),
+        name="forward_conv",
+    )(info, x, scale, shift, w_own, w_far, *(extra or ()))
+
+
+def to_wide(value, step):
+    return lax.ppermute(value, "wide", [(i, i ^ step) for i in range(16)])
+
+
+def to_far(value):
+    return lax.ppermute(value, "narrow", [(0, 1), (1, 0)])
+
+
+def gather_all(row):
+    rows = row[None]
+    rows = jnp.concatenate([rows, to_far(rows)])
+    for step in (1, 2, 4, 8):
+        rows = jnp.concatenate([rows, to_wide(rows, step)])
+    return rows
+
+
+def half_of(value, core, axis):
+    size = value.shape[axis] // 2
+    return lax.dynamic_slice_in_dim(value, core * size, size, axis)
+
+
+def share_source(value_t, core):
+    far = to_far(half_of(value_t, 1 - core, 0))
+    pair = jnp.stack([half_of(value_t, core, 0), far])
+    return (pair, to_wide(pair, 1), to_wide(pair, 2), to_wide(pair, 3))
+
+
+def pair_of(value_t, core):
+    far = to_far(half_of(value_t, 1 - core, 0))
+    return jnp.concatenate([half_of(value_t, core, 0), far], axis=1)
+
+
+def pair_body(
+    pixels,
+    layout,
+    noise_group,
+    cond_embed,
+    text_embed,
+    cotangent,
+    gn_gain,
+    gn_bias,
+    conv_in,
+    film_weight,
+    film_bias,
+    conv_out,
+    ln_gain,
+    qkv_weight,
+    out_weight,
+    text_weight,
+):
+    f32, bf16 = jnp.float32, jnp.bfloat16
+    wide = lax.axis_index("wide")
+    core = lax.axis_index("narrow")
+    group_total = lax.axis_size("wide")
+
+    conv_in_far = to_far(conv_in)
+    vectors = jnp.concatenate([gn_gain, gn_bias, ln_gain, film_bias])
+    vectors_far = to_far(vectors)
+    low_vec = jnp.where(core == 0, vectors, vectors_far)
+    high_vec = jnp.where(core == 0, vectors_far, vectors)
+
+    def joined_vec(start, size):
+        return jnp.concatenate([low_vec[start : start + size], high_vec[start : start + size]])
+
+    gain_row = joined_vec(0, 512).astype(f32)[None]
+    bias_row = joined_vec(512, 512).astype(f32)[None]
+    ln_row = joined_vec(1024, 512).astype(f32)[None]
+    film_bias_full = joined_vec(1536, 1024).astype(f32)
+    conv_out_far = to_far(conv_out)
+
+    facts = jnp.stack([noise_group[0], layout[0]])
+    facts = jnp.pad(facts.astype(f32), (0, 126))
+    early = gather_all(jnp.concatenate([cond_embed[0].astype(f32), facts]))
+    cond_all = early[:, :1024]
+    alike = jnp.sum((early[:, 1024] == facts[0]).astype(f32))
+    weight = 1.0 / (group_total * alike)
+    info = jnp.stack([core.astype(jnp.int32), layout[0]])
+    layouts = early[:8, 1025].astype(jnp.int32)
+
+    text_one = text_embed[0]
+    text_sources = share_source(text_one.T, core)
+    cot = cotangent[0]
+    film_full = lax.all_gather(film_weight, "narrow", axis=0, tiled=True)
+    qkv_full = lax.all_gather(qkv_weight, "narrow", axis=0, tiled=True)
+    out_full = lax.all_gather(out_weight, "narrow", axis=0, tiled=True)
+    text_full = lax.all_gather(text_weight, "narrow", axis=0, tiled=True)
+
+    region_ids = region_ids_of(layout[0])
+    field = pixels[0]
+    condition = jax.nn.silu(cond_embed[0].astype(f32)).astype(bf16)
+    film_out = jnp.dot(condition, film_full, preferred_element_type=f32) + film_bias_full
+    film_scale = 1.0 + film_out[None, :1024]
+    film_shift = film_out[None, 1024:]
+
+    first_low, hidden_one = forward_conv(info, field, gain_row, bias_row, conv_in, conv_in_far)
+    first_sources = share_source(first_low.T, core)
+    second_low, joined, normed = forward_conv(
+        info, hidden_one, film_scale, film_shift, conv_out, conv_out_far, (field, ln_row)
+    )
+    second_sources = share_source(second_low.T, core)
+
+    attn_full = (ln_row[0], qkv_full, out_full, text_full)
+    result, stored = attention_mid(normed, joined, text_one, region_ids, attn_full)
+    output = result.astype(bf16)
+    grad_joined, ln_term, grad_triple, grad_pair = attention_back(
+        cot, joined, stored, attn_full
+    )
+    mixed = stored[5]
+    grad_two = grad_joined * inv_root_two
+    grad_two_low = grad_two.astype(bf16)
+
+    pair_w = (weight * grad_pair).astype(bf16)
+    pair_q = pair_w.reshape(TEXT_LEN, 2, 4, CHUNK).transpose(2, 0, 1, 3).reshape(4, TEXT_LEN, 512)
+    two_w = (weight * grad_two).astype(bf16)
+    two_q = two_w.reshape(512, 4, CHUNK).transpose(1, 0, 2)
+    both_w = (weight * jnp.concatenate([grad_triple, cot.astype(f32)], axis=1)).astype(bf16)
+    rows = jnp.concatenate(
+        [film_scale, film_shift, gain_row, bias_row, ln_term[None], jnp.zeros((3, 1024), f32)]
+    )
+
+    big, _, input_grad, small_all = late(
+        layouts,
+        weight.reshape(1),
+        pair_q,
+        two_q,
+        both_w,
+        *text_sources,
+        *second_sources,
+        *first_sources,
+        pair_of(normed.T, core),
+        pair_of(mixed.T, core),
+        grad_two_low,
+        hidden_one,
+        field,
+        grad_joined,
+        rows,
+        conv_out,
+        conv_out_far,
+        conv_in,
+        conv_in_far,
+    )
+    me = 2 * wide + core
+    film_all = small_all[:, :2].reshape(32, 2048)
+    cond_low = jax.nn.silu(cond_all).astype(bf16)[jnp.bitwise_xor(jnp.arange(32), me)]
+    grad_film_weight = lax.dot_general(
+        half_of(cond_low, core, 1),
+        film_all.astype(bf16),
+        (((0,), (0,)), ((), ())),
+        preferred_element_type=f32,
+    )
+    small_sum = jnp.sum(small_all, axis=0)
+    grad_film_bias = half_of(small_sum[:2].reshape(-1), core, 0)
+    grad_gn_gain = half_of(small_sum[2], core, 0)
+    grad_gn_bias = half_of(small_sum[3], core, 0)
+    grad_ln_gain = half_of(small_sum[4], core, 0)
+    tap = (1, 512, 1024)
+    conv_shape = (9, 512, 1024)
+    return (
+        output[None],
+        input_grad[None],
+        grad_gn_gain,
+        grad_gn_bias,
+        widen(big, FIRST_IN, conv_shape, tap, 9, lambda k: (k, 0, 0)),
+        grad_film_weight,
+        grad_film_bias,
+        widen(big, FIRST_OUT, conv_shape, tap, 9, lambda k: (k, 0, 0)),
+        grad_ln_gain,
+        widen(big, FIRST_ATTN, (512, 3072), tap[1:], 3, lambda k: (0, k)),
+        widen(big, FIRST_ATTN + 3, (512, 1024), tap[1:], 1, lambda k: (0, 0)),
+        widen(big, 0, (2048, 2048), tap[1:], 8, lambda k: (k // 2, k % 2)),
+    )
+
+
+def attention_mid(normed_low, joined, text_one, region_ids, attn_full):
+    _, qkv_full, out_full, text_full = attn_full
+    pixel_count, channels = joined.shape
+    head_dim = channels // HEADS
+    score_scale = head_dim ** (-0.5)
+    triple = jnp.dot(normed_low, qkv_full, preferred_element_type=jnp.float32).astype(jnp.bfloat16)
+    text_pair = jnp.dot(text_one, text_full, preferred_element_type=jnp.float32).astype(
+        jnp.bfloat16
+    )
+    queries = triple[:, :channels].reshape(pixel_count, HEADS, head_dim)
+    key_rows = jnp.concatenate(
+        [triple[:, channels : 2 * channels], text_pair[:, :channels]], axis=0
+    ).reshape(-1, HEADS, head_dim)
+    value_rows = jnp.concatenate(
+        [triple[:, 2 * channels :], text_pair[:, channels:]], axis=0
+    ).reshape(-1, HEADS, head_dim)
+    allowed = allowed_keys(region_ids)
+    masked = jnp.where(
+        allowed[None],
+        jnp.einsum("phd,jhd->hpj", queries, key_rows, preferred_element_type=jnp.float32)
+        * score_scale,
+        masked_score,
+    )
+    row_peak = jnp.max(masked, axis=2, keepdims=True)
+    exponent = jnp.exp(masked - row_peak)
+    exp_total = jnp.sum(exponent, axis=2, keepdims=True)
+    attn_probs = exponent / exp_total
+    log_total = row_peak + jnp.log(exp_total)
+    mixed = (
+        jnp.einsum(
+            "hpj,jhd->phd",
+            attn_probs.astype(jnp.bfloat16),
+            value_rows,
+            preferred_element_type=jnp.float32,
+        )
+        .reshape(pixel_count, channels)
+        .astype(jnp.bfloat16)
+    )
+    result = joined + jnp.dot(mixed, out_full, preferred_element_type=jnp.float32)
+    return (result, (normed_low, queries, key_rows, value_rows, log_total, mixed, allowed))
+
+
+def attention_back(grad_result, joined, stored, attn_full):
+    gain_row, qkv_full, out_full, text_full = attn_full
+    normed_low, queries, key_rows, value_rows, log_total, mixed, allowed = stored
+    pixel_count, channels = joined.shape
+    head_dim = channels // HEADS
+    score_scale = head_dim ** (-0.5)
+    grad_mixed = (
+        jnp.einsum("pd,cd->pc", grad_result, out_full, preferred_element_type=jnp.float32)
+        .astype(jnp.bfloat16)
+        .reshape(pixel_count, HEADS, head_dim)
+    )
+    masked = jnp.where(
+        allowed[None],
+        jnp.einsum("phd,jhd->hpj", queries, key_rows, preferred_element_type=jnp.float32)
+        * score_scale,
+        masked_score,
+    )
+    attn_probs = jnp.exp(masked - log_total)
+    grad_probs = jnp.einsum(
+        "phd,jhd->hpj", grad_mixed, value_rows, preferred_element_type=jnp.float32
+    )
+    grad_values = jnp.einsum(
+        "hpj,phd->jhd",
+        attn_probs.astype(jnp.bfloat16),
+        grad_mixed,
+        preferred_element_type=jnp.float32,
+    )
+    row_inner = jnp.sum(attn_probs * grad_probs, axis=2, keepdims=True)
+    grad_scores = (attn_probs * (grad_probs - row_inner)).astype(jnp.bfloat16)
+    grad_queries = (
+        jnp.einsum("hpj,jhd->phd", grad_scores, key_rows, preferred_element_type=jnp.float32)
+        * score_scale
+    )
+    grad_keys = (
+        jnp.einsum("hpj,phd->jhd", grad_scores, queries, preferred_element_type=jnp.float32)
+        * score_scale
+    )
+    grad_triple = jnp.concatenate(
+        [
+            grad_queries.reshape(pixel_count, channels),
+            grad_keys[:pixel_count].reshape(pixel_count, channels),
+            grad_values[:pixel_count].reshape(pixel_count, channels),
+        ],
+        axis=1,
+    )
+    grad_pair = jnp.concatenate(
+        [
+            grad_keys[pixel_count:].reshape(-1, channels),
+            grad_values[pixel_count:].reshape(-1, channels),
+        ],
+        axis=1,
+    )
+    grad_normed = jnp.einsum(
+        "pk,ck->pc", grad_triple.astype(jnp.bfloat16), qkv_full, preferred_element_type=jnp.float32
+    )
+    _, norm_back = jax.vjp(layer_norm, joined, gain_row)
+    grad_joined_norm, term_gain = norm_back(grad_normed)
+    return (grad_result.astype(jnp.float32) + grad_joined_norm, term_gain, grad_triple, grad_pair)
+
+
+MESH = pl.DeviceIdType.MESH
+CHUNKS = 30
+FIRST_OUT, FIRST_ATTN, FIRST_IN = 8, 17, 21
+
+
+def late_kernel(
+    layouts, weight,
+    pair_q, two_q, both_w, text0, text1, text2, text3, second0, second1, second2, second3,
+    first0, first1, first2, first3, normed_t, mixed_t, two_low_in, hidden_in, field_in,
+    passed_in, rows_in, out_own, out_far, in_own, in_far,
+    big, both_far, input_grad, small_out,
+    held, total, cross, taps, sources, pair_slots, two_slots, hid_slots, rhs, rs_in,
+    weights, acc, wide_field, field, two_low, hidden_low, hidden_q, rows, small,
+    s1s, s1r, s2s, s2r, s3s, s3r, xs, xr, ys, yr, d0s, d0r, d1s, d1r, own_sem,
+    pair_s, pair_r, two_s, two_r, hid_s, hid_r, both_s, both_r, rs_s, rs_r, small_s, small_r,
+    text_sem, source_sem, rhs_sem, load_sem, weight_sem, keep_sem,
+):
+    f32, bf16 = jnp.float32, jnp.bfloat16
+    w = lax.axis_index("wide")
+    c = lax.axis_index("narrow")
+    p = w % 4
+    z = w // 4
+    wx = w + 1 - 2 * (w % 2)
+    wy = w + 2 - 4 * ((w // 2) % 2)
+    wd = 4 * z + 3 - p
+    wz = w + 4 - 8 * (z % 2)
+    wm = (3 - z) * 4 + p
+    px = p + 1 - 2 * (p % 2)
+    py = p + 2 - 4 * (p // 2)
+    pd = 3 - p
+    steps = ((wx, px), (wy, py), (wd, pd))
+    is_mid = (z == 1) | (z == 2)
+    is_end = (z == 0) | (z == 3)
+    single = layouts[0] == 1
+
+    bar = pltpu.get_barrier_semaphore()
+    for t in (wx, wy, wd, wz):
+        pl.semaphore_signal(bar, inc=1, device_id=(t, c), device_id_type=MESH)
+    pl.semaphore_signal(bar, inc=1, device_id=(w, 1 - c), device_id_type=MESH)
+
+    @pl.when(is_mid)
+    def _():
+        pl.semaphore_signal(bar, inc=1, device_id=(wm, c), device_id_type=MESH)
+        pl.semaphore_wait(bar, 6)
+
+    @pl.when(is_end)
+    def _():
+        pl.semaphore_wait(bar, 5)
+
+    def remote(src, dst, ss, rs, t):
+        return pltpu.make_async_remote_copy(
+            src_ref=src, dst_ref=dst, send_sem=ss, recv_sem=rs, device_id=(t, c), device_id_type=MESH
+        )
+
+    def across(src, dst, ss, rs):
+        return pltpu.make_async_remote_copy(
+            src_ref=src, dst_ref=dst, send_sem=ss, recv_sem=rs, device_id=(w, 1 - c),
+            device_id_type=MESH,
+        )
+
+    def local(src, dst, sem):
+        return pltpu.make_async_copy(src, dst, sem)
+
+    def quarter_copies(quarters, slots, ss, rs):
+        sends = [
+            remote(quarters.at[q], slots.at[2 * (i + 1)], ss.at[i], rs.at[i], t)
+            for i, (t, q) in enumerate(steps)
+        ]
+        sends.append(across(quarters.at[p], slots.at[1], ss.at[3], rs.at[3]))
+        passes = [
+            across(slots.at[2 * i + 2], slots.at[2 * i + 3], ss.at[4 + i], rs.at[4 + i])
+            for i in range(3)
+        ]
+        return sends, passes
+
+    def start_quarters(quarters, slots, ss, rs, sem):
+        sends, _ = quarter_copies(quarters, slots, ss, rs)
+        for copy in (sends[2], sends[0], sends[1], sends[3]):
+            copy.start()
+        local(quarters.at[p], slots.at[0], sem).start()
+
+    def pass_quarters(quarters, slots, ss, rs):
+        sends, passes = quarter_copies(quarters, slots, ss, rs)
+        for i in range(3):
+            sends[i].wait_recv()
+            passes[i].start()
+
+    def finish_quarters(quarters, slots, ss, rs, sem):
+        sends, passes = quarter_copies(quarters, slots, ss, rs)
+        for copy in sends:
+            copy.wait_send()
+        sends[3].wait_recv()
+        for copy in passes:
+            copy.wait()
+        local(quarters.at[p], slots.at[0], sem).wait()
+
+    def column(q):
+        return pl.ds(pl.multiple_of(q * CHUNK, CHUNK), CHUNK)
+
+    def up(k):
+        return remote(held.at[k], total.at[k], s1s.at[k], s1r.at[k], wz)
+
+    def over(k):
+        return remote(held.at[k], cross.at[k], s2s.at[k], s2r.at[k], wm)
+
+    def down(k):
+        return remote(total.at[k], total.at[k], s3s.at[k], s3r.at[k], wz)
+
+    def to_x(k, q):
+        return remote(total.at[k], big.at[k, :, column(q)], xs.at[k], xr.at[k], wx)
+
+    def to_y(k, q):
+        return remote(total.at[k], big.at[k, :, column(q)], ys.at[k], yr.at[k], wy)
+
+    def on_x(k, q):
+        part = big.at[k, pl.ds(0, 256), column(q)]
+        return remote(part, part, d0s.at[k], d0r.at[k], wx)
+
+    def on_y(k, q):
+        part = big.at[k, pl.ds(256, 256), column(q)]
+        return remote(part, part, d1s.at[k], d1r.at[k], wy)
+
+    def own(k):
+        return local(total.at[k], big.at[k, :, column(p)], own_sem.at[k])
+
+    def offer(k):
+        @pl.when(is_end)
+        def _():
+            up(k).start()
+
+    def tick(k):
+        @pl.when(is_mid & (k < CHUNKS))
+        def _():
+            up(k).wait_recv()
+            held[k] = (held[k].astype(f32) + total[k].astype(f32)).astype(bf16)
+            over(k).start()
+
+        kb = k - 1
+
+        @pl.when((kb >= 0) & (kb < CHUNKS))
+        def _():
+            @pl.when(is_mid)
+            def _():
+                over(kb).wait_recv()
+                total[kb] = (held[kb].astype(f32) + cross[kb].astype(f32)).astype(bf16)
+                down(kb).start()
+
+            @pl.when(is_end)
+            def _():
+                down(kb).wait_recv()
+
+            to_x(kb, p).start()
+            to_y(kb, p).start()
+            own(kb).start()
+
+        kc = k - 2
+
+        @pl.when((kc >= 0) & (kc < CHUNKS))
+        def _():
+            to_x(kc, px).wait_recv()
+            to_y(kc, py).wait_recv()
+            on_x(kc, py).start()
+            on_y(kc, px).start()
+
+        kd = k - 3
+
+        @pl.when((kd >= 0) & (kd < CHUNKS))
+        def _():
+            on_x(kd, pd).wait_recv()
+            on_y(kd, pd).wait_recv()
+
+    start_quarters(pair_q, pair_slots, pair_s, pair_r, keep_sem.at[0])
+    across(both_w, both_far, both_s, both_r).start()
+    start_quarters(two_q, two_slots, two_s, two_r, keep_sem.at[1])
+
+    text = (text0, text1, text2, text3)
+
+    def text_loads(i):
+        slot = 2 * (i % 2)
+        rows_i = pl.ds(pl.multiple_of(i * 512, 512), 512)
+        return [
+            local(
+                text[j].at[e, rows_i],
+                sources.at[slot + j // 2, :, pl.ds(TEXT_LEN * (2 * (j % 2) + e), TEXT_LEN)],
+                text_sem.at[i % 2, 2 * j + e],
+            )
+            for j in range(4)
+            for e in range(2)
+        ]
+
+    for copy in text_loads(0):
+        copy.start()
+    loads = [
+        local(normed_t, weights.at[0, 0], load_sem.at[0]),
+        local(mixed_t, weights.at[0, 1], load_sem.at[1]),
+        local(hidden_in, wide_field, load_sem.at[2]),
+        local(field_in, field, load_sem.at[3]),
+        local(two_low_in, two_low, load_sem.at[4]),
+        local(rows_in, rows, load_sem.at[5]),
+    ]
+    for copy in loads:
+        copy.start()
+    pass_quarters(pair_q, pair_slots, pair_s, pair_r)
+    finish_quarters(pair_q, pair_slots, pair_s, pair_r, keep_sem.at[0])
+
+    def text_step(i, _):
+        @pl.when(i < 3)
+        def _():
+            for copy in text_loads(i + 1):
+                copy.start()
+
+        for copy in text_loads(i):
+            copy.wait()
+        slot = 2 * (i % 2)
+        right = pair_slots[...].reshape(8 * TEXT_LEN, 2 * CHUNK)
+        value = jnp.dot(sources[slot], right[:512], preferred_element_type=f32)
+        value += jnp.dot(sources[slot + 1], right[512:], preferred_element_type=f32)
+        value = value.astype(bf16)
+        held[2 * i] = value[:, :CHUNK]
+        held[2 * i + 1] = value[:, CHUNK:]
+        offer(2 * i)
+        offer(2 * i + 1)
+        return 0
+
+    lax.fori_loop(0, 4, text_step, 0)
+
+    def source_loads(parts):
+        return [
+            local(parts[j].at[e], sources.at[2 * j + e], source_sem.at[2 * j + e])
+            for j in range(4)
+            for e in range(2)
+        ]
+
+    second_loads = source_loads((second0, second1, second2, second3))
+    for copy in second_loads:
+        copy.start()
+
+    across(both_w, both_far, both_s, both_r).wait()
+    loads[0].wait()
+    loads[1].wait()
+
+    def rhs_loads(q, j, slot):
+        col = pl.ds(pl.multiple_of(j * 1024 + q * CHUNK, CHUNK), CHUNK)
+        return (
+            local(both_w.at[:, col], rhs.at[slot, pl.ds(0, 512)], rhs_sem.at[slot, 0]),
+            local(both_far.at[:, col], rhs.at[slot, pl.ds(512, 512)], rhs_sem.at[slot, 1]),
+        )
+
+    staged = (hidden_q, held, held, held)
+    staged_base = (0, FIRST_IN, FIRST_IN + 4, FIRST_ATTN)
+
+    def rs_copy(m, j):
+        return remote(
+            staged[m].at[staged_base[m] + j], rs_in.at[m, j], rs_s.at[m, j], rs_r.at[m, j], steps[m][0]
+        )
+
+    order = (2, 0, 1, 3)
+    quarter_of = (px, py, pd, p)
+    for copy in rhs_loads(quarter_of[2], 0, 0):
+        copy.start()
+    for place, m in enumerate(order):
+
+        def attn_step(j, _, m=m, place=place):
+            slot = j % 2
+
+            @pl.when(j < 3)
+            def _():
+                for copy in rhs_loads(quarter_of[m], j + 1, 1 - slot):
+                    copy.start()
+
+            if place < 3:
+
+                @pl.when(j == 3)
+                def _():
+                    for copy in rhs_loads(quarter_of[order[place + 1]], 0, 1 - slot):
+                        copy.start()
+
+            for copy in rhs_loads(quarter_of[m], j, slot):
+                copy.wait()
+            left = weights[0, j // 3]
+            value = jnp.dot(left, rhs[slot], preferred_element_type=f32)
+            staged[m][staged_base[m] + j] = value.astype(bf16)
+            if m < 3:
+                rs_copy(m, j).start()
+            return 0
+
+        lax.fori_loop(0, 4, attn_step, 0)
+        if place == 1:
+            pass_quarters(two_q, two_slots, two_s, two_r)
+            tick(0)
+        if place == 3:
+            tick(1)
+
+    def conv_term_taps(slots):
+        for i in range(8):
+            put_shifts(slots[i].astype(f32), layouts[i] == 1, taps.at[i], slice(None))
+
+    def conv_term_loop(base, first_tick):
+        def step(t, _):
+            value = jnp.zeros((512, CHUNK), f32)
+            for i in range(8):
+                part = tap_rows(taps.at[i], 2 - t % 3, 2 - t // 3, slice(None))
+                value += jnp.dot(sources[i], part, preferred_element_type=f32)
+            held[base + t] = value.astype(bf16)
+            offer(base + t)
+
+            @pl.when(t % 3 == 2)
+            def _():
+                tick(first_tick + t // 3)
+
+            return 0
+
+        lax.fori_loop(0, 9, step, 0)
+
+    finish_quarters(two_q, two_slots, two_s, two_r, keep_sem.at[1])
+    conv_term_taps(two_slots)
+    for copy in second_loads:
+        copy.wait()
+    conv_term_loop(FIRST_OUT, 2)
+    first_loads = source_loads((first0, first1, first2, first3))
+    for copy in first_loads:
+        copy.start()
+
+    def conv_back(grad, w_own, w_far, first_tick):
+        def weight_loads(t):
+            slot = t % 2
+            return (
+                local(w_own.at[t], weights.at[slot, 0], weight_sem.at[slot, 0]),
+                local(w_far.at[t], weights.at[slot, 1], weight_sem.at[slot, 1]),
+            )
+
+        for copy in weight_loads(0):
+            copy.start()
+        for i in range(4):
+            put_shifts(
+                grad[:, i * CHUNK : (i + 1) * CHUNK].astype(f32), single, taps.at[i], slice(None)
+            )
+        acc[...] = jnp.zeros((512, 1024), f32)
+        last = (((1,), (1,)), ((), ()))
+
+        def step(t, _):
+            @pl.when(t < 8)
+            def _():
+                for copy in weight_loads(t + 1):
+                    copy.start()
+
+            for copy in weight_loads(t):
+                copy.wait()
+            part = jnp.concatenate(
+                [tap_rows(taps.at[i], 2 - t % 3, 2 - t // 3, slice(None)) for i in range(4)], axis=1
+            )
+            for side in range(2):
+                acc[:, side * 512 : side * 512 + 512] += lax.dot_general(
+                    part, weights[t % 2, side], last, preferred_element_type=f32
+                )
+
+            @pl.when(t % 3 == 2)
+            def _():
+                tick(first_tick + t // 3)
+
+            return 0
+
+        lax.fori_loop(0, 9, step, 0)
+
+    def norm_back(x, at, put):
+        ones = group_ones()
+
+        def block(i, _):
+            lanes = column(i)
+            parts = quadrants(x[:, lanes].astype(f32))
+            normed, rates = normalise(parts, single, ones)
+            gains = rows[at : at + 1, lanes]
+            shift = rows[at + 1 : at + 2, lanes]
+            pre = [part * gains[None] + shift[None] for part in normed]
+            grads = quadrants(acc[:, own_first(i * CHUNK, c, CHUNK)])
+            sig = [jax.nn.sigmoid(part) for part in pre]
+            grads = [g * s * (1.0 + v * (1.0 - s)) for g, s, v in zip(grads, sig, pre)]
+            small[pl.ds(2 * w + c, 1), at : at + 1, lanes] = sum(
+                jnp.sum(g * n, axis=(0, 1), keepdims=True) for g, n in zip(grads, normed)
+            )
+            small[pl.ds(2 * w + c, 1), at + 1 : at + 2, lanes] = sum(
+                jnp.sum(g, axis=(0, 1), keepdims=True) for g in grads
+            )
+            grads = [g * gains[None] for g in grads]
+            mean = region_mean(grads, single, ones)
+            slope = region_mean([g * n for g, n in zip(grads, normed)], single, ones)
+            put(
+                i,
+                lanes,
+                rejoin(
+                    [
+                        r[None] * (g - m[None] - n * s[None])
+                        for r, g, m, n, s in zip(rates, grads, mean, normed, slope)
+                    ]
+                ),
+            )
+            return 0
+
+        lax.fori_loop(0, 4, block, 0)
+
+    loads[4].wait()
+    loads[5].wait()
+    conv_back(two_low, out_own, out_far, 5)
+    loads[2].wait()
+
+    for m in range(3):
+        for j in range(4):
+            rs_copy(m, j).wait_send()
+
+    def put_hidden(i, lanes, value):
+        hidden_low[:, lanes] = value.astype(bf16)
+        hidden_q[i] = (value * weight[0]).astype(bf16)
+
+    norm_back(wide_field, 0, put_hidden)
+    start_quarters(hidden_q, hid_slots, hid_s, hid_r, keep_sem.at[2])
+    pass_load = local(passed_in, wide_field, keep_sem.at[3])
+    pass_load.start()
+
+    for m in range(3):
+        for j in range(4):
+            rs_copy(m, j).wait_recv()
+
+    def attn_sum(j, _):
+        k = FIRST_ATTN + j
+        value = held[k].astype(f32)
+        for m in range(3):
+            value += rs_in[m, j].astype(f32)
+        held[k] = value.astype(bf16)
+        offer(k)
+        return 0
+
+    lax.fori_loop(0, 4, attn_sum, 0)
+    tick(8)
+
+    conv_back(hidden_low, in_own, in_far, 9)
+    loads[3].wait()
+    pass_load.wait()
+
+    def put_input(i, lanes, value):
+        two_low[:, lanes] = (value + wide_field[:, lanes] * inv_root_two).astype(bf16)
+
+    norm_back(field, 2, put_input)
+    keep = local(two_low, input_grad, keep_sem.at[4])
+    keep.start()
+    me = 2 * w + c
+    small[pl.ds(me, 1), 4:8] = rows[4:8][None]
+    small[pl.ds(me, 1)] = small[pl.ds(me, 1)] * weight[0]
+    pass_quarters(hidden_q, hid_slots, hid_s, hid_r)
+    tick(12)
+    finish_quarters(hidden_q, hid_slots, hid_s, hid_r, keep_sem.at[2])
+    conv_term_taps(hid_slots)
+    for copy in first_loads:
+        copy.wait()
+
+    def small_rows(start, count):
+        return small.at[pl.ds(start, count)]
+
+    def small_copy(r):
+        if r == 0:
+            part = small_rows(me, 1)
+            return across(part, part, small_s.at[0], small_r.at[0])
+        if r == 1:
+            part = small_rows(2 * w, 2)
+            return remote(part, part, small_s.at[1], small_r.at[1], wx)
+        if r == 2:
+            part = small_rows(4 * (w // 2), 4)
+            return remote(part, part, small_s.at[2], small_r.at[2], wy)
+        if r == 3:
+            part = small_rows(8 * z, 8)
+            return remote(part, part, small_s.at[3], small_r.at[3], wz)
+        if r == 4:
+            part = small_rows(16 * (z // 2), 16)
+            return remote(part, part, small_s.at[4], small_r.at[4], wm)
+        part = small_rows(16 * (1 - z // 2), 16)
+        return remote(part, part, small_s.at[5], small_r.at[5], wz)
+
+    def small_arrival(r):
+        if r == 0:
+            part = small_rows(2 * w + 1 - c, 1)
+            return across(part, part, small_s.at[0], small_r.at[0])
+        if r == 1:
+            part = small_rows(2 * wx, 2)
+            return remote(part, part, small_s.at[1], small_r.at[1], wx)
+        if r == 2:
+            part = small_rows(4 * (wy // 2), 4)
+            return remote(part, part, small_s.at[2], small_r.at[2], wy)
+        if r == 3:
+            part = small_rows(8 * (wz // 4), 8)
+            return remote(part, part, small_s.at[3], small_r.at[3], wz)
+        if r == 4:
+            part = small_rows(16 * (wm // 8), 16)
+            return remote(part, part, small_s.at[4], small_r.at[4], wm)
+        part = small_rows(16 * (1 - z // 2), 16)
+        return remote(part, part, small_s.at[5], small_r.at[5], wz)
+
+    small_copy(0).start()
+    conv_term_loop(FIRST_IN, 13)
+    for r in range(4):
+        small_arrival(r).wait_recv()
+        if r < 3:
+            small_copy(r + 1).start()
+        tick(16 + r)
+
+    @pl.when(is_mid)
+    def _():
+        small_copy(4).start()
+        small_arrival(4).wait_recv()
+        small_copy(5).start()
+
+    def rest(k, _):
+        tick(k)
+        return 0
+
+    lax.fori_loop(20, CHUNKS + 3, rest, 0)
+
+    @pl.when(is_end)
+    def _():
+        small_arrival(5).wait_recv()
+
+    for r in range(4):
+        small_copy(r).wait_send()
+
+    @pl.when(is_mid)
+    def _():
+        small_copy(4).wait_send()
+        small_copy(5).wait_send()
+
+    small_keep = local(small, small_out, keep_sem.at[5])
+    small_keep.start()
+
+    def finish(k, _):
+        @pl.when(is_end)
+        def _():
+            up(k).wait_send()
+
+        @pl.when(is_mid)
+        def _():
+            over(k).wait_send()
+            down(k).wait_send()
+
+        to_x(k, p).wait_send()
+        to_y(k, p).wait_send()
+        on_x(k, py).wait_send()
+        on_y(k, px).wait_send()
+        own(k).wait()
+        return 0
+
+    lax.fori_loop(0, CHUNKS, finish, 0)
+    keep.wait()
+    small_keep.wait()
+
+
+def late(layouts, weight, *operands):
+    bf16, f32 = jnp.bfloat16, jnp.float32
+    any_spec = pl.BlockSpec(memory_space=pl.ANY)
+    smem = pl.BlockSpec(memory_space=pltpu.SMEM)
+    dma = pltpu.SemaphoreType.DMA
+    chunks = pltpu.VMEM((CHUNKS, 512, CHUNK), bf16)
+    map_low = pltpu.VMEM((512, 1024), bf16)
+    map_full = pltpu.VMEM((512, 1024), f32)
+    slots = pltpu.VMEM((8, 512, CHUNK), bf16)
+    return pl.pallas_call(
+        late_kernel,
+        out_shape=(
+            jax.ShapeDtypeStruct((CHUNKS, 512, 1024), bf16),
+            jax.ShapeDtypeStruct((512, 4096), bf16),
+            jax.ShapeDtypeStruct((512, 1024), bf16),
+            jax.ShapeDtypeStruct((32, 8, 1024), f32),
+        ),
+        in_specs=[smem, smem] + [any_spec] * len(operands),
+        out_specs=[any_spec] * 4,
+        scratch_shapes=[
+            chunks, chunks, chunks,
+            pltpu.VMEM((8, 3, 2, HALF_ROWS, CHUNK), bf16),
+            pltpu.VMEM((8, 512, 512), bf16),
+            pltpu.VMEM((8, TEXT_LEN, 2 * CHUNK), bf16),
+            slots, slots,
+            pltpu.VMEM((2, 1024, CHUNK), bf16),
+            pltpu.VMEM((3, 4, 512, CHUNK), bf16),
+            pltpu.VMEM((2, 2, 512, 1024), bf16),
+            map_full, map_full, map_low, map_low, map_low,
+            pltpu.VMEM((4, 512, CHUNK), bf16),
+            pltpu.VMEM((8, 1024), f32),
+            pltpu.VMEM((32, 8, 1024), f32),
+        ]
+        + [dma((CHUNKS,))] * 15
+        + [dma((7,))] * 6
+        + [dma, dma, dma((3, 4)), dma((3, 4)), dma((6,)), dma((6,))]
+        + [dma((2, 8)), dma((8,)), dma((2, 2)), dma((6,)), dma((2, 2)), dma((6,))],
+        compiler_params=pltpu.CompilerParams(
+            collective_id=0, has_side_effects=True, vmem_limit_bytes=62 << 20
+        ),
+        name="late_terms",
+    )(layouts, weight, *operands)
+
+
+def widen_kernel(low, out):
+    out[...] = low[...].reshape(out.shape).astype(jnp.float32)
+
+
+def widen(big, first, shape, block, count, where):
+    return pl.pallas_call(
+        widen_kernel,
+        out_shape=jax.ShapeDtypeStruct(shape, jnp.float32),
+        grid=(count,),
+        in_specs=[pl.BlockSpec((1, 512, 1024), lambda k: (first + k, 0, 0))],
+        out_specs=pl.BlockSpec(block, where),
+        name="widen",
+    )(big)
+
+
 def solution(mesh):
+    fits = mesh.shape["wide"] == 16 and mesh.shape["narrow"] == 2
+    body = pair_body if fits else plain_body
     placed = (
         P(("wide", "narrow"), None, None),
         P(("wide", "narrow")),

time: 1460 us -> 734 us (0.50)
  waiting for transfers between devices: 833 us -> 70.4 us
  Pallas kernels: 0 us -> 470 us
  matrix products: 186 us -> 55.2 us
  local copies, waits for them, and re-layouts: 165 us -> 49 us
  other arithmetic: 144 us -> 39.4 us
  blocking collectives: 98.1 us -> 0 us
  starting transfers between devices: 1.1 us -> 23.3 us
    psum x1 -> x0, waiting for transfers between devices: 780 us -> none  [every_wide_sum(): lax.psum(parts[9].astype(jnp.bfloat16), 'wide').astype(jnp.float32)]
    pallas_call x0 -> x8, Pallas kernels: none -> 470 us  [the longest x1 384 us: late(): pl.pallas_call(late_kernel, out_shape=(jax.ShapeDtypeStruct((CHUNKS, 512,...]
    dot_general x37 -> x13, matrix products: 186 us -> 55.2 us  [the longest x1 8.19 us: attention_mid(): jnp.dot(text_one, text_full, preferred_element_type=jnp.float32)]
    psum x2 -> x0, blocking collectives: 87 us -> none  [the longest x1 45.1 us: every_wide_sum(): lax.psum(parts[0].astype(jnp.bfloat16), 'wide').astype(jnp.float32)]
    ppermute x0 -> x22, waiting for transfers between devices: none -> 67.8 us  [the longest x13 61.4 us: to_wide(): return lax.ppermute(value, 'wide', [(i, i ^ step) for i in range(16)])]
    reshape x11 -> x8, local copies, waits for them, and re-layouts: 68.5 us -> 16.2 us  [the longest x1 3.03 us: attention_back(): grad_keys[:pixel_count].reshape(pixel_count, channels)]
    convert_element_type x26 -> x14, other arithmetic: 62.4 us -> 11.8 us  [the longest x1 3.64 us: pair_body(): (weight * jnp.concatenate([grad_triple, cot.astype(f32)], axis=1)).astype...]
    reduce_scatter x6 -> x0, waiting for transfers between devices: 49.2 us -> none  [the longest x1 32.3 us: body(): lax.psum_scatter(res_big[0].astype(jnp.bfloat16), 'narrow', scatter_dimen...]
  transfers between devices with their start and end apart: 13 -> 26, of which waited for: 3 -> 10; matrix products, arithmetic and copies ran while one was open for 27% -> 18% of each run, Pallas kernels for 0% -> 6%
where the time goes in v2:
time: 734 us; the launch traced here: 724 us
  Pallas kernels  470 us (64%)
  waiting for transfers between devices  70.4 us (10%)
  matrix products  55.2 us (8%)
  local copies, waits for them, and re-layouts  49 us (7%)
  other arithmetic  39.4 us (5%)
  starting transfers between devices  23.3 us (3%)
  between operations  16.9 us (2%)
    pallas_call x1, Pallas kernels, late(): pl.pallas_call(late_kernel, out_shape=(jax.ShapeDtypeStruct((CHUNKS, 512,...  384 us
    ppermute x13, waiting for transfers between devices, to_wide(): return lax.ppermute(value, 'wide', [(i, i ^ step) for i in range(16)])  61.4 us
    pallas_call x2, Pallas kernels, forward_conv(): pl.pallas_call(functools.partial(forward_conv_kernel, finish), out_shape=...  45.9 us
    pallas_call x5, Pallas kernels, widen(): pl.pallas_call(widen_kernel, out_shape=jax.ShapeDtypeStruct(shape, jnp.fl...  40.6 us
    ppermute x13, starting transfers between devices, to_wide(): return lax.ppermute(value, 'wide', [(i, i ^ step) for i in range(16)])  20.9 us
  transfers between devices with their start and end apart: 26, of which 10 were waited for; matrix products, arithmetic and copies ran while one was open for 18% of the time, Pallas kernels for 6%

profile of v2, /device:TPU:0, one launch (start us, length us, event | category | flops | bytes accessed | tf_op | source)
XLA Modules:
  0.0 724.4 jit_solution(14175263703519237331)
XLA Ops:
  18.5 6.4 collective-permute-done.3
  24.9 2.9 collective-permute-start.4
  29.5 2.1 collective-permute-start.5
  33.4 2.1 collective-permute-start.6
  37.5 3.5 collective-permute-start.7
  47.0 2.4 collective-permute-start.11
  50.0 2.9 convolution_convert_fusion.2
  53.5 3.6 fusion.51
  57.7 22.3 %forward_conv.2 = (bf16[512,1024]{1,0:T(8,128)(2,1)}, f32[512,1024]{1,0:T(8,128)}) custom-call(s32[2]{0:T(128)} %pad_add_fusion.info, bf16[512,1024]{1,0:T(8,128)(2,1)} %bitcast.129, f32[1,1024]{1,0:T(1,128)} %maximum_convert_fusion.scale, f32[1,1024]{1,0:T(1,128)} %maximum_convert_fusion.1.shift, bf16[9,512,1024]{2,1,0:T(8,128)(2,1)} %in_own.1, ...), custom_call_target="tpu_custom_call" | custom-call | tf_op jit(solution)/shard_map/forward_conv/pallas_call | solution.py:576
  82.7 23.6 %forward_conv.3 = (bf16[512,1024]{1,0:T(8,128)(2,1)}, f32[512,1024]{1,0:T(8,128)}, bf16[512,1024]{1,0:T(8,128)(2,1)}) custom-call(s32[2]{0:T(128)} %pad_add_fusion.info, f32[512,1024]{1,0:T(8,128)} %get-tuple-element.20.x.hidden_in, f32[1,1024]{1,0:T(1,128)} %bitcast.149, f32[1,1024]{1,0:T(1,128)} %bitcast.147, bf16[9,512,1024]{2,1,0:T(8,128)(2,1)} %out_own.1, ...), custom_call_target="tpu_custom_call" | custom-call | tf_op jit(solution)/shard_map/forward_conv/pallas_call | solution.py:576
  109.4 2.4 copy.70
  111.8 2.3 dynamic-slice_bitcast_fusion.3
  114.4 6.5 convolution_convert_fusion
  124.6 2.7 pad_maximum_fusion.3.first0
  127.4 2.4 collective-permute-start.19
  129.8 2.3 pad_maximum_fusion.2.second0
  132.1 2.1 pad_maximum_fusion.4.normed_t
  134.2 8.2 %convolution_convert_fusion.1 = bf16[128,2048]{1,0:T(8,128)(2,1)S(1)} fusion(bf16[4096,2048]{1,0:T(8,128)(2,1)} %all-gather.9.cloned.1.call-done, bf16[1,128,4096]{2,1,0:T(8,128)(2,1)S(1)} %copy-done.16), kind=kOutput, calls=%fused_computation.23 | convolution fusion | flops 2147745792 | bytes 18350080 | tf_op jit(solution)/shard_map/dot_general | solution.py:770
  144.3 2.1 copy.76
  146.4 3.8 fusion.50
  150.2 2.3 fusion
  152.6 4.5 fusion.16
  157.1 2.8 fusion.13
  159.9 5.2 multiply_reduce_fusion
  165.1 2.4 multiply_convert_fusion
  167.6 3.1 convolution_multiply_fusion
  174.5 2.9 copy.74
  177.4 2.7 convert.15
  180.1 3.0 copy.72
  184.7 3.0 copy.73
  190.8 6.6 multiply_reduce_fusion.1
  201.3 2.0 copy.57
  203.3 3.0 fusion.26
  206.3 2.2 reshape.291.pair_q
  213.5 2.2 collective-permute-start.15
  217.0 4.2 fusion.17
  221.2 3.6 fusion.1.both_w
  224.9 2.2 pad_maximum_fusion.5.mixed_t
  227.0 11.4 %collective-permute-done.18.first2 = bf16[2,512,512]{2,1,0:T(8,128)(2,1)S(1)} collective-permute-done((bf16[2,512,512]{2,1,0:T(8,128)(2,1)}, bf16[2,512,512]{2,1,0:T(8,128)(2,1)S(1)}, u32[]{:S(2)}, u32[]{:S(2)}) %collective-permute-start.18) | collective-permute-done | bytes 1048608 | tf_op jit(solution)/shard_map/ppermute | solution.py:592
  239.1 23.3 %collective-permute-done.15.second3 = bf16[2,512,512]{2,1,0:T(8,128)(2,1)S(1)} collective-permute-done((bf16[2,512,512]{2,1,0:T(8,128)(2,1)S(1)}, bf16[2,512,512]{2,1,0:T(8,128)(2,1)S(1)}, u32[]{:S(2)}, u32[]{:S(2)}) %collective-permute-start.15) | collective-permute-done | bytes 1048608 | tf_op jit(solution)/shard_map/ppermute | solution.py:592
  262.4 20.5 %collective-permute-done.14.second2 = bf16[2,512,512]{2,1,0:T(8,128)(2,1)S(1)} collective-permute-done((bf16[2,512,512]{2,1,0:T(8,128)(2,1)S(1)}, bf16[2,512,512]{2,1,0:T(8,128)(2,1)S(1)}, u32[]{:S(2)}, u32[]{:S(2)}) %collective-permute-start.14) | collective-permute-done | bytes 1048608 | tf_op jit(solution)/shard_map/ppermute | solution.py:592
  284.4 383.7 %late_terms.1 = (bf16[30,512,1024]{2,1,0:T(8,128)(2,1)}, bf16[512,4096]{1,0:T(8,128)(2,1)}, bf16[512,1024]{1,0:T(8,128)(2,1)}, f32[32,8,1024]{2,1,0:T(8,128)}) custom-call(s32[8]{0:T(128)} %fusion.29.layouts, f32[1]{0:T(128)} %bitcast.12.weight, bf16[4,128,512]{2,1,0:T(8,128)(2,1)} %reshape.291.pair_q, bf16[4,512,256]{2,1,0:T(8,128)(2,1)} %bitcast.137, ...), custom_call_target="tpu_custom_call" | custom-call | tf_op jit(solution)/shard_map/late_terms/pallas_call | solution.py:1427
  670.7 2.7 widen.8
  673.4 4.9 widen.7
  678.3 10.3 %widen.9 = f32[2048,2048]{1,0:T(8,128)} custom-call(bf16[30,512,1024]{2,1,0:T(8,128)(2,1)} %get-tuple-element.27.low), custom_call_target="tpu_custom_call" | custom-call | tf_op jit(solution)/shard_map/widen/pallas_call | solution.py:1467
  688.6 11.4 %widen.6 = f32[9,512,1024]{2,1,0:T(8,128)} custom-call(bf16[30,512,1024]{2,1,0:T(8,128)(2,1)} %get-tuple-element.27.low), custom_call_target="tpu_custom_call" | custom-call | tf_op jit(solution)/shard_map/widen/pallas_call | solution.py:1467
  699.9 11.4 %widen.5 = f32[9,512,1024]{2,1,0:T(8,128)} custom-call(bf16[30,512,1024]{2,1,0:T(8,128)(2,1)} %get-tuple-element.27.low), custom_call_target="tpu_custom_call" | custom-call | tf_op jit(solution)/shard_map/widen/pallas_call | solution.py:1467
  713.7 2.7 fusion.27
  (225 shorter events, 60.5 us)
Async XLA Ops:
  7.2 42.8 %all-gather.11.cloned.1.call-start = ((), (), s32[]{:S(2)}) async-start(), calls=%async_computation.3 | async-start | bytes 3145728 | tf_op jit(solution)/shard_map/all_gather | solution.py:675
  7.9 45.5 %all-gather.5.cloned.1.call-start = ((), (), s32[]{:S(2)}) async-start(), calls=%async_computation | async-start | bytes 6291456 | tf_op jit(solution)/shard_map/all_gather | solution.py:673
  8.7 105.7 %all-gather.7.cloned.1.call-start = ((), (), s32[]{:S(2)}) async-start(), calls=%async_computation.1 | async-start | bytes 9437184 | tf_op jit(solution)/shard_map/all_gather | solution.py:674
  9.4 3.7 copy-start.41
  9.4 4.1 copy-start.15
  9.5 124.7 %all-gather.9.cloned.1.call-start = ((), (), s32[]{:S(2)}) async-start(), calls=%async_computation.2 | async-start | bytes 25165824 | tf_op jit(solution)/shard_map/all_gather | solution.py:676
  10.0 5.3 copy-start.18
  10.0 47.7 %collective-permute-start.1 = (bf16[9,512,1024]{2,1,0:T(8,128)(2,1)}, bf16[9,512,1024]{2,1,0:T(8,128)(2,1)}, u32[]{:S(2)}, u32[]{:S(2)}) collective-permute-start(bf16[9,512,1024]{2,1,0:T(8,128)(2,1)} %in_own.1), channel_id=1, source_target_pairs={{0,1},{1,0},{2,3},{3,2},{4,5},{5,4},{6,7},{7,6},{8,9},{9,8},{10,11... | collective-permute-start | bytes 28311560 | tf_op jit(solution)/shard_map/ppermute | solution.py:596
  10.6 72.2 %collective-permute-start.2 = (bf16[9,512,1024]{2,1,0:T(8,128)(2,1)}, bf16[9,512,1024]{2,1,0:T(8,128)(2,1)}, u32[]{:S(2)}, u32[]{:S(2)}) collective-permute-start(bf16[9,512,1024]{2,1,0:T(8,128)(2,1)} %out_own.1), channel_id=1, source_target_pairs={{0,1},{1,0},{2,3},{3,2},{4,5},{5,4},{6,7},{7,6},{8,9},{9,8},{10,11... | collective-permute-start | bytes 28311560 | tf_op jit(solution)/shard_map/ppermute | solution.py:596
  12.1 12.8 %collective-permute-start.3 = (f32[1,1152]{1,0:T(1,128)S(1)}, f32[1,1152]{1,0:T(1,128)S(1)}, u32[]{:S(2)}, u32[]{:S(2)}) collective-permute-start(f32[1,1152]{1,0:T(1,128)S(1)} %broadcast_in_dim.61), channel_id=1, source_target_pairs={{0,1},{1,0},{2,3},{3,2},{4,5},{5,4},{6,7},{7,6},{8,9},{9,8},{10,11... | collective-permute-start | bytes 13832 | tf_op jit(solution)/shard_map/ppermute | solution.py:596
  13.4 14.4 %collective-permute-start = (bf16[2560]{0:T(1024)(128)(2,1)S(1)}, bf16[2560]{0:T(1024)(128)(2,1)S(1)}, u32[]{:S(2)}, u32[]{:S(2)}) collective-permute-start(bf16[2560]{0:T(1024)(128)(2,1)S(1)} %dynamic-update-slice.3), channel_id=1, source_target_pairs={{0,1},{1,0},{2,3},{3,2},{4,5},{5,4},{6,7},{7,6},{8,9},{9,8},{10,11... | collective-permute-start | bytes 15368 | tf_op jit(solution)/shard_map/ppermute | solution.py:596
  14.6 31.4 %collective-permute-start.8 = (bf16[2048,128]{1,0:T(8,128)(2,1)}, bf16[2048,128]{1,0:T(8,128)(2,1)S(1)}, u32[]{:S(2)}, u32[]{:S(2)}) collective-permute-start(bf16[2048,128]{1,0:T(8,128)(2,1)} %bitcast.29), channel_id=1, source_target_pairs={{0,1},{1,0},{2,3},{3,2},{4,5},{5,4},{6,7},{7,6},{8,9},{9,8},{10,11... | collective-permute-start | bytes 1572872 | tf_op jit(solution)/shard_map/ppermute | solution.py:596
  24.9 4.6 collective-permute-start.4
  29.5 3.9 collective-permute-start.5
  33.4 4.1 collective-permute-start.6
  37.5 5.8 collective-permute-start.7
  47.0 165.1 %collective-permute-start.11 = (bf16[2,2048,128]{2,1,0:T(8,128)(2,1)}, bf16[2,2048,128]{2,1,0:T(8,128)(2,1)}, u32[]{:S(2)}, u32[]{:S(2)}) collective-permute-start(bf16[2,2048,128]{2,1,0:T(8,128)(2,1)} %pad_maximum_fusion.1.text0), channel_id=1, source_target_pairs={{0,6},{2,4},{4,2},{6,0},{8,14},{10,12},{12,10},{14,8},{16,22},{18,... | collective-permute-start | bytes 3145736 | tf_op jit(solution)/shard_map/ppermute | solution.py:592
  49.5 163.4 %collective-permute-start.10 = (bf16[2,2048,128]{2,1,0:T(8,128)(2,1)}, bf16[2,2048,128]{2,1,0:T(8,128)(2,1)}, u32[]{:S(2)}, u32[]{:S(2)}) collective-permute-start(bf16[2,2048,128]{2,1,0:T(8,128)(2,1)} %pad_maximum_fusion.1.text0), channel_id=1, source_target_pairs={{0,4},{2,6},{4,0},{6,2},{8,12},{10,14},{12,8},{14,10},{16,20},{18,... | collective-permute-start | bytes 3145736 | tf_op jit(solution)/shard_map/ppermute | solution.py:592
  53.4 103.7 %copy-start.13 = (bf16[512,1024]{0,1:T(8,128)(2,1)}, bf16[512,1024]{0,1:T(8,128)(2,1)S(1)}, u32[]{:S(2)}) copy-start(bf16[512,1024]{0,1:T(8,128)(2,1)S(1)} %copy.77) | copy-start | bytes 3145732
  82.7 41.8 %collective-permute-start.16 = (bf16[512,512]{1,0:T(8,128)(2,1)}, bf16[512,512]{1,0:T(8,128)(2,1)}, u32[]{:S(2)}, u32[]{:S(2)}) collective-permute-start(bf16[512,512]{1,0:T(8,128)(2,1)} %get-tuple-element.42), channel_id=1, source_target_pairs={{0,1},{1,0},{2,3},{3,2},{4,5},{5,4},{6,7},{7,6},{8,9},{9,8},{10,11... | collective-permute-start | bytes 1572872 | tf_op jit(solution)/shard_map/ppermute | solution.py:596
  108.9 5.3 copy-start.5
  108.9 18.5 %collective-permute-start.12 = (bf16[512,512]{1,0:T(8,128)(2,1)}, bf16[512,512]{1,0:T(8,128)(2,1)}, u32[]{:S(2)}, u32[]{:S(2)}) collective-permute-start(bf16[512,512]{1,0:T(8,128)(2,1)} %get-tuple-element.44), channel_id=1, source_target_pairs={{0,1},{1,0},{2,3},{3,2},{4,5},{5,4},{6,7},{7,6},{8,9},{9,8},{10,11... | collective-permute-start | bytes 1572872 | tf_op jit(solution)/shard_map/ppermute | solution.py:596
  114.1 18.0 %collective-permute-start.20 = (bf16[512,512]{1,0:T(8,128)(2,1)}, bf16[512,512]{1,0:T(8,128)(2,1)}, u32[]{:S(2)}, u32[]{:S(2)}) collective-permute-start(bf16[512,512]{1,0:T(8,128)(2,1)} %get-tuple-element.40), channel_id=1, source_target_pairs={{0,1},{1,0},{2,3},{3,2},{4,5},{5,4},{6,7},{7,6},{8,9},{9,8},{10,11... | collective-permute-start | bytes 1572872 | tf_op jit(solution)/shard_map/ppermute | solution.py:596
  124.5 21.9 %copy-start.8 = (bf16[512,1024]{0,1:T(8,128)(2,1)}, bf16[512,1024]{0,1:T(8,128)(2,1)S(1)}, u32[]{:S(2)}) copy-start(bf16[512,1024]{0,1:T(8,128)(2,1)S(1)} %copy.75) | copy-start | bytes 3145732
  124.5 7.6 %copy-start.24 = (bf16[512,512]{1,0:T(8,128)(2,1)S(1)}, bf16[512,512]{1,0:T(8,128)(2,1)}, u32[]{:S(2)}) copy-start(bf16[512,512]{1,0:T(8,128)(2,1)} %get-tuple-element.39) | copy-start | bytes 1572868
  124.6 89.0 %collective-permute-start.9 = (bf16[2,2048,128]{2,1,0:T(8,128)(2,1)}, bf16[2,2048,128]{2,1,0:T(8,128)(2,1)}, u32[]{:S(2)}, u32[]{:S(2)}) collective-permute-start(bf16[2,2048,128]{2,1,0:T(8,128)(2,1)} %pad_maximum_fusion.1.text0), channel_id=1, source_target_pairs={{0,2},{2,0},{4,6},{6,4},{8,10},{10,8},{12,14},{14,12},{16,18},{18,... | collective-permute-start | bytes 3145736 | tf_op jit(solution)/shard_map/ppermute | solution.py:592
  127.4 6.8 copy-start.16
  127.4 88.4 %collective-permute-start.19 = (bf16[2,512,512]{2,1,0:T(8,128)(2,1)}, bf16[2,512,512]{2,1,0:T(8,128)(2,1)}, u32[]{:S(2)}, u32[]{:S(2)}) collective-permute-start(bf16[2,512,512]{2,1,0:T(8,128)(2,1)} %pad_maximum_fusion.3.first0), channel_id=1, source_target_pairs={{0,6},{2,4},{4,2},{6,0},{8,14},{10,12},{12,10},{14,8},{16,22},{18,... | collective-permute-start | bytes 3145736 | tf_op jit(solution)/shard_map/ppermute | solution.py:592
  134.2 8.9 %copy-start.22 = (bf16[512,1024]{1,0:T(8,128)(2,1)S(1)}, bf16[512,1024]{1,0:T(8,128)(2,1)}, u32[]{:S(2)}) copy-start(bf16[512,1024]{1,0:T(8,128)(2,1)} %get-tuple-element.35) | copy-start | bytes 3145732
  146.4 3.8 copy-start.10
  159.9 13.0 %copy-start.12 = (f32[640,8,128]{0,2,1:T(8,128)}, f32[640,8,128]{0,2,1:T(8,128)S(1)}, u32[]{:S(2)}) copy-start(f32[640,8,128]{0,2,1:T(8,128)S(1)} %fusion.13) | copy-start | bytes 7864324
  172.9 43.5 %collective-permute-start.21 = (bf16[512,512]{1,0:T(8,128)(2,1)}, bf16[512,512]{1,0:T(8,128)(2,1)}, u32[]{:S(2)}, u32[]{:S(2)}) collective-permute-start(bf16[512,512]{1,0:T(8,128)(2,1)} %get-tuple-element.38), channel_id=1, source_target_pairs={{0,1},{1,0},{2,3},{3,2},{4,5},{5,4},{6,7},{7,6},{8,9},{9,8},{10,11... | collective-permute-start | bytes 1572872 | tf_op jit(solution)/shard_map/ppermute | solution.py:596
  200.2 8.2 %copy-start.14 = (f32[512,1024]{1,0:T(8,128)S(1)}, f32[512,1024]{1,0:T(8,128)}, u32[]{:S(2)}) copy-start(f32[512,1024]{1,0:T(8,128)} %get-tuple-element.33) | copy-start | bytes 6291460
  201.3 7.2 copy-start.19
  209.9 7.2 copy-start.7
  212.2 9.0 %copy-start = (f32[512,1024]{1,0:T(8,128)S(1)}, f32[512,1024]{1,0:T(8,128)}, u32[]{:S(2)}) copy-start(f32[512,1024]{1,0:T(8,128)} %copy.74) | copy-start | bytes 6291460
  212.2 9.0 %copy-start.1 = (f32[512,1024]{1,0:T(8,128)S(1)}, f32[512,1024]{1,0:T(8,128)}, u32[]{:S(2)}) copy-start(f32[512,1024]{1,0:T(8,128)} %copy.72) | copy-start | bytes 6291460
  212.2 9.0 %copy-start.3 = (f32[512,1024]{1,0:T(8,128)S(1)}, f32[512,1024]{1,0:T(8,128)}, u32[]{:S(2)}) copy-start(f32[512,1024]{1,0:T(8,128)} %copy.73) | copy-start | bytes 6291460
  212.2 26.2 %collective-permute-start.18 = (bf16[2,512,512]{2,1,0:T(8,128)(2,1)}, bf16[2,512,512]{2,1,0:T(8,128)(2,1)S(1)}, u32[]{:S(2)}, u32[]{:S(2)}) collective-permute-start(bf16[2,512,512]{2,1,0:T(8,128)(2,1)} %pad_maximum_fusion.3.first0), channel_id=1, source_target_pairs={{0,4},{2,6},{4,0},{6,2},{8,12},{10,14},{12,8},{14,10},{16,20},{18,... | collective-permute-start | bytes 3145736 | tf_op jit(solution)/shard_map/ppermute | solution.py:592
  212.9 26.2 %collective-permute-start.17 = (bf16[2,512,512]{2,1,0:T(8,128)(2,1)}, bf16[2,512,512]{2,1,0:T(8,128)(2,1)S(1)}, u32[]{:S(2)}, u32[]{:S(2)}) collective-permute-start(bf16[2,512,512]{2,1,0:T(8,128)(2,1)} %pad_maximum_fusion.3.first0), channel_id=1, source_target_pairs={{0,2},{2,0},{4,6},{6,4},{8,10},{10,8},{12,14},{14,12},{16,18},{18,... | collective-permute-start | bytes 3145736 | tf_op jit(solution)/shard_map/ppermute | solution.py:592
  213.5 48.9 %collective-permute-start.15 = (bf16[2,512,512]{2,1,0:T(8,128)(2,1)S(1)}, bf16[2,512,512]{2,1,0:T(8,128)(2,1)S(1)}, u32[]{:S(2)}, u32[]{:S(2)}) collective-permute-start(bf16[2,512,512]{2,1,0:T(8,128)(2,1)S(1)} %copy-done.17), channel_id=1, source_target_pairs={{0,6},{2,4},{4,2},{6,0},{8,14},{10,12},{12,10},{14,8},{16,22},{18,... | collective-permute-start | bytes 3145736 | tf_op jit(solution)/shard_map/ppermute | solution.py:592
  215.7 67.2 %collective-permute-start.14 = (bf16[2,512,512]{2,1,0:T(8,128)(2,1)S(1)}, bf16[2,512,512]{2,1,0:T(8,128)(2,1)S(1)}, u32[]{:S(2)}, u32[]{:S(2)}) collective-permute-start(bf16[2,512,512]{2,1,0:T(8,128)(2,1)S(1)} %copy-done.17), channel_id=1, source_target_pairs={{0,4},{2,6},{4,0},{6,2},{8,12},{10,14},{12,8},{14,10},{16,20},{18,... | collective-permute-start | bytes 3145736 | tf_op jit(solution)/shard_map/ppermute | solution.py:592
  216.4 67.0 %collective-permute-start.13 = (bf16[2,512,512]{2,1,0:T(8,128)(2,1)S(1)}, bf16[2,512,512]{2,1,0:T(8,128)(2,1)S(1)}, u32[]{:S(2)}, u32[]{:S(2)}) collective-permute-start(bf16[2,512,512]{2,1,0:T(8,128)(2,1)S(1)} %copy-done.17), channel_id=1, source_target_pairs={{0,2},{2,0},{4,6},{6,4},{8,10},{10,8},{12,14},{14,12},{16,18},{18,... | collective-permute-start | bytes 3145736 | tf_op jit(solution)/shard_map/ppermute | solution.py:592
  238.4 45.0 %copy-start.25 = (bf16[2,512,512]{2,1,0:T(8,128)(2,1)}, bf16[2,512,512]{2,1,0:T(8,128)(2,1)S(1)}, u32[]{:S(2)}) copy-start(bf16[2,512,512]{2,1,0:T(8,128)(2,1)S(1)} %collective-permute-done.18.first2) | copy-start | bytes 3145732
  239.1 44.3 %copy-start.26 = (bf16[2,512,512]{2,1,0:T(8,128)(2,1)}, bf16[2,512,512]{2,1,0:T(8,128)(2,1)S(1)}, u32[]{:S(2)}) copy-start(bf16[2,512,512]{2,1,0:T(8,128)(2,1)S(1)} %collective-permute-done.17.first1) | copy-start | bytes 3145732
  262.4 21.0 %copy-start.27 = (bf16[2,512,512]{2,1,0:T(8,128)(2,1)}, bf16[2,512,512]{2,1,0:T(8,128)(2,1)S(1)}, u32[]{:S(2)}) copy-start(bf16[2,512,512]{2,1,0:T(8,128)(2,1)S(1)} %collective-permute-done.15.second3) | copy-start | bytes 3145732
  699.9 13.8 %copy-start.35 = (bf16[32,1024]{1,0:T(8,128)(2,1)S(1)}, bf16[32,1024]{1,0:T(8,128)(2,1)}, u32[]{:S(2)}) copy-start(bf16[32,1024]{1,0:T(8,128)(2,1)} %gather_fusion) | copy-start | bytes 196612
  711.3 5.1 copy-start.33
  (24 other events, 58.2 us)
Sparse Core Ops, SparseCore 0:
  9.6 19.2 all-gather.10
  30.4 16.2 all-gather.4
  48.2 17.9 all-gather.6
  67.5 31.2 all-gather.8

commit v3 on v2

--- a/solution.py
+++ b/solution.py
@@ -440,6 +440,7 @@
 
 CHUNK = 256
 HALF_ROWS = 10 * MAP_W
+HEAD_DIM = 128
 
 
 def quadrants(values):
@@ -484,24 +485,26 @@
 
 
 def put_shifts(values, single, taps, lanes):
-    pixel = lax.broadcasted_iota(jnp.int32, values.shape, 0) % MAP_W
+    shape = values.shape
+    pixel = lax.broadcasted_iota(jnp.int32, shape, 0) % MAP_W
+    blank = jnp.zeros((MAP_W, shape[1]), jnp.bfloat16)
     for s in range(3):
         if s == 1:
             moved = values
         elif s == 2:
             moved = pltpu.roll(values, MAP_H * MAP_W - 1, 0)
-            moved = jnp.where(
-                (pixel != MAP_W - 1) & (single | (pixel != MAP_W // 2 - 1)), moved, 0.0
-            )
+            keep = single(shape) | (pixel != MAP_W // 2 - 1)
+            moved = jnp.where((pixel != MAP_W - 1) & keep, moved, 0.0)
         else:
             moved = pltpu.roll(values, 1, 0)
-            moved = jnp.where((pixel != 0) & (single | (pixel != MAP_W // 2)), moved, 0.0)
+            keep = single(shape) | (pixel != MAP_W // 2)
+            moved = jnp.where((pixel != 0) & keep, moved, 0.0)
         low = moved.astype(jnp.bfloat16)
-        blank = jnp.zeros((MAP_W, values.shape[1]), jnp.bfloat16)
+        strip = single((MAP_W, shape[1]))
         taps[s, 0, 0:32, lanes] = blank
         taps[s, 0, 32:288, lanes] = low[0:256]
-        taps[s, 0, 288:320, lanes] = jnp.where(single, moved[256:288], 0.0).astype(jnp.bfloat16)
-        taps[s, 1, 0:32, lanes] = jnp.where(single, moved[224:256], 0.0).astype(jnp.bfloat16)
+        taps[s, 0, 288:320, lanes] = jnp.where(strip, moved[256:288], 0.0).astype(jnp.bfloat16)
+        taps[s, 1, 0:32, lanes] = jnp.where(strip, moved[224:256], 0.0).astype(jnp.bfloat16)
         taps[s, 1, 32:288, lanes] = low[256:512]
         taps[s, 1, 288:320, lanes] = blank
 
@@ -513,111 +516,6 @@
 
 def own_first(start, core, width):
     return pl.ds(pl.multiple_of((start + core * 512) % 1024, width), width)
-
-
-def forward_conv_kernel(finish, info, x, scale, shift, w_own, w_far, *refs):
-    if finish:
-        pixels, ln_gain, low_out, joined_out, normed_out, taps, acc = refs
-    else:
-        low_out, acc, taps = refs
-    t = pl.program_id(0)
-    core = info[0]
-    single = info[1] == 1
-
-    @pl.when(t == 0)
-    def _():
-        ones = group_ones()
-        for start in range(0, 1024, CHUNK):
-            lanes = pl.ds(start, CHUNK)
-            parts = quadrants(x[:, lanes].astype(jnp.float32))
-            normed, _ = normalise(parts, single, ones)
-            pre = rejoin(normed) * scale[:, lanes] + shift[:, lanes]
-            act = pre * jax.nn.sigmoid(pre)
-            low_out[:, lanes] = act.astype(jnp.bfloat16)
-            put_shifts(act, single, taps, own_first(start, core, CHUNK))
-
-    rows = tap_rows(taps, t % 3, t // 3, slice(None))
-    fresh = jnp.dot(rows[:, :512], w_own[0], preferred_element_type=jnp.float32)
-    fresh += jnp.dot(rows[:, 512:], w_far[0], preferred_element_type=jnp.float32)
-
-    @pl.when(t == 0)
-    def _():
-        acc[...] = fresh
-
-    @pl.when(t > 0)
-    def _():
-        acc[...] += fresh
-
-    if finish:
-
-        @pl.when(t == 8)
-        def _():
-            joined = (pixels[...].astype(jnp.float32) + acc[...]) * inv_root_two
-            joined_out[...] = joined
-            centre = joined - jnp.mean(joined, axis=1, keepdims=True)
-            rate = lax.rsqrt(jnp.mean(centre * centre, axis=1, keepdims=True) + epsilon)
-            normed_out[...] = (centre * rate * ln_gain[...]).astype(jnp.bfloat16)
-
-
-def whole(shape):
-    return pl.BlockSpec(shape, lambda t, *_: (0,) * len(shape))
-
-
-def forward_conv(info, x, scale, shift, w_own, w_far, extra=None):
-    finish = extra is not None
-    full = jax.ShapeDtypeStruct((512, 1024), jnp.float32)
-    low = jax.ShapeDtypeStruct((512, 1024), jnp.bfloat16)
-    field = whole((512, 1024))
-    row = whole((1, 1024))
-    tap = pl.BlockSpec((1, 512, 1024), lambda t, *_: (t, 0, 0))
-    scratch = [pltpu.VMEM((3, 2, HALF_ROWS, 1024), jnp.bfloat16)]
-    if finish:
-        scratch += [pltpu.VMEM((512, 1024), jnp.float32)]
-    return pl.pallas_call(
-        functools.partial(forward_conv_kernel, finish),
-        out_shape=(low, full, low) if finish else (low, full),
-        grid_spec=pltpu.PrefetchScalarGridSpec(
-            num_scalar_prefetch=1,
-            grid=(9,),
-            in_specs=[field, row, row, tap, tap] + ([field, row] if finish else []),
-            out_specs=(field, field, field) if finish else (field, field),
-            scratch_shapes=scratch,
-        ),
-        compiler_params=pltpu.CompilerParams(vmem_limit_bytes=56 << 20),
-        name="forward_conv",
-    )(info, x, scale, shift, w_own, w_far, *(extra or ()))
-
-
-def to_wide(value, step):
-    return lax.ppermute(value, "wide", [(i, i ^ step) for i in range(16)])
-
-
-def to_far(value):
-    return lax.ppermute(value, "narrow", [(0, 1), (1, 0)])
-
-
-def gather_all(row):
-    rows = row[None]
-    rows = jnp.concatenate([rows, to_far(rows)])
-    for step in (1, 2, 4, 8):
-        rows = jnp.concatenate([rows, to_wide(rows, step)])
-    return rows
-
-
-def half_of(value, core, axis):
-    size = value.shape[axis] // 2
-    return lax.dynamic_slice_in_dim(value, core * size, size, axis)
-
-
-def share_source(value_t, core):
-    far = to_far(half_of(value_t, 1 - core, 0))
-    pair = jnp.stack([half_of(value_t, core, 0), far])
-    return (pair, to_wide(pair, 1), to_wide(pair, 2), to_wide(pair, 3))
-
-
-def pair_of(value_t, core):
-    far = to_far(half_of(value_t, 1 - core, 0))
-    return jnp.concatenate([half_of(value_t, core, 0), far], axis=1)
 
 
 def pair_body(
@@ -639,102 +537,31 @@
     text_weight,
 ):
     f32, bf16 = jnp.float32, jnp.bfloat16
-    wide = lax.axis_index("wide")
     core = lax.axis_index("narrow")
-    group_total = lax.axis_size("wide")
-
-    conv_in_far = to_far(conv_in)
-    vectors = jnp.concatenate([gn_gain, gn_bias, ln_gain, film_bias])
-    vectors_far = to_far(vectors)
-    low_vec = jnp.where(core == 0, vectors, vectors_far)
-    high_vec = jnp.where(core == 0, vectors_far, vectors)
-
-    def joined_vec(start, size):
-        return jnp.concatenate([low_vec[start : start + size], high_vec[start : start + size]])
-
-    gain_row = joined_vec(0, 512).astype(f32)[None]
-    bias_row = joined_vec(512, 512).astype(f32)[None]
-    ln_row = joined_vec(1024, 512).astype(f32)[None]
-    film_bias_full = joined_vec(1536, 1024).astype(f32)
-    conv_out_far = to_far(conv_out)
-
-    facts = jnp.stack([noise_group[0], layout[0]])
-    facts = jnp.pad(facts.astype(f32), (0, 126))
-    early = gather_all(jnp.concatenate([cond_embed[0].astype(f32), facts]))
-    cond_all = early[:, :1024]
-    alike = jnp.sum((early[:, 1024] == facts[0]).astype(f32))
-    weight = 1.0 / (group_total * alike)
-    info = jnp.stack([core.astype(jnp.int32), layout[0]])
-    layouts = early[:8, 1025].astype(jnp.int32)
-
     text_one = text_embed[0]
-    text_sources = share_source(text_one.T, core)
-    cot = cotangent[0]
-    film_full = lax.all_gather(film_weight, "narrow", axis=0, tiled=True)
-    qkv_full = lax.all_gather(qkv_weight, "narrow", axis=0, tiled=True)
-    out_full = lax.all_gather(out_weight, "narrow", axis=0, tiled=True)
-    text_full = lax.all_gather(text_weight, "narrow", axis=0, tiled=True)
-
-    region_ids = region_ids_of(layout[0])
-    field = pixels[0]
-    condition = jax.nn.silu(cond_embed[0].astype(f32)).astype(bf16)
-    film_out = jnp.dot(condition, film_full, preferred_element_type=f32) + film_bias_full
-    film_scale = 1.0 + film_out[None, :1024]
-    film_shift = film_out[None, 1024:]
-
-    first_low, hidden_one = forward_conv(info, field, gain_row, bias_row, conv_in, conv_in_far)
-    first_sources = share_source(first_low.T, core)
-    second_low, joined, normed = forward_conv(
-        info, hidden_one, film_scale, film_shift, conv_out, conv_out_far, (field, ln_row)
-    )
-    second_sources = share_source(second_low.T, core)
-
-    attn_full = (ln_row[0], qkv_full, out_full, text_full)
-    result, stored = attention_mid(normed, joined, text_one, region_ids, attn_full)
-    output = result.astype(bf16)
-    grad_joined, ln_term, grad_triple, grad_pair = attention_back(
-        cot, joined, stored, attn_full
-    )
-    mixed = stored[5]
-    grad_two = grad_joined * inv_root_two
-    grad_two_low = grad_two.astype(bf16)
-
-    pair_w = (weight * grad_pair).astype(bf16)
-    pair_q = pair_w.reshape(TEXT_LEN, 2, 4, CHUNK).transpose(2, 0, 1, 3).reshape(4, TEXT_LEN, 512)
-    two_w = (weight * grad_two).astype(bf16)
-    two_q = two_w.reshape(512, 4, CHUNK).transpose(1, 0, 2)
-    both_w = (weight * jnp.concatenate([grad_triple, cot.astype(f32)], axis=1)).astype(bf16)
-    rows = jnp.concatenate(
-        [film_scale, film_shift, gain_row, bias_row, ln_term[None], jnp.zeros((3, 1024), f32)]
-    )
-
-    big, _, input_grad, small_all = late(
-        layouts,
-        weight.reshape(1),
-        pair_q,
-        two_q,
-        both_w,
-        *text_sources,
-        *second_sources,
-        *first_sources,
-        pair_of(normed.T, core),
-        pair_of(mixed.T, core),
-        grad_two_low,
-        hidden_one,
-        field,
-        grad_joined,
-        rows,
+    facts = jnp.stack([noise_group[0], layout[0]]).astype(f32)
+    facts = jnp.stack([cond_embed[0].astype(f32), jnp.pad(facts, (0, 1022))])
+    halves = jnp.stack([gn_gain, gn_bias, ln_gain]).astype(f32)
+    big, output, input_grad, small_all, early = run_whole(
+        layout,
+        pixels[0],
+        cotangent[0],
+        text_one.T,
+        text_one,
+        conv_in,
         conv_out,
-        conv_out_far,
-        conv_in,
-        conv_in_far,
-    )
-    me = 2 * wide + core
-    film_all = small_all[:, :2].reshape(32, 2048)
-    cond_low = jax.nn.silu(cond_all).astype(bf16)[jnp.bitwise_xor(jnp.arange(32), me)]
+        film_weight,
+        qkv_weight,
+        out_weight,
+        text_weight,
+        jnp.pad(facts, ((0, 6), (0, 0))),
+        jnp.pad(halves, ((0, 5), (0, 0))),
+        jnp.pad(film_bias.astype(f32)[None], ((0, 7), (0, 0))),
+    )
+    cond_low = jax.nn.silu(early[:, 0]).astype(bf16)
     grad_film_weight = lax.dot_general(
         half_of(cond_low, core, 1),
-        film_all.astype(bf16),
+        small_all[:, :2].reshape(32, 2048).astype(bf16),
         (((0,), (0,)), ((), ())),
         preferred_element_type=f32,
     )
@@ -761,128 +588,40 @@
     )
 
 
-def attention_mid(normed_low, joined, text_one, region_ids, attn_full):
-    _, qkv_full, out_full, text_full = attn_full
-    pixel_count, channels = joined.shape
-    head_dim = channels // HEADS
-    score_scale = head_dim ** (-0.5)
-    triple = jnp.dot(normed_low, qkv_full, preferred_element_type=jnp.float32).astype(jnp.bfloat16)
-    text_pair = jnp.dot(text_one, text_full, preferred_element_type=jnp.float32).astype(
-        jnp.bfloat16
-    )
-    queries = triple[:, :channels].reshape(pixel_count, HEADS, head_dim)
-    key_rows = jnp.concatenate(
-        [triple[:, channels : 2 * channels], text_pair[:, :channels]], axis=0
-    ).reshape(-1, HEADS, head_dim)
-    value_rows = jnp.concatenate(
-        [triple[:, 2 * channels :], text_pair[:, channels:]], axis=0
-    ).reshape(-1, HEADS, head_dim)
-    allowed = allowed_keys(region_ids)
-    masked = jnp.where(
-        allowed[None],
-        jnp.einsum("phd,jhd->hpj", queries, key_rows, preferred_element_type=jnp.float32)
-        * score_scale,
-        masked_score,
-    )
-    row_peak = jnp.max(masked, axis=2, keepdims=True)
-    exponent = jnp.exp(masked - row_peak)
-    exp_total = jnp.sum(exponent, axis=2, keepdims=True)
-    attn_probs = exponent / exp_total
-    log_total = row_peak + jnp.log(exp_total)
-    mixed = (
-        jnp.einsum(
-            "hpj,jhd->phd",
-            attn_probs.astype(jnp.bfloat16),
-            value_rows,
-            preferred_element_type=jnp.float32,
-        )
-        .reshape(pixel_count, channels)
-        .astype(jnp.bfloat16)
-    )
-    result = joined + jnp.dot(mixed, out_full, preferred_element_type=jnp.float32)
-    return (result, (normed_low, queries, key_rows, value_rows, log_total, mixed, allowed))
-
-
-def attention_back(grad_result, joined, stored, attn_full):
-    gain_row, qkv_full, out_full, text_full = attn_full
-    normed_low, queries, key_rows, value_rows, log_total, mixed, allowed = stored
-    pixel_count, channels = joined.shape
-    head_dim = channels // HEADS
-    score_scale = head_dim ** (-0.5)
-    grad_mixed = (
-        jnp.einsum("pd,cd->pc", grad_result, out_full, preferred_element_type=jnp.float32)
-        .astype(jnp.bfloat16)
-        .reshape(pixel_count, HEADS, head_dim)
-    )
-    masked = jnp.where(
-        allowed[None],
-        jnp.einsum("phd,jhd->hpj", queries, key_rows, preferred_element_type=jnp.float32)
-        * score_scale,
-        masked_score,
-    )
-    attn_probs = jnp.exp(masked - log_total)
-    grad_probs = jnp.einsum(
-        "phd,jhd->hpj", grad_mixed, value_rows, preferred_element_type=jnp.float32
-    )
-    grad_values = jnp.einsum(
-        "hpj,phd->jhd",
-        attn_probs.astype(jnp.bfloat16),
-        grad_mixed,
-        preferred_element_type=jnp.float32,
-    )
-    row_inner = jnp.sum(attn_probs * grad_probs, axis=2, keepdims=True)
-    grad_scores = (attn_probs * (grad_probs - row_inner)).astype(jnp.bfloat16)
-    grad_queries = (
-        jnp.einsum("hpj,jhd->phd", grad_scores, key_rows, preferred_element_type=jnp.float32)
-        * score_scale
-    )
-    grad_keys = (
-        jnp.einsum("hpj,phd->jhd", grad_scores, queries, preferred_element_type=jnp.float32)
-        * score_scale
-    )
-    grad_triple = jnp.concatenate(
-        [
-            grad_queries.reshape(pixel_count, channels),
-            grad_keys[:pixel_count].reshape(pixel_count, channels),
-            grad_values[:pixel_count].reshape(pixel_count, channels),
-        ],
-        axis=1,
-    )
-    grad_pair = jnp.concatenate(
-        [
-            grad_keys[pixel_count:].reshape(-1, channels),
-            grad_values[pixel_count:].reshape(-1, channels),
-        ],
-        axis=1,
-    )
-    grad_normed = jnp.einsum(
-        "pk,ck->pc", grad_triple.astype(jnp.bfloat16), qkv_full, preferred_element_type=jnp.float32
-    )
-    _, norm_back = jax.vjp(layer_norm, joined, gain_row)
-    grad_joined_norm, term_gain = norm_back(grad_normed)
-    return (grad_result.astype(jnp.float32) + grad_joined_norm, term_gain, grad_triple, grad_pair)
+def half_of(value, core, axis):
+    size = value.shape[axis] // 2
+    return lax.dynamic_slice_in_dim(value, core * size, size, axis)
 
 
 MESH = pl.DeviceIdType.MESH
 CHUNKS = 30
 FIRST_OUT, FIRST_ATTN, FIRST_IN = 8, 17, 21
-
-
-def late_kernel(
-    layouts, weight,
-    pair_q, two_q, both_w, text0, text1, text2, text3, second0, second1, second2, second3,
-    first0, first1, first2, first3, normed_t, mixed_t, two_low_in, hidden_in, field_in,
-    passed_in, rows_in, out_own, out_far, in_own, in_far,
-    big, both_far, input_grad, small_out,
-    held, total, cross, taps, sources, pair_slots, two_slots, hid_slots, rhs, rs_in,
-    weights, acc, wide_field, field, two_low, hidden_low, hidden_q, rows, small,
+NORMED, GRAD_MIXED, MIXED, TEXT_KEYS, TEXT_VALUES = 12, 16, 20, 24, 25
+LAST = (((1,), (1,)), ((), ()))
+ROWS = (((0,), (0,)), ((), ()))
+
+
+def whole_kernel(
+    layout,
+    field_in, cot_in, text_t, text_in, conv_in, conv_out, film, qkv, out_w, text_w,
+    facts_in, halves_in, film_bias_in,
+    big, output, input_grad, small_out, early_out,
+    in_far, out_far, film_far, qkv_far, out_w_far, text_w_far, cot_far,
+    text_src, first_src, second_src, turned, both_own, both_far, rs_land,
+    held, total, cross, taps, sources, pair_slots, two_slots, hid_slots, rhs,
+    weights, acc, wide_field, extra, field, two_low, hidden_low, hidden_q, pair_q, text_low,
+    rows, halves, film_bias, small, early,
     s1s, s1r, s2s, s2r, s3s, s3r, xs, xr, ys, yr, d0s, d0r, d1s, d1r, own_sem,
-    pair_s, pair_r, two_s, two_r, hid_s, hid_r, both_s, both_r, rs_s, rs_r, small_s, small_r,
-    text_sem, source_sem, rhs_sem, load_sem, weight_sem, keep_sem,
+    pair_s, pair_r, two_s, two_r, hid_s, hid_r, both_s, both_r, rs_s, rs_r,
+    small_s, small_r, early_s, early_r,
+    in_s, in_r, out_s, out_r, far_s, far_r, text_ws, text_wr,
+    src_s, src_r, turn_s, turn_r,
+    text_sem, source_sem, rhs_sem, load_sem, weight_sem, keep_sem, turn_sem, both_sem,
 ):
     f32, bf16 = jnp.float32, jnp.bfloat16
     w = lax.axis_index("wide")
     c = lax.axis_index("narrow")
+    me = 2 * w + c
     p = w % 4
     z = w // 4
     wx = w + 1 - 2 * (w % 2)
@@ -896,21 +635,7 @@
     steps = ((wx, px), (wy, py), (wd, pd))
     is_mid = (z == 1) | (z == 2)
     is_end = (z == 0) | (z == 3)
-    single = layouts[0] == 1
-
-    bar = pltpu.get_barrier_semaphore()
-    for t in (wx, wy, wd, wz):
-        pl.semaphore_signal(bar, inc=1, device_id=(t, c), device_id_type=MESH)
-    pl.semaphore_signal(bar, inc=1, device_id=(w, 1 - c), device_id_type=MESH)
-
-    @pl.when(is_mid)
-    def _():
-        pl.semaphore_signal(bar, inc=1, device_id=(wm, c), device_id_type=MESH)
-        pl.semaphore_wait(bar, 6)
-
-    @pl.when(is_end)
-    def _():
-        pl.semaphore_wait(bar, 5)
+    single = layout[0] == 1
 
     def remote(src, dst, ss, rs, t):
         return pltpu.make_async_remote_copy(
@@ -925,6 +650,30 @@
 
     def local(src, dst, sem):
         return pltpu.make_async_copy(src, dst, sem)
+
+    loads = [
+        local(field_in, field, load_sem.at[0]),
+        local(halves_in, halves.at[:, pl.ds(pl.multiple_of(c * 512, 512), 512)], load_sem.at[1]),
+        local(film_bias_in, film_bias.at[c], load_sem.at[2]),
+        local(facts_in, early.at[me], load_sem.at[3]),
+        local(cot_in, two_low, load_sem.at[4]),
+    ]
+    for copy in loads:
+        copy.start()
+
+    bar = pltpu.get_barrier_semaphore()
+    for t in (wx, wy, wd, wz):
+        pl.semaphore_signal(bar, inc=1, device_id=(t, c), device_id_type=MESH)
+    pl.semaphore_signal(bar, inc=1, device_id=(w, 1 - c), device_id_type=MESH)
+
+    @pl.when(is_mid)
+    def _():
+        pl.semaphore_signal(bar, inc=1, device_id=(wm, c), device_id_type=MESH)
+        pl.semaphore_wait(bar, 6)
+
+    @pl.when(is_end)
+    def _():
+        pl.semaphore_wait(bar, 5)
 
     def quarter_copies(quarters, slots, ss, rs):
         sends = [
@@ -1034,18 +783,547 @@
             on_x(kd, pd).wait_recv()
             on_y(kd, pd).wait_recv()
 
+    def in_tap(t):
+        return across(conv_in.at[t], in_far.at[t], in_s.at[t], in_r.at[t])
+
+    def out_tap(t):
+        return across(conv_out.at[t], out_far.at[t], out_s.at[t], out_r.at[t])
+
+    def text_rows(i):
+        part = pl.ds(pl.multiple_of(i * 512, 512), 512)
+        return across(text_w.at[part], text_w_far.at[part], text_ws.at[i], text_wr.at[i])
+
+    film_copy = across(film, film_far, far_s.at[0], far_r.at[0])
+    qkv_copy = across(qkv, qkv_far, far_s.at[1], far_r.at[1])
+    out_w_copy = across(out_w, out_w_far, far_s.at[2], far_r.at[2])
+    cot_copy = across(cot_in, cot_far, far_s.at[3], far_r.at[3])
+    loads[1].wait()
+    loads[2].wait()
+    loads[3].wait()
+    mine = halves.at[:, pl.ds(pl.multiple_of(c * 512, 512), 512)]
+    theirs = halves.at[:, pl.ds(pl.multiple_of(512 - c * 512, 512), 512)]
+    halves_copy = across(mine, mine, far_s.at[4], far_r.at[4])
+    bias_copy = across(film_bias.at[c], film_bias.at[c], far_s.at[5], far_r.at[5])
+    halves_copy.start()
+    bias_copy.start()
+
+    def each(count, make):
+        def go(i, _):
+            make(i).start()
+            return 0
+
+        lax.fori_loop(0, count, go, 0)
+
+    each(9, in_tap)
+    film_copy.start()
+
+    def doubling(buffer, ss, rs):
+        def rows_at(start, count):
+            return buffer.at[pl.ds(start, count)]
+
+        def made(r, part):
+            if r == 0:
+                return across(part, part, ss.at[0], rs.at[0])
+            return remote(part, part, ss.at[r], rs.at[r], (None, wx, wy, wz, wm, wz)[r])
+
+        def send(r):
+            return made(
+                r,
+                (
+                    rows_at(me, 1),
+                    rows_at(2 * w, 2),
+                    rows_at(4 * (w // 2), 4),
+                    rows_at(8 * z, 8),
+                    rows_at(16 * (z // 2), 16),
+                    rows_at(16 * (1 - z // 2), 16),
+                )[r],
+            )
+
+        def arrival(r):
+            return made(
+                r,
+                (
+                    rows_at(2 * w + 1 - c, 1),
+                    rows_at(2 * wx, 2),
+                    rows_at(4 * (wy // 2), 4),
+                    rows_at(8 * (wz // 4), 8),
+                    rows_at(16 * (wm // 8), 16),
+                    rows_at(16 * (1 - z // 2), 16),
+                )[r],
+            )
+
+        return send, arrival
+
+    early_send, early_arrival = doubling(early, early_s, early_r)
+    small_send, small_arrival = doubling(small, small_s, small_r)
+    early_send(0).start()
+
+    def plane(n, buffer):
+        ss, rs = src_s.at[n], src_r.at[n]
+        return (
+            remote(buffer.at[0], buffer.at[1], ss.at[0], rs.at[0], wx),
+            remote(buffer.at[0], buffer.at[2], ss.at[1], rs.at[1], wy),
+            remote(buffer.at[2, 0], buffer.at[3, 0], ss.at[2], rs.at[2], wx),
+            remote(buffer.at[1, 1], buffer.at[3, 1], ss.at[3], rs.at[3], wy),
+        )
+
+    def plane_first(n, buffer):
+        x_copy, y_copy, _, _ = plane(n, buffer)
+        x_copy.start()
+        y_copy.start()
+
+    def plane_second(n, buffer):
+        x_copy, y_copy, on_x_copy, on_y_copy = plane(n, buffer)
+        x_copy.wait_recv()
+        y_copy.wait_recv()
+        on_x_copy.start()
+        on_y_copy.start()
+
+    def plane_last(n, buffer):
+        x_copy, y_copy, on_x_copy, on_y_copy = plane(n, buffer)
+        on_x_copy.wait()
+        on_y_copy.wait()
+        x_copy.wait_send()
+        y_copy.wait_send()
+
+    text_mine = text_t.at[pl.ds(pl.multiple_of(c * 2048, 2048), 2048)]
+    text_other = text_t.at[pl.ds(pl.multiple_of(2048 - c * 2048, 2048), 2048)]
+    text_turn = (
+        local(text_mine, text_src.at[0, 0], turn_sem.at[0]),
+        across(text_other, text_src.at[0, 1], turn_s.at[0], turn_r.at[0]),
+    )
+    for copy in text_turn:
+        copy.start()
+
+    def turn(n, own_place, far_place):
+        return (
+            local(sources.at[2 * (n - 1)], own_place, turn_sem.at[n]),
+            across(sources.at[2 * (n - 1) + 1], far_place, turn_s.at[n], turn_r.at[n]),
+        )
+
+    first_turn = turn(1, first_src.at[0, 0], first_src.at[0, 1])
+    second_turn = turn(2, second_src.at[0, 0], second_src.at[0, 1])
+    normed_turn = turn(3, turned.at[0, 0], turned.at[0, 1])
+    mixed_turn = turn(4, turned.at[1, 0], turned.at[1, 1])
+
+    def put_turned(n, i, value):
+        side = (i // 2 + c) % 2
+        sources[2 * (n - 1) + side, pl.ds(pl.multiple_of((i % 2) * CHUNK, CHUNK), CHUNK)] = value.T
+
+    def norm_forward(x, gain, shift, n):
+        ones = group_ones()
+
+        def block(i, _):
+            lanes = column(i)
+            normed, _ = normalise(quadrants(x[:, lanes].astype(f32)), single, ones)
+            pre = rejoin(normed) * gain(lanes) + shift(lanes)
+            act = pre * jax.nn.sigmoid(pre)
+            put_turned(n, i, act.astype(bf16))
+            put_shifts(act, lambda shape: single, taps.at[i], slice(None))
+            return 0
+
+        lax.fori_loop(0, 4, block, 0)
+
+    def conv_forward(into, side, w_side, arrived):
+        def load(t):
+            return local(w_side.at[t], weights.at[t % 2, 0], weight_sem.at[t % 2, 0])
+
+        if arrived is not None:
+            arrived(0).wait_recv()
+        load(0).start()
+        half = 2 * ((c + side) % 2)
+
+        def step(t, _):
+            @pl.when(t < 8)
+            def _():
+                if arrived is not None:
+                    arrived(t + 1).wait_recv()
+                load(t + 1).start()
+
+            load(t).wait()
+            part = jnp.concatenate(
+                [tap_rows(taps.at[half + i], t % 3, t // 3, slice(None)) for i in range(2)], axis=1
+            )
+            fresh = jnp.dot(part, weights[t % 2, 0], preferred_element_type=f32)
+            if side == 0:
+
+                @pl.when(t == 0)
+                def _():
+                    into[...] = fresh
+
+                @pl.when(t > 0)
+                def _():
+                    into[...] += fresh
+            else:
+                into[...] += fresh
+            return 0
+
+        lax.fori_loop(0, 9, step, 0)
+
+    loads[0].wait()
+    halves_copy.wait_send()
+    across(theirs, theirs, far_s.at[4], far_r.at[4]).wait_recv()
+    norm_forward(field, lambda lanes: halves[0:1, lanes], lambda lanes: halves[1:2, lanes], 1)
+    for copy in first_turn:
+        copy.start()
+    for copy in text_turn:
+        copy.wait()
+    plane_first(0, text_src)
+    early_arrival(0).wait_recv()
+    early_send(1).start()
+    conv_forward(wide_field, 0, conv_in, None)
+    conv_forward(wide_field, 1, in_far, in_tap)
+    each(9, out_tap)
+    qkv_copy.start()
+    out_w_copy.start()
+    early_arrival(1).wait_recv()
+    early_send(2).start()
+
+    film_copy.wait()
+    bias_copy.wait_send()
+    across(film_bias.at[1 - c], film_bias.at[1 - c], far_s.at[5], far_r.at[5]).wait_recv()
+    film_loads = [
+        local(
+            ref.at[:, pl.ds(1024 * b, 1024)], weights.at[side, b], weight_sem.at[side, b]
+        )
+        for side, ref in enumerate((film, film_far))
+        for b in range(2)
+    ]
+    for copy in film_loads:
+        copy.start()
+    for copy in film_loads:
+        copy.wait()
+    cond = early[pl.ds(me, 1), 0:1].reshape(1, 1024)
+    early_row = early.at[me]
+    for b in range(2):
+        value = film_bias[b, 0:1]
+        for side in range(2):
+            lanes = pl.ds(pl.multiple_of(((c + side) % 2) * 512, 512), 512)
+            part = early_row[0:1, lanes]
+            part = jnp.broadcast_to(part * jax.nn.sigmoid(part), (16, 512)).astype(bf16)
+            value += jnp.dot(part, weights[side, b], preferred_element_type=f32)[0:1]
+        rows[b : b + 1] = value + (1.0 - b)
+    rows[2:3] = halves[0:1]
+    rows[3:4] = halves[1:2]
+
+    norm_forward(wide_field, lambda lanes: rows[0:1, lanes], lambda lanes: rows[1:2, lanes], 2)
+    for copy in second_turn:
+        copy.start()
+    for copy in second_turn:
+        copy.wait()
+    plane_first(1, second_src)
+    plane_second(0, text_src)
+    early_arrival(2).wait_recv()
+    early_send(3).start()
+    conv_forward(acc, 0, conv_out, None)
+    each(4, text_rows)
+    cot_copy.start()
+    conv_forward(acc, 1, out_far, out_tap)
+
+    def by_rows(body):
+        def go(i, _):
+            body(pl.ds(pl.multiple_of(i * 128, 128), 128))
+            return 0
+
+        lax.fori_loop(0, 4, go, 0)
+
+    def layer_norm_rows(part):
+        joined = (field[part].astype(f32) + acc[part]) * inv_root_two
+        acc[part] = joined
+        centre = joined - jnp.mean(joined, axis=1, keepdims=True)
+        rate = lax.rsqrt(jnp.mean(centre * centre, axis=1, keepdims=True) + epsilon)
+        normed = (centre * rate * halves[2:3]).astype(bf16)
+        for i in range(4):
+            held[NORMED + i, part] = normed[:, i * CHUNK : (i + 1) * CHUNK]
+
+    by_rows(layer_norm_rows)
+    early_arrival(3).wait_recv()
+
+    @pl.when(is_mid)
+    def _():
+        early_send(4).start()
+
+    def turn_block(n, base):
+        def go(i, _):
+            put_turned(n, i, held[base + i])
+            return 0
+
+        lax.fori_loop(0, 4, go, 0)
+
+    turn_block(3, NORMED)
+    for copy in normed_turn:
+        copy.start()
+
+    def sides(base, side):
+        half = base + 2 * ((c + side) % 2)
+        return jnp.concatenate([held[half], held[half + 1]], axis=1)
+
+    qkv_copy.wait()
+
+    def qkv_loads(m):
+        lanes = pl.ds(pl.multiple_of(m * 1024, 1024), 1024)
+        return [
+            local(ref.at[:, lanes], weights.at[m % 2, side], weight_sem.at[m % 2, side])
+            for side, ref in enumerate((qkv, qkv_far))
+        ]
+
+    def qkv_pass(body):
+        for copy in qkv_loads(0):
+            copy.start()
+
+        def step(m, _):
+            @pl.when(m < 2)
+            def _():
+                for copy in qkv_loads(m + 1):
+                    copy.start()
+
+            for copy in qkv_loads(m):
+                copy.wait()
+            body(m)
+            return 0
+
+        lax.fori_loop(0, 3, step, 0)
+
+    def project(m):
+        value = jnp.dot(sides(NORMED, 0), weights[m % 2, 0], preferred_element_type=f32)
+        value += jnp.dot(sides(NORMED, 1), weights[m % 2, 1], preferred_element_type=f32)
+        value = value.astype(bf16)
+        for i in range(4):
+            held[4 * m + i] = value[:, i * CHUNK : (i + 1) * CHUNK]
+
+    qkv_pass(project)
+
+    out_w_copy.wait()
+    out_w_loads = [
+        local(ref, weights.at[1, side], weight_sem.at[1, side])
+        for side, ref in enumerate((out_w, out_w_far))
+    ]
+    for copy in out_w_loads:
+        copy.start()
+    loads[4].wait()
+    for copy in out_w_loads:
+        copy.wait()
+    for side in range(2):
+        value = lax.dot_general(two_low[...], weights[1, side], LAST, preferred_element_type=f32)
+        value = value.astype(bf16)
+        half = GRAD_MIXED + 2 * ((c + side) % 2)
+        held[half] = value[:, :CHUNK]
+        held[half + 1] = value[:, CHUNK:]
+
+    def text_w_loads(s):
+        side = s // 4
+        part = pl.ds(pl.multiple_of((s % 4) * 512, 512), 512)
+        lanes = pl.ds(pl.multiple_of(((c + side) % 2) * 2048 + (s % 4) * 512, 512), 512)
+        slot = s % 2
+        return (
+            [
+                local(
+                    ref.at[part, pl.ds(1024 * b, 1024)], weights.at[slot, b], weight_sem.at[slot, b]
+                )
+                for ref in (text_w, text_w_far)
+                for b in range(2)
+            ],
+            local(text_in.at[:, lanes], text_low.at[slot], turn_sem.at[5 + slot]),
+        )
+
+    def start_text(s):
+        weight_copies, text_copy = text_w_loads(s)
+        text_copy.start()
+
+        @pl.when(s < 4)
+        def _():
+            for copy in weight_copies[:2]:
+                copy.start()
+
+        @pl.when(s >= 4)
+        def _():
+            text_rows(s - 4).wait_recv()
+            for copy in weight_copies[2:]:
+                copy.start()
+
+    start_text(0)
+    extra[0:256] = jnp.zeros((256, 1024), f32)
+
+    def text_pair_step(s, _):
+        @pl.when(s < 7)
+        def _():
+            start_text(s + 1)
+
+        weight_copies, text_copy = text_w_loads(s)
+        text_copy.wait()
+        for b in range(2):
+            weight_copies[b].wait()
+            extra[128 * b : 128 * b + 128] += jnp.dot(
+                text_low[s % 2], weights[s % 2, b], preferred_element_type=f32
+            )
+        return 0
+
+    lax.fori_loop(0, 8, text_pair_step, 0)
+    for i in range(4):
+        lanes = slice(i * CHUNK, (i + 1) * CHUNK)
+        held[TEXT_KEYS, 128 * i : 128 * i + 128] = extra[0:128, lanes].astype(bf16)
+        held[TEXT_VALUES, 128 * i : 128 * i + 128] = extra[128:256, lanes].astype(bf16)
+
+    @pl.when(is_mid)
+    def _():
+        early_arrival(4).wait_recv()
+        early_send(5).start()
+
+    @pl.when(is_end)
+    def _():
+        early_arrival(5).wait_recv()
+
+    groups = early[:, 1:2, 0:1]
+
+    def image_weight(row):
+        alike = (groups == early[pl.ds(row, 1), 1:2, 0:1]).astype(f32)
+        return (1.0 / (16.0 * jnp.sum(alike, axis=0, keepdims=True))).reshape(1, 1)
+
+    weight = image_weight(me)
+    far_weight = image_weight(2 * w + 1 - c)
+
+    def layout_of(i):
+        chip = (w, wx, wy, wd)[i // 2]
+        row = 2 * chip + (c if i % 2 == 0 else 1 - c)
+        flag = early[pl.ds(row, 1), 1:2, 1:2].reshape(1, 1)
+        return lambda shape: jnp.broadcast_to(flag, shape) == 1.0
+
+    scale = HEAD_DIM ** (-0.5)
+
+    def region(axis, shape):
+        position = lax.broadcasted_iota(jnp.int32, shape, axis)
+        return 2 * (position // 256) + (position % MAP_W) // (MAP_W // 2)
+
+    def attention(j, _):
+        for h in range(2):
+            lanes = slice(h * HEAD_DIM, (h + 1) * HEAD_DIM)
+            q, key, value = held[j, :, lanes], held[4 + j, :, lanes], held[8 + j, :, lanes]
+            text_part = pl.ds(pl.multiple_of(128 * j, 128), 128)
+            text_key, text_value = held[TEXT_KEYS, text_part, lanes], held[TEXT_VALUES, text_part, lanes]
+            grad = held[GRAD_MIXED + j, :, lanes]
+            keys = jnp.concatenate([key, text_key], axis=0)
+            values = jnp.concatenate([value, text_value], axis=0)
+            scores = lax.dot_general(q, keys, LAST, preferred_element_type=f32) * scale
+            shape = (512, 640)
+            allowed = (region(0, shape) == region(1, shape)) | (
+                lax.broadcasted_iota(jnp.int32, shape, 1) >= 512
+            )
+            scores = jnp.where(single | allowed, scores, masked_score)
+            exponent = jnp.exp(scores - jnp.max(scores, axis=1, keepdims=True))
+            probs = exponent / jnp.sum(exponent, axis=1, keepdims=True)
+            probs_low = probs.astype(bf16)
+            held[MIXED + j, :, lanes] = jnp.dot(
+                probs_low, values, preferred_element_type=f32
+            ).astype(bf16)
+            grad_probs = lax.dot_general(grad, values, LAST, preferred_element_type=f32)
+            grad_values = lax.dot_general(probs_low, grad, ROWS, preferred_element_type=f32)
+            inner = jnp.sum(probs * grad_probs, axis=1, keepdims=True)
+            grad_scores = (probs * (grad_probs - inner)).astype(bf16)
+            grad_q = jnp.dot(grad_scores, keys, preferred_element_type=f32) * scale
+            grad_keys = lax.dot_general(grad_scores, q, ROWS, preferred_element_type=f32) * scale
+            held[j, :, lanes] = grad_q.astype(bf16)
+            held[4 + j, :, lanes] = grad_keys[:512].astype(bf16)
+            held[8 + j, :, lanes] = grad_values[:512].astype(bf16)
+            pair_q[j, :, lanes] = (grad_keys[512:] * weight).astype(bf16)
+            pair_q[j, :, CHUNK + h * HEAD_DIM : CHUNK + (h + 1) * HEAD_DIM] = (
+                grad_values[512:] * weight
+            ).astype(bf16)
+        return 0
+
+    lax.fori_loop(0, 4, attention, 0)
     start_quarters(pair_q, pair_slots, pair_s, pair_r, keep_sem.at[0])
-    across(both_w, both_far, both_s, both_r).start()
+    turn_block(4, MIXED)
+    for copy in mixed_turn:
+        copy.start()
+
+    def both_place(ref, i):
+        return ref.at[:, pl.ds(pl.multiple_of(i * CHUNK, CHUNK), CHUNK)]
+
+    def both_keep(i):
+        return local(held.at[i], both_place(both_own, i), both_sem.at[i])
+
+    def both_send(i):
+        return across(held.at[i], both_place(both_far, i), both_s.at[i], both_r.at[i])
+
+    each(12, both_send)
+    each(12, both_keep)
+
+    def project_back(m):
+        left = jnp.concatenate([held[4 * m + i] for i in range(4)], axis=1)
+        for side in range(2):
+            lanes = pl.ds(pl.multiple_of(((c + side) % 2) * 512, 512), 512)
+            fresh = lax.dot_general(left, weights[m % 2, side], LAST, preferred_element_type=f32)
+
+            @pl.when(m == 0)
+            def _():
+                extra[:, lanes] = fresh
+
+            @pl.when(m > 0)
+            def _():
+                extra[:, lanes] += fresh
+
+    qkv_pass(project_back)
+    rows[4:8] = jnp.zeros((4, 1024), f32)
+
+    def layer_norm_back(part):
+        joined = acc[part]
+        centre = joined - jnp.mean(joined, axis=1, keepdims=True)
+        rate = lax.rsqrt(jnp.mean(centre * centre, axis=1, keepdims=True) + epsilon)
+        y = centre * rate
+        grad = extra[part]
+        rows[4:5] += jnp.sum(grad * y, axis=0, keepdims=True)
+        grad = grad * halves[2:3]
+        mean = jnp.mean(grad, axis=1, keepdims=True)
+        slope = jnp.mean(grad * y, axis=1, keepdims=True)
+        grad = two_low[part].astype(f32) + (grad - mean - y * slope) * rate
+        extra[part] = grad
+        two = grad * inv_root_two
+        two_low[part] = two.astype(bf16)
+        two = (two * weight).astype(bf16)
+        for i in range(4):
+            held[NORMED + i, part] = two[:, i * CHUNK : (i + 1) * CHUNK]
+
+    by_rows(layer_norm_back)
+    two_q = held.at[pl.ds(NORMED, 4)]
     start_quarters(two_q, two_slots, two_s, two_r, keep_sem.at[1])
-
-    text = (text0, text1, text2, text3)
+    pass_quarters(pair_q, pair_slots, pair_s, pair_r)
+
+    out_w_loads = [
+        local(ref, weights.at[1, side], weight_sem.at[1, side])
+        for side, ref in enumerate((out_w, out_w_far))
+    ]
+    for copy in out_w_loads:
+        copy.start()
+    for copy in out_w_loads:
+        copy.wait()
+    value = jnp.dot(sides(MIXED, 0), weights[1, 0], preferred_element_type=f32)
+    value += jnp.dot(sides(MIXED, 1), weights[1, 1], preferred_element_type=f32)
+    hidden_low[...] = (acc[...] + value).astype(bf16)
+    output_keep = local(hidden_low, output, keep_sem.at[6])
+    output_keep.start()
+
+    plane_second(1, second_src)
+    plane_last(0, text_src)
+    for copy in first_turn:
+        copy.wait()
+    plane_first(2, first_src)
+    finish_quarters(pair_q, pair_slots, pair_s, pair_r, keep_sem.at[0])
+
+    def both_done(i, _):
+        both_send(i).wait()
+        both_keep(i).wait()
+        return 0
+
+    lax.fori_loop(0, 12, both_done, 0)
+    for copy in normed_turn + mixed_turn:
+        copy.wait()
 
     def text_loads(i):
         slot = 2 * (i % 2)
         rows_i = pl.ds(pl.multiple_of(i * 512, 512), 512)
         return [
             local(
-                text[j].at[e, rows_i],
+                text_src.at[j, e, rows_i],
                 sources.at[slot + j // 2, :, pl.ds(TEXT_LEN * (2 * (j % 2) + e), TEXT_LEN)],
                 text_sem.at[i % 2, 2 * j + e],
             )
@@ -1055,18 +1333,17 @@
 
     for copy in text_loads(0):
         copy.start()
-    loads = [
-        local(normed_t, weights.at[0, 0], load_sem.at[0]),
-        local(mixed_t, weights.at[0, 1], load_sem.at[1]),
-        local(hidden_in, wide_field, load_sem.at[2]),
-        local(field_in, field, load_sem.at[3]),
-        local(two_low_in, two_low, load_sem.at[4]),
-        local(rows_in, rows, load_sem.at[5]),
+    turned_loads = [
+        local(
+            turned.at[kind, side],
+            weights.at[0, kind, :, pl.ds(512 * side, 512)],
+            weight_sem.at[kind, side],
+        )
+        for kind in range(2)
+        for side in range(2)
     ]
-    for copy in loads:
+    for copy in turned_loads:
         copy.start()
-    pass_quarters(pair_q, pair_slots, pair_s, pair_r)
-    finish_quarters(pair_q, pair_slots, pair_s, pair_r, keep_sem.at[0])
 
     def text_step(i, _):
         @pl.when(i < 3)
@@ -1091,38 +1368,55 @@
 
     def source_loads(parts):
         return [
-            local(parts[j].at[e], sources.at[2 * j + e], source_sem.at[2 * j + e])
+            local(parts.at[j, e], sources.at[2 * j + e], source_sem.at[2 * j + e])
             for j in range(4)
             for e in range(2)
         ]
 
-    second_loads = source_loads((second0, second1, second2, second3))
-    for copy in second_loads:
-        copy.start()
-
-    across(both_w, both_far, both_s, both_r).wait()
-    loads[0].wait()
-    loads[1].wait()
-
-    def rhs_loads(q, j, slot):
-        col = pl.ds(pl.multiple_of(j * 1024 + q * CHUNK, CHUNK), CHUNK)
-        return (
-            local(both_w.at[:, col], rhs.at[slot, pl.ds(0, 512)], rhs_sem.at[slot, 0]),
-            local(both_far.at[:, col], rhs.at[slot, pl.ds(512, 512)], rhs_sem.at[slot, 1]),
-        )
+
+    cot_copy.wait()
+    for copy in turned_loads:
+        copy.wait()
+
+    class rhs_loads:
+        def __init__(self, q, j, slot):
+            self.q, self.j, self.slot = q, j, slot
+
+        def copies(self, pair, col):
+            return [
+                local(
+                    ref.at[:, col], rhs.at[self.slot, pl.ds(512 * i, 512)], rhs_sem.at[self.slot, i]
+                )
+                for i, ref in enumerate(pair)
+            ]
+
+        def start(self):
+            @pl.when(self.j < 3)
+            def _():
+                col = pl.ds(pl.multiple_of(self.j * 1024 + self.q * CHUNK, CHUNK), CHUNK)
+                for copy in self.copies((both_own, both_far), col):
+                    copy.start()
+
+            @pl.when(self.j == 3)
+            def _():
+                for copy in self.copies((cot_in, cot_far), column(self.q)):
+                    copy.start()
+
+        def wait(self):
+            for copy in self.copies((cot_in, cot_far), column(self.q)):
+                copy.wait()
 
     staged = (hidden_q, held, held, held)
     staged_base = (0, FIRST_IN, FIRST_IN + 4, FIRST_ATTN)
 
     def rs_copy(m, j):
         return remote(
-            staged[m].at[staged_base[m] + j], rs_in.at[m, j], rs_s.at[m, j], rs_r.at[m, j], steps[m][0]
+            staged[m].at[staged_base[m] + j], rs_land.at[m, j], rs_s.at[m, j], rs_r.at[m, j], steps[m][0]
         )
 
     order = (2, 0, 1, 3)
     quarter_of = (px, py, pd, p)
-    for copy in rhs_loads(quarter_of[2], 0, 0):
-        copy.start()
+    rhs_loads(quarter_of[2], jnp.int32(0), 0).start()
     for place, m in enumerate(order):
 
         def attn_step(j, _, m=m, place=place):
@@ -1130,20 +1424,19 @@
 
             @pl.when(j < 3)
             def _():
-                for copy in rhs_loads(quarter_of[m], j + 1, 1 - slot):
-                    copy.start()
+                rhs_loads(quarter_of[m], j + 1, 1 - slot).start()
 
             if place < 3:
 
                 @pl.when(j == 3)
                 def _():
-                    for copy in rhs_loads(quarter_of[order[place + 1]], 0, 1 - slot):
-                        copy.start()
-
-            for copy in rhs_loads(quarter_of[m], j, slot):
-                copy.wait()
+                    rhs_loads(quarter_of[order[place + 1]], jnp.int32(0), 1 - slot).start()
+
+            rhs_loads(quarter_of[m], j, slot).wait()
             left = weights[0, j // 3]
-            value = jnp.dot(left, rhs[slot], preferred_element_type=f32)
+            value = weight * jnp.dot(
+                left[:, :512], rhs[slot, :512], preferred_element_type=f32
+            ) + far_weight * jnp.dot(left[:, 512:], rhs[slot, 512:], preferred_element_type=f32)
             staged[m][staged_base[m] + j] = value.astype(bf16)
             if m < 3:
                 rs_copy(m, j).start()
@@ -1158,7 +1451,7 @@
 
     def conv_term_taps(slots):
         for i in range(8):
-            put_shifts(slots[i].astype(f32), layouts[i] == 1, taps.at[i], slice(None))
+            put_shifts(slots[i].astype(f32), layout_of(i), taps.at[i], slice(None))
 
     def conv_term_loop(base, first_tick):
         def step(t, _):
@@ -1179,12 +1472,13 @@
 
     finish_quarters(two_q, two_slots, two_s, two_r, keep_sem.at[1])
     conv_term_taps(two_slots)
+    plane_last(1, second_src)
+    second_loads = source_loads(second_src)
+    for copy in second_loads:
+        copy.start()
     for copy in second_loads:
         copy.wait()
     conv_term_loop(FIRST_OUT, 2)
-    first_loads = source_loads((first0, first1, first2, first3))
-    for copy in first_loads:
-        copy.start()
 
     def conv_back(grad, w_own, w_far, first_tick):
         def weight_loads(t):
@@ -1198,10 +1492,12 @@
             copy.start()
         for i in range(4):
             put_shifts(
-                grad[:, i * CHUNK : (i + 1) * CHUNK].astype(f32), single, taps.at[i], slice(None)
+                grad[:, i * CHUNK : (i + 1) * CHUNK].astype(f32),
+                lambda shape: single,
+                taps.at[i],
+                slice(None),
             )
         acc[...] = jnp.zeros((512, 1024), f32)
-        last = (((1,), (1,)), ((), ()))
 
         def step(t, _):
             @pl.when(t < 8)
@@ -1216,7 +1512,7 @@
             )
             for side in range(2):
                 acc[:, side * 512 : side * 512 + 512] += lax.dot_general(
-                    part, weights[t % 2, side], last, preferred_element_type=f32
+                    part, weights[t % 2, side], LAST, preferred_element_type=f32
                 )
 
             @pl.when(t % 3 == 2)
@@ -1263,10 +1559,8 @@
 
         lax.fori_loop(0, 4, block, 0)
 
-    loads[4].wait()
-    loads[5].wait()
-    conv_back(two_low, out_own, out_far, 5)
-    loads[2].wait()
+    conv_back(two_low, conv_out, out_far, 5)
+    output_keep.wait()
 
     for m in range(3):
         for j in range(4):
@@ -1274,12 +1568,10 @@
 
     def put_hidden(i, lanes, value):
         hidden_low[:, lanes] = value.astype(bf16)
-        hidden_q[i] = (value * weight[0]).astype(bf16)
+        hidden_q[i] = (value * weight).astype(bf16)
 
     norm_back(wide_field, 0, put_hidden)
     start_quarters(hidden_q, hid_slots, hid_s, hid_r, keep_sem.at[2])
-    pass_load = local(passed_in, wide_field, keep_sem.at[3])
-    pass_load.start()
 
     for m in range(3):
         for j in range(4):
@@ -1288,8 +1580,18 @@
     def attn_sum(j, _):
         k = FIRST_ATTN + j
         value = held[k].astype(f32)
+        fresh = [
+            local(
+                rs_land.at[m, j], rhs.at[m // 2, pl.ds(512 * (m % 2), 512)], rhs_sem.at[m // 2, m % 2]
+            )
+            for m in range(3)
+        ]
+        for copy in fresh:
+            copy.start()
+        for copy in fresh:
+            copy.wait()
         for m in range(3):
-            value += rs_in[m, j].astype(f32)
+            value += rhs[m // 2, 512 * (m % 2) : 512 * (m % 2) + 512].astype(f32)
         held[k] = value.astype(bf16)
         offer(k)
         return 0
@@ -1297,80 +1599,41 @@
     lax.fori_loop(0, 4, attn_sum, 0)
     tick(8)
 
-    conv_back(hidden_low, in_own, in_far, 9)
-    loads[3].wait()
-    pass_load.wait()
+    plane_second(2, first_src)
+    conv_back(hidden_low, conv_in, in_far, 9)
 
     def put_input(i, lanes, value):
-        two_low[:, lanes] = (value + wide_field[:, lanes] * inv_root_two).astype(bf16)
+        two_low[:, lanes] = (value + extra[:, lanes] * inv_root_two).astype(bf16)
 
     norm_back(field, 2, put_input)
     keep = local(two_low, input_grad, keep_sem.at[4])
     keep.start()
-    me = 2 * w + c
     small[pl.ds(me, 1), 4:8] = rows[4:8][None]
-    small[pl.ds(me, 1)] = small[pl.ds(me, 1)] * weight[0]
+    small[pl.ds(me, 1)] = small[pl.ds(me, 1)] * weight[None]
     pass_quarters(hidden_q, hid_slots, hid_s, hid_r)
     tick(12)
     finish_quarters(hidden_q, hid_slots, hid_s, hid_r, keep_sem.at[2])
     conv_term_taps(hid_slots)
+    plane_last(2, first_src)
+    first_loads = source_loads(first_src)
+    for copy in first_loads:
+        copy.start()
     for copy in first_loads:
         copy.wait()
 
-    def small_rows(start, count):
-        return small.at[pl.ds(start, count)]
-
-    def small_copy(r):
-        if r == 0:
-            part = small_rows(me, 1)
-            return across(part, part, small_s.at[0], small_r.at[0])
-        if r == 1:
-            part = small_rows(2 * w, 2)
-            return remote(part, part, small_s.at[1], small_r.at[1], wx)
-        if r == 2:
-            part = small_rows(4 * (w // 2), 4)
-            return remote(part, part, small_s.at[2], small_r.at[2], wy)
-        if r == 3:
-            part = small_rows(8 * z, 8)
-            return remote(part, part, small_s.at[3], small_r.at[3], wz)
-        if r == 4:
-            part = small_rows(16 * (z // 2), 16)
-            return remote(part, part, small_s.at[4], small_r.at[4], wm)
-        part = small_rows(16 * (1 - z // 2), 16)
-        return remote(part, part, small_s.at[5], small_r.at[5], wz)
-
-    def small_arrival(r):
-        if r == 0:
-            part = small_rows(2 * w + 1 - c, 1)
-            return across(part, part, small_s.at[0], small_r.at[0])
-        if r == 1:
-            part = small_rows(2 * wx, 2)
-            return remote(part, part, small_s.at[1], small_r.at[1], wx)
-        if r == 2:
-            part = small_rows(4 * (wy // 2), 4)
-            return remote(part, part, small_s.at[2], small_r.at[2], wy)
-        if r == 3:
-            part = small_rows(8 * (wz // 4), 8)
-            return remote(part, part, small_s.at[3], small_r.at[3], wz)
-        if r == 4:
-            part = small_rows(16 * (wm // 8), 16)
-            return remote(part, part, small_s.at[4], small_r.at[4], wm)
-        part = small_rows(16 * (1 - z // 2), 16)
-        return remote(part, part, small_s.at[5], small_r.at[5], wz)
-
-    small_copy(0).start()
+    small_send(0).start()
     conv_term_loop(FIRST_IN, 13)
     for r in range(4):
         small_arrival(r).wait_recv()
         if r < 3:
-            small_copy(r + 1).start()
+            small_send(r + 1).start()
         tick(16 + r)
 
     @pl.when(is_mid)
     def _():
-        small_copy(4).start()
+        small_send(4).start()
         small_arrival(4).wait_recv()
-        small_copy(5).start()
+        small_send(5).start()
 
     def rest(k, _):
         tick(k)
@@ -1383,15 +1646,37 @@
         small_arrival(5).wait_recv()
 
     for r in range(4):
-        small_copy(r).wait_send()
+        small_send(r).wait_send()
 
     @pl.when(is_mid)
     def _():
-        small_copy(4).wait_send()
-        small_copy(5).wait_send()
+        small_send(4).wait_send()
+        small_send(5).wait_send()
 
     small_keep = local(small, small_out, keep_sem.at[5])
     small_keep.start()
+    early_keep = local(early, early_out, keep_sem.at[3])
+    early_keep.start()
+    for r in range(4):
+        early_send(r).wait_send()
+
+    @pl.when(is_mid)
+    def _():
+        early_send(4).wait_send()
+        early_send(5).wait_send()
+
+    def sent(i, _):
+        in_tap(i).wait_send()
+        out_tap(i).wait_send()
+        return 0
+
+    lax.fori_loop(0, 9, sent, 0)
+
+    def text_sent(i, _):
+        text_rows(i).wait_send()
+        return 0
+
+    lax.fori_loop(0, 4, text_sent, 0)
 
     def finish(k, _):
         @pl.when(is_end)
@@ -1413,27 +1698,32 @@
     lax.fori_loop(0, CHUNKS, finish, 0)
     keep.wait()
     small_keep.wait()
-
-
-def late(layouts, weight, *operands):
+    early_keep.wait()
+
+
+def run_whole(layout, *operands):
     bf16, f32 = jnp.bfloat16, jnp.float32
     any_spec = pl.BlockSpec(memory_space=pl.ANY)
-    smem = pl.BlockSpec(memory_space=pltpu.SMEM)
     dma = pltpu.SemaphoreType.DMA
     chunks = pltpu.VMEM((CHUNKS, 512, CHUNK), bf16)
     map_low = pltpu.VMEM((512, 1024), bf16)
     map_full = pltpu.VMEM((512, 1024), f32)
     slots = pltpu.VMEM((8, 512, CHUNK), bf16)
-    return pl.pallas_call(
-        late_kernel,
-        out_shape=(
-            jax.ShapeDtypeStruct((CHUNKS, 512, 1024), bf16),
-            jax.ShapeDtypeStruct((512, 4096), bf16),
-            jax.ShapeDtypeStruct((512, 1024), bf16),
-            jax.ShapeDtypeStruct((32, 8, 1024), f32),
-        ),
-        in_specs=[smem, smem] + [any_spec] * len(operands),
-        out_specs=[any_spec] * 4,
+    table = pltpu.VMEM((32, 8, 1024), f32)
+    low_shapes = (
+        (9, 512, 1024), (9, 512, 1024), (512, 2048), (512, 3072), (512, 1024), (2048, 2048),
+        (512, 1024), (4, 2, 2048, TEXT_LEN), (4, 2, 512, 512), (4, 2, 512, 512), (2, 2, 512, 512),
+        (512, 3072), (512, 3072), (3, 4, 512, CHUNK),
+    )
+    full_rows = jax.ShapeDtypeStruct((32, 8, 1024), f32)
+    field = jax.ShapeDtypeStruct((512, 1024), bf16)
+    outs = (jax.ShapeDtypeStruct((CHUNKS, 512, 1024), bf16), field, field, full_rows, full_rows)
+    outs += tuple(jax.ShapeDtypeStruct(shape, bf16) for shape in low_shapes)
+    found = pl.pallas_call(
+        whole_kernel,
+        out_shape=outs,
+        in_specs=[pl.BlockSpec(memory_space=pltpu.SMEM)] + [any_spec] * len(operands),
+        out_specs=[any_spec] * len(outs),
         scratch_shapes=[
             chunks, chunks, chunks,
             pltpu.VMEM((8, 3, 2, HALF_ROWS, CHUNK), bf16),
@@ -1441,22 +1731,28 @@
             pltpu.VMEM((8, TEXT_LEN, 2 * CHUNK), bf16),
             slots, slots,
             pltpu.VMEM((2, 1024, CHUNK), bf16),
-            pltpu.VMEM((3, 4, 512, CHUNK), bf16),
             pltpu.VMEM((2, 2, 512, 1024), bf16),
-            map_full, map_full, map_low, map_low, map_low,
+            map_full, map_full, map_full, map_low, map_low, map_low,
             pltpu.VMEM((4, 512, CHUNK), bf16),
+            pltpu.VMEM((4, TEXT_LEN, 2 * CHUNK), bf16),
+            pltpu.VMEM((2, TEXT_LEN, 512), bf16),
             pltpu.VMEM((8, 1024), f32),
-            pltpu.VMEM((32, 8, 1024), f32),
+            pltpu.VMEM((8, 1024), f32),
+            pltpu.VMEM((2, 8, 1024), f32),
+            table, table,
         ]
         + [dma((CHUNKS,))] * 15
         + [dma((7,))] * 6
-        + [dma, dma, dma((3, 4)), dma((3, 4)), dma((6,)), dma((6,))]
-        + [dma((2, 8)), dma((8,)), dma((2, 2)), dma((6,)), dma((2, 2)), dma((6,))],
+        + [dma((12,))] * 2 + [dma((3, 4))] * 2 + [dma((6,))] * 4
+        + [dma((9,))] * 4 + [dma((6,))] * 2 + [dma((4,))] * 2
+        + [dma((3, 4))] * 2 + [dma((5,))] * 2
+        + [dma((2, 8)), dma((8,)), dma((2, 2)), dma((5,)), dma((2, 2)), dma((7,)), dma((7,)), dma((12,))],
         compiler_params=pltpu.CompilerParams(
-            collective_id=0, has_side_effects=True, vmem_limit_bytes=62 << 20
+            collective_id=0, has_side_effects=True, vmem_limit_bytes=63 << 20
         ),
-        name="late_terms",
-    )(layouts, weight, *operands)
+        name="whole_step",
+    )(layout, *operands)
+    return found[:5]
 
 
 def widen_kernel(low, out):

time: 734 us -> 615 us (0.84)
  Pallas kernels: 470 us -> 592 us
  waiting for transfers between devices: 70.4 us -> 0 us
  matrix products: 55.2 us -> 2.76 us
  local copies, waits for them, and re-layouts: 49 us -> 11.4 us
  other arithmetic: 39.4 us -> 3.93 us
  starting transfers between devices: 23.3 us -> 0 us
  between operations: 16.9 us -> 2 us
    pallas_call x3 -> x1, Pallas kernels: 430 us -> 551 us  [run_whole(): pl.pallas_call(whole_kernel, out_shape=outs, in_specs=[pl.BlockSpec(memor...]
    ppermute x22 -> x0, waiting for transfers between devices: 67.8 us -> none  [the longest x13 61.4 us: to_wide(): return lax.ppermute(value, 'wide', [(i, i ^ step) for i in range(16)])]
    dot_general x13 -> x1, matrix products: 55.2 us -> 2.76 us  [pair_body(): lax.dot_general(half_of(cond_low, core, 1), small_all[:, :2].reshape(32,...]
    ppermute x22 -> x0, starting transfers between devices: 23.1 us -> none  [the longest x13 20.9 us: to_wide(): return lax.ppermute(value, 'wide', [(i, i ^ step) for i in range(16)])]
    reshape x8 -> x0, local copies, waits for them, and re-layouts: 16.2 us -> none  [the longest x1 3.03 us: attention_back(): grad_keys[:pixel_count].reshape(pixel_count, channels)]
    convert_element_type x14 -> x2, other arithmetic: 11.8 us -> 0.77 us  [the longest x1 0.69 us: pair_body(): facts = jnp.stack([cond_embed[0].astype(f32), jnp.pad(facts, (0, 1022))])]
    another operation x7 -> x1, other arithmetic: 11.5 us -> 0.63 us  [pair_body(): facts = jnp.stack([cond_embed[0].astype(f32), jnp.pad(facts, (0, 1022))])]
  transfers between devices with their start and end apart: 26 -> 0, of which waited for: 10 -> 0; matrix products, arithmetic and copies ran while one was open for 18% -> 0% of each run, Pallas kernels for 6% -> 0%
where the time goes in v3:
time: 615 us; the launch traced here: 612 us
  Pallas kernels  592 us (96%)
  local copies, waits for them, and re-layouts  11.4 us (2%)
    pallas_call x1, Pallas kernels, run_whole(): pl.pallas_call(whole_kernel, out_shape=outs, in_specs=[pl.BlockSpec(memor...  551 us
    pallas_call x5, Pallas kernels, widen(): pl.pallas_call(widen_kernel, out_shape=jax.ShapeDtypeStruct(shape, jnp.fl...  40.7 us

profile of v3, /device:TPU:0, one launch (start us, length us, event | category | flops | bytes accessed | tf_op | source)
XLA Modules:
  0.0 611.9 jit_solution(8731518613960955000)
XLA Ops:
  1.9 0.1 add_convert_fusion
  2.0 0.7 stack.25
  2.7 0.7 stack.26
  3.4 0.7 stack.27
  4.1 0.7 convert_element_type.24
  4.8 0.7 broadcast_in_dim.10
  5.4 0.6 fusion.7.halves_in
  6.1 0.6 select_maximum_fusion.facts_in
  6.7 0.6 pad_convert_fusion.film_bias_in
  7.3 2.3 copy.28.text_t
  9.6 551.1 %whole_step.1 = (bf16[30,512,1024]{2,1,0:T(8,128)(2,1)}, bf16[512,1024]{1,0:T(8,128)(2,1)}, bf16[512,1024]{1,0:T(8,128)(2,1)}, f32[32,8,1024]{2,1,0:T(8,128)}, f...) custom-call(s32[1]{0:T(128)S(6)} %copy.38.layout, ...), custom_call_target="tpu_custom_call" | custom-call | tf_op jit(solution)/shard_map/whole_step/pallas_call | solution.py:1722
  560.7 1.3 reduce_sum.9
  562.0 1.3 slice.32
  563.4 0.6 constant_dynamic-slice_fusion
  564.0 0.6 dynamic_slice.26
  564.6 0.6 constant_dynamic-slice_fusion.2
  565.1 1.3 slice.21
  566.5 2.7 widen.8
  569.1 2.8 fusion
  571.9 4.9 widen.7
  576.8 10.3 %widen.9 = f32[2048,2048]{1,0:T(8,128)} custom-call(bf16[30,512,1024]{2,1,0:T(8,128)(2,1)} %get-tuple-element.20.low), custom_call_target="tpu_custom_call" | custom-call | tf_op jit(solution)/shard_map/widen/pallas_call | solution.py:1763
  587.1 11.4 %widen.6 = f32[9,512,1024]{2,1,0:T(8,128)} custom-call(bf16[30,512,1024]{2,1,0:T(8,128)(2,1)} %get-tuple-element.20.low), custom_call_target="tpu_custom_call" | custom-call | tf_op jit(solution)/shard_map/widen/pallas_call | solution.py:1763
  598.4 0.0 copy-start.1
  598.4 0.0 copy-start
  598.4 11.5 %widen.5 = f32[9,512,1024]{2,1,0:T(8,128)} custom-call(bf16[30,512,1024]{2,1,0:T(8,128)(2,1)} %get-tuple-element.20.low), custom_call_target="tpu_custom_call" | custom-call | tf_op jit(solution)/shard_map/widen/pallas_call | solution.py:1763
  610.0 0.0 copy-done.1
  610.0 1.0 copy.40
  610.9 0.0 copy-done
  610.9 1.0 copy.41
  (6 shorter events, 0.1 us)
Async XLA Ops:
  598.4 11.5 %copy-start.1 = (bf16[512,1024]{1,0:T(8,128)(2,1)S(1)}, bf16[512,1024]{1,0:T(8,128)(2,1)}, u32[]{:S(2)}) copy-start(bf16[512,1024]{1,0:T(8,128)(2,1)} %get-tuple-element.17) | copy-start | bytes 3145732
  598.4 12.5 %copy-start = (bf16[512,1024]{1,0:T(8,128)(2,1)S(1)}, bf16[512,1024]{1,0:T(8,128)(2,1)}, u32[]{:S(2)}) copy-start(bf16[512,1024]{1,0:T(8,128)(2,1)} %get-tuple-element.18) | copy-start | bytes 3145732
